TPU v7x, 32 devices: a whole 2x2x4 slice. The times are simulated.
32 devices in a mesh: dp: 4 (over y, core), seq: 8 (over z, x).
Axes of the slice: x: 2, y: 2, z: 4, core: 2. Of those that a mesh axis runs over, the one named last changes fastest.
Arguments:
- inputs: float32 [8, 1024, 768], P('dp', 'seq'), may hold values from -6 to 6
- segments: int32 [8, 1024], P('dp', 'seq'), may hold values from 0 to 3
- padding: int32 [8, 1024], P('dp', 'seq'), may hold values 0 or 1
- type_table: float32 [4, 768], replicated, may hold values from -3 to 3
- ln_gain: float32 [2, 2, 768], replicated, may hold values from 0.5 to 1.5
- ln_bias: float32 [2, 2, 768], replicated, may hold values from -1 to 1
- up_weight: bfloat16 [2, 768, 3072], replicated, may hold values from -0.21875 to 0.21875
- up_bias: float32 [2, 3072], replicated, may hold values from -1 to 1
- down_weight: bfloat16 [2, 3072, 768], replicated, may hold values from -0.109375 to 0.109375
- down_bias: float32 [2, 768], replicated, may hold values from -1 to 1
- out_grad: float32 [8, 1024, 768], P('dp', 'seq'), may hold values from -6 to 6
Outputs:
- outputs: float32 [8, 1024, 768], P('dp', 'seq')
- input_grad: float32 [8, 1024, 768], P('dp', 'seq')
- table_grad: float32 [4, 768], replicated
- gain_grad: float32 [2, 2, 768], replicated
- bias_grad: float32 [2, 2, 768], replicated
- up_weight_grad: float32 [2, 768, 3072], P(None, None, 'seq')
- up_bias_grad: float32 [2, 3072], P(None, 'seq')
- down_weight_grad: float32 [2, 3072, 768], P(None, 'seq')
- down_bias_grad: float32 [2, 768], replicated
All inputs are finite; a program needn't handle non-finite values. No bound on the sum of `padding` on one device may be relied on, other than what follows from the above.
Results may differ from a plain program's by a relative error of at most 0.0065.
Values sent between devices are 32-bit elements; how exact they have to be, the bound alone decides.
No kernel may reach another device: no remote copies, remote signals or barrier semaphores. Data moves between devices by JAX's collectives and lax.ppermute only.
A program may use at most 192 MiB of HBM per device.

v0:
```python
import math

import jax
import jax.numpy as jnp
from jax import lax
from jax.sharding import PartitionSpec as P

EPSILON = 1e-05


def angle_table(row_count, col_count, period):
    row_index = jnp.arange(row_count, dtype=jnp.int32)
    col_index = jnp.arange(col_count, dtype=jnp.int32)
    product_mod = row_index[:, None] * col_index[None, :] % period
    angles = product_mod.astype(jnp.float32) * (2.0 * math.pi / period)
    return (jnp.cos(angles), jnp.sin(angles))


def precise(form, left, right):
    return jnp.einsum(form, left, right, precision=lax.Precision.HIGHEST)


def positions(part_real, part_imag, tables):
    outer_cos, outer_sin, twist_cos, twist_sin, inner_cos, inner_sin = tables
    blocks = outer_cos.shape[0]
    within = inner_cos.shape[0]
    number, length, width = part_real.shape
    shaped_real = part_real.reshape(number, blocks, within, width)
    shaped_imag = part_imag.reshape(number, blocks, within, width)
    section_real = precise("ks,rsmj->rkmj", outer_cos, shaped_real) + precise(
        "ks,rsmj->rkmj", outer_sin, shaped_imag
    )
    section_imag = precise("ks,rsmj->rkmj", outer_cos, shaped_imag) - precise(
        "ks,rsmj->rkmj", outer_sin, shaped_real
    )
    turn_cos = twist_cos[None, :, :, None]
    turn_sin = twist_sin[None, :, :, None]
    twisted_real = turn_cos * section_real + turn_sin * section_imag
    twisted_imag = turn_cos * section_imag - turn_sin * section_real
    final_real = precise("qm,rkmj->rqkj", inner_cos, twisted_real) + precise(
        "qm,rkmj->rqkj", inner_sin, twisted_imag
    )
    final_imag = precise("qm,rkmj->rqkj", inner_cos, twisted_imag) - precise(
        "qm,rkmj->rqkj", inner_sin, twisted_real
    )
    scale = 1.0 / math.sqrt(length)
    return (
        final_real.reshape(number, length, width) * scale,
        final_imag.reshape(number, length, width) * scale,
    )


def mixer(values, feature_tables, position_tables):
    hid_cos, hid_sin, cos_half, sin_packed = feature_tables
    real_part = precise("rcd,dj->rcj", values, hid_cos)
    imag_part = precise("rcd,dj->rcj", values, hid_sin)
    spec_real, spec_imag = positions(
        lax.all_to_all(real_part, "seq", split_axis=2, concat_axis=1, tiled=True),
        -lax.all_to_all(imag_part, "seq", split_axis=2, concat_axis=1, tiled=True),
        position_tables,
    )
    return lax.all_to_all(spec_real, "seq", split_axis=1, concat_axis=2, tiled=True)


def normalize(values, gain, shift):
    average = jnp.mean(values, axis=-1, keepdims=True)
    centered = values - average
    variance = jnp.mean(centered * centered, axis=-1, keepdims=True)
    inverse = lax.rsqrt(variance + EPSILON)
    unit = centered * inverse
    return (unit * gain + shift, unit, inverse)


def norm_back(upstream, unit, inverse, gain):
    scaled = upstream * gain
    first_term = jnp.mean(scaled, axis=-1, keepdims=True)
    second_term = jnp.mean(scaled * unit, axis=-1, keepdims=True)
    return inverse * (scaled - first_term - unit * second_term)


def gelu_tanh(values):
    return jax.nn.gelu(values, approximate=True)


def local(
    inputs,
    segments,
    padding,
    type_table,
    ln_gain,
    ln_bias,
    up_weight,
    up_bias,
    down_weight,
    down_bias,
    out_grad,
):
    seq_part = inputs.shape[1]
    features = inputs.shape[2]
    seq_count = lax.axis_size("seq")
    length = seq_part * seq_count
    hid_cos, hid_sin = angle_table(features, features, features)
    hid_scale = 1.0 / math.sqrt(features)
    hid_cos = hid_cos * hid_scale
    hid_sin = hid_sin * hid_scale
    half_feat = features // 2
    cos_half = hid_cos[:, :half_feat]
    sin_packed = jnp.concatenate(
        (hid_cos[:, half_feat : half_feat + 1], hid_sin[:, 1:half_feat]), axis=1
    )
    feature_tables = (hid_cos, hid_sin, cos_half, sin_packed)
    outer_cos, outer_sin = angle_table(seq_count, seq_count, seq_count)
    twist_cos, twist_sin = angle_table(seq_count, seq_part, length)
    inner_cos, inner_sin = angle_table(seq_part, seq_part, seq_part)
    position_tables = (outer_cos, outer_sin, twist_cos, twist_sin, inner_cos, inner_sin)
    type_count = type_table.shape[0]
    layer_count = ln_gain.shape[0]
    onehot = (segments[..., None] == jnp.arange(type_count, dtype=jnp.int32)).astype(jnp.float32)
    live_mask = padding[..., None].astype(jnp.float32)

    def mixing_of(values):
        return mixer(values, feature_tables, position_tables)

    def feed(normed, layer_at):
        normed_low = normed.astype(jnp.bfloat16)
        preact = (
            jnp.einsum(
                "rcd,df->rcf", normed_low, up_weight[layer_at], preferred_element_type=jnp.float32
            )
            + up_bias[layer_at]
        )
        hidden = gelu_tanh(preact).astype(jnp.bfloat16)
        branch = (
            jnp.einsum(
                "rcf,fd->rcd", hidden, down_weight[layer_at], preferred_element_type=jnp.float32
            )
            + down_bias[layer_at]
        )
        return (normed_low, preact, hidden, branch)

    carried = inputs + precise("rct,td->rcd", onehot, type_table)
    inputs_kept = []
    for layer_at in range(layer_count):
        inputs_kept.append(carried)
        mixing = mixing_of(carried * live_mask)
        normed, unit_first, inverse_first = normalize(
            carried + mixing, ln_gain[layer_at, 0], ln_bias[layer_at, 0]
        )
        normed_low, preact, hidden, branch = feed(normed, layer_at)
        carried, unit_second, inverse_second = normalize(
            normed + branch, ln_gain[layer_at, 1], ln_bias[layer_at, 1]
        )
    upstream = out_grad
    gain_parts = []
    shift_parts = []
    up_mat_parts = []
    up_vec_parts = []
    down_mat_parts = []
    down_vec_parts = []
    for layer_at in reversed(range(layer_count)):
        layer_input = inputs_kept[layer_at]
        mixing = mixing_of(layer_input * live_mask)
        normed, unit_first, inverse_first = normalize(
            layer_input + mixing, ln_gain[layer_at, 0], ln_bias[layer_at, 0]
        )
        normed_low, preact, hidden, branch = feed(normed, layer_at)
        combined, unit_second, inverse_second = normalize(
            normed + branch, ln_gain[layer_at, 1], ln_bias[layer_at, 1]
        )
        gain_second = jnp.sum(upstream * unit_second, axis=(0, 1))
        shift_second = jnp.sum(upstream, axis=(0, 1))
        delta_out = norm_back(upstream, unit_second, inverse_second, ln_gain[layer_at, 1])
        delta_branch = delta_out.astype(jnp.bfloat16)
        down_vec_parts.append(jnp.sum(delta_branch.astype(jnp.float32), axis=(0, 1)))
        down_mat_parts.append(
            jnp.einsum("rcf,rcd->fd", hidden, delta_branch, preferred_element_type=jnp.float32)
        )
        delta_hidden = jnp.einsum(
            "rcd,fd->rcf", delta_branch, down_weight[layer_at], preferred_element_type=jnp.float32
        )
        preact_out, puller = jax.vjp(gelu_tanh, preact)
        delta_preact = puller(delta_hidden)[0].astype(jnp.bfloat16)
        up_vec_parts.append(jnp.sum(delta_preact.astype(jnp.float32), axis=(0, 1)))
        up_mat_parts.append(
            jnp.einsum("rcd,rcf->df", normed_low, delta_preact, preferred_element_type=jnp.float32)
        )
        delta_normed = delta_out + jnp.einsum(
            "rcf,df->rcd", delta_preact, up_weight[layer_at], preferred_element_type=jnp.float32
        )
        gain_first = jnp.sum(delta_normed * unit_first, axis=(0, 1))
        shift_first = jnp.sum(delta_normed, axis=(0, 1))
        delta_summed = norm_back(delta_normed, unit_first, inverse_first, ln_gain[layer_at, 0])
        upstream = delta_summed + live_mask * mixing_of(delta_summed)
        gain_parts.append(jnp.stack((gain_first, gain_second), axis=0))
        shift_parts.append(jnp.stack((shift_first, shift_second), axis=0))
    gain_local = jnp.stack(gain_parts[::-1], axis=0)
    shift_local = jnp.stack(shift_parts[::-1], axis=0)
    down_vec_local = jnp.stack(down_vec_parts[::-1], axis=0)
    up_vec_local = jnp.stack(up_vec_parts[::-1], axis=0)
    up_mat_local = jnp.stack(up_mat_parts[::-1], axis=0)
    down_mat_local = jnp.stack(down_mat_parts[::-1], axis=0)
    table_local = precise("rct,rcd->td", onehot, upstream)
    minor_sums = lax.psum((gain_local, shift_local, down_vec_local, table_local), ("dp", "seq"))
    dense_sums = lax.psum((up_mat_local, up_vec_local, down_mat_local), "dp")
    up_mat_sum, up_vec_sum, down_mat_sum = (
        lax.psum_scatter(dense_sums[0], "seq", scatter_dimension=2, tiled=True),
        lax.psum_scatter(dense_sums[1], "seq", scatter_dimension=1, tiled=True),
        lax.psum_scatter(dense_sums[2], "seq", scatter_dimension=1, tiled=True),
    )
    return (
        carried,
        upstream,
        minor_sums[3],
        minor_sums[0],
        minor_sums[1],
        up_mat_sum,
        up_vec_sum,
        down_mat_sum,
        minor_sums[2],
    )


def solution(mesh):
    in_specs = (
        P("dp", "seq", None),
        P("dp", "seq"),
        P("dp", "seq"),
        P(),
        P(),
        P(),
        P(),
        P(),
        P(),
        P(),
        P("dp", "seq", None),
    )
    out_specs = (
        P("dp", "seq", None),
        P("dp", "seq", None),
        P(),
        P(),
        P(),
        P(None, None, "seq"),
        P(None, "seq"),
        P(None, "seq", None),
        P(),
    )
    return jax.shard_map(local, mesh=mesh, in_specs=in_specs, out_specs=out_specs, check_vma=False)
```

profile of v0, /device:TPU:0, one launch (start us, length us, event | category | flops | bytes accessed | tf_op | source)
XLA Modules:
  0.0 1213.6 jit_solution(15672659054378717872)
XLA Ops:
  9.6 11.4 fusion.56
  22.1 7.3 all-to-all-start.1
  29.4 11.1 fusion.64
  41.7 7.9 all-to-all-done.1
  49.6 3.8 all-to-all-start
  54.8 19.0 %all-to-all-done = f32[2,128,768]{1,0,2:T(2,128)S(1)} async-done(((f32[2,128,768]{1,0,2:T(2,128)}), f32[2,128,768]{1,0,2:T(2,128)S(1)}, u32[]{:S(2)}, u32[]{:S(2)}) %all-to-all-start) | async-done | bytes 786464 | tf_op jit(solution)/shard_map/all_to_all | solution.py:58
  81.9 3.6 all-to-all-start.2
  85.7 25.8 %all-to-all-done.2 = f32[2,1024,96]{2,0,1:T(2,128)S(1)} async-done(((f32[2,1024,96]{2,0,1:T(2,128)}), f32[2,1024,96]{2,0,1:T(2,128)S(1)}, u32[]{:S(2)}, u32[]{:S(2)}) %all-to-all-start.2) | async-done | bytes 786464 | tf_op jit(solution)/shard_map/all_to_all | solution.py:62
  113.1 3.8 fusion.24
  116.9 5.5 fusion.417
  122.7 11.5 fusion.54
  135.4 3.6 all-to-all-start.4
  139.0 11.3 fusion.62
  151.4 7.9 all-to-all-done.4
  160.3 3.8 all-to-all-start.3
  167.4 16.8 %all-to-all-done.3 = f32[2,128,768]{1,0,2:T(2,128)S(1)} async-done(((f32[2,128,768]{1,0,2:T(2,128)}), f32[2,128,768]{1,0,2:T(2,128)S(1)}, u32[]{:S(2)}, u32[]{:S(2)}) %all-to-all-start.3) | async-done | bytes 786464 | tf_op jit(solution)/shard_map/all_to_all | solution.py:58
  192.5 29.7 %all_to_all.198 = f32[2,1024,96]{2,0,1:T(2,128)S(1)} all-to-all(f32[2,1024,96]{2,0,1:T(2,128)S(1)} %copy.106), channel_id=1, replica_groups=mesh['dp'=4,'seq'=8] {'seq'}, dimensions={1} | all-to-all | bytes 1572864 | tf_op jit(solution)/shard_map/all_to_all | solution.py:62
  225.4 3.8 fusion.27
  229.3 5.6 fusion.418
  236.9 3.1 convert_reduce_fusion
  243.2 12.0 fusion.52
  256.4 3.6 all-to-all-start.7
  260.0 13.3 %fusion.60 = f32[2,128,768]{2,1,0:T(8,128)} fusion(f32[2,128,768]{2,1,0:T(8,128)} %copy-done.12), kind=kOutput, calls=%fused_computation.67 | convolution fusion | flops 1817837568 | bytes 1572864 | tf_op jit(solution)/shard_map/rcd,dj->rcj/dot_general | solution.py:20
  275.4 4.4 all-to-all-done.7
  280.8 3.8 all-to-all-start.6
  288.8 16.1 %all-to-all-done.6 = f32[2,128,768]{1,0,2:T(2,128)S(1)} async-done(((f32[2,128,768]{1,0,2:T(2,128)}), f32[2,128,768]{1,0,2:T(2,128)S(1)}, u32[]{:S(2)}, u32[]{:S(2)}) %all-to-all-start.6) | async-done | bytes 786464 | tf_op jit(solution)/shard_map/all_to_all | solution.py:58
  316.2 3.6 all-to-all-start.8
  319.8 7.8 convolution_bitcast_fusion
  327.6 18.1 %all-to-all-done.8 = f32[2,1024,96]{2,0,1:T(2,128)S(1)} async-done(((f32[2,1024,96]{2,0,1:T(2,128)}), f32[2,1024,96]{2,0,1:T(2,128)S(1)}, u32[]{:S(2)}, u32[]{:S(2)}) %all-to-all-start.8) | async-done | bytes 786464 | tf_op jit(solution)/shard_map/all_to_all | solution.py:62
  354.6 6.6 pad_maximum_fusion.1
  361.3 3.2 convolution_bitcast_fusion.2
  364.4 5.2 convert_reduce_fusion.1
  371.3 7.1 pad_maximum_fusion
  379.5 4.7 multiply_reduce_fusion.3
  384.5 11.9 fusion.50
  397.6 3.6 all-to-all-start.10
  401.2 11.8 fusion.58
  414.2 29.5 %all-to-all-done.10 = f32[2,128,768]{1,0,2:T(2,128)S(1)} async-done(((f32[2,128,768]{1,0,2:T(2,128)}), f32[2,128,768]{1,0,2:T(2,128)S(1)}, u32[]{:S(2)}, u32[]{:S(2)}) %all-to-all-start.10) | async-done | bytes 786464 | tf_op jit(solution)/shard_map/all_to_all | solution.py:59
  443.7 3.6 all-to-all-start.9
  450.6 35.9 %all-to-all-done.9 = f32[2,128,768]{1,0,2:T(2,128)S(1)} async-done(((f32[2,128,768]{1,0,2:T(2,128)}), f32[2,128,768]{1,0,2:T(2,128)S(1)}, u32[]{:S(2)}, u32[]{:S(2)}) %all-to-all-start.9) | async-done | bytes 786464 | tf_op jit(solution)/shard_map/all_to_all | solution.py:58
  489.9 217.2 %reduce-scatter.8.cloned.1.call-done = f32[2,384,768]{2,1,0:T(8,128)} async-done(((f32[2,3072,768]{2,1,0:T(8,128)}), f32[2,384,768]{2,1,0:T(8,128)}) %reduce-scatter.8.cloned.1.call-update) | async-done | bytes 2359312 | tf_op jit(solution)/shard_map/reduce_scatter | solution.py:208
  707.0 316.3 %reduce-scatter.6.cloned.1.call-done = f32[2,768,384]{2,1,0:T(8,128)} async-done(((f32[2,768,3072]{2,1,0:T(8,128)}), f32[2,768,384]{2,1,0:T(8,128)}) %reduce-scatter.6.cloned.1.call-update) | async-done | bytes 2359312 | tf_op jit(solution)/shard_map/reduce_scatter | solution.py:206
  1029.0 3.7 all-to-all-start.11
  1033.0 72.0 %reduce-scatter.10.cloned.1.call-done = f32[384,2]{1,0:T(8,128)} async-done(((f32[3072,2]{1,0:T(8,128)}), f32[384,2]{1,0:T(8,128)}) %reduce-scatter.10.cloned.1.call-update) | async-done | bytes 3088
  1106.1 6.2 psum.57
  1113.6 42.0 %all-reduce = (f32[4,768]{1,0:T(4,128)}, f32[2,2,768]{2,1,0:T(2,128)}, f32[2,2,768]{2,1,0:T(2,128)}, f32[2,768]{1,0:T(2,128)}) all-reduce(f32[4,768]{1,0:T(4,128)S(1)} %convolution_bitcast_fusion.4, f32[2,2,768]{2,1,0:T(2,128)S(1)} %pad_maximum_fusion.3, ...), channel_id=1, replica_groups=mesh['dp'=4,'seq'=8] {'dp','seq'}, use_global_device_ids=true, to_apply=%region_16.17 | all-reduce | flops 10752 | bytes 86016 | tf_op jit(solution)/shard_map/psum | solution.py:203
  1155.6 46.4 %all-reduce.4.cloned.1.call-done = (f32[2,768,384]{2,1,0:T(8,128)}, f32[2,384,768]{2,1,0:T(8,128)}) async-done(((f32[2,768,384]{2,1,0:T(8,128)}, f32[2,384,768]{2,1,0:T(8,128)}), (f32[2,768,384]{2,1,0:T(8,128)}, f32[2,384,768]{2,1,0:T(8,128)})) %all-reduce.4.cloned.1.call-update) | async-done | bytes 4718608 | tf_op jit(solution)/shard_map/psum | solution.py:204
  1202.1 3.4 copy.260
  (192 shorter events, 89.3 us)
Async XLA Ops:
  22.1 27.4 %all-to-all-start.1 = ((f32[2,128,768]{1,0,2:T(2,128)}), f32[2,128,768]{1,0,2:T(2,128)S(1)}, u32[]{:S(2)}, u32[]{:S(2)}) async-start(f32[2,128,768]{1,0,2:T(2,128)} %copy.87), calls=%async_computation.1 | async-start | bytes 1572864 | tf_op jit(solution)/shard_map/all_to_all | solution.py:59
  49.6 24.1 %all-to-all-start = ((f32[2,128,768]{1,0,2:T(2,128)}), f32[2,128,768]{1,0,2:T(2,128)S(1)}, u32[]{:S(2)}, u32[]{:S(2)}) async-start(f32[2,128,768]{1,0,2:T(2,128)} %copy.84), calls=%async_computation | async-start | bytes 1572864 | tf_op jit(solution)/shard_map/all_to_all | solution.py:58
  79.7 5.8 copy-start.23
  79.7 5.8 copy-start.21
  79.7 5.8 copy-start.22
  79.7 5.9 copy-start.20
  81.9 29.5 %all-to-all-start.2 = ((f32[2,1024,96]{2,0,1:T(2,128)}), f32[2,1024,96]{2,0,1:T(2,128)S(1)}, u32[]{:S(2)}, u32[]{:S(2)}) async-start(f32[2,1024,96]{2,0,1:T(2,128)} %copy.93), calls=%async_computation.2 | async-start | bytes 2097152 | tf_op jit(solution)/shard_map/all_to_all | solution.py:62
  116.9 5.5 copy-start.4
  135.4 24.0 %all-to-all-start.4 = ((f32[2,128,768]{1,0,2:T(2,128)}), f32[2,128,768]{1,0,2:T(2,128)S(1)}, u32[]{:S(2)}, u32[]{:S(2)}) async-start(f32[2,128,768]{1,0,2:T(2,128)} %copy.100), calls=%async_computation.4 | async-start | bytes 1572864 | tf_op jit(solution)/shard_map/all_to_all | solution.py:59
  159.4 0.9 copy-start.8
  160.3 23.9 %all-to-all-start.3 = ((f32[2,128,768]{1,0,2:T(2,128)}), f32[2,128,768]{1,0,2:T(2,128)S(1)}, u32[]{:S(2)}, u32[]{:S(2)}) async-start(f32[2,128,768]{1,0,2:T(2,128)} %copy.97), calls=%async_computation.3 | async-start | bytes 1572864 | tf_op jit(solution)/shard_map/all_to_all | solution.py:58
  229.2 7.6 copy-start.7
  229.2 7.6 slice-start.3
  229.2 5.9 copy-start.10
  229.3 7.6 slice-start.4
  229.3 7.6 slice-start.5
  235.6 4.5 slice-start.6
  236.8 3.2 copy-start.19
  236.8 3.2 slice-start.7
  236.9 3.2 slice-start.8
  240.0 2.0 copy-start.17
  242.3 0.9 copy-start.12
  256.4 23.5 %all-to-all-start.7 = ((f32[2,128,768]{1,0,2:T(2,128)}), f32[2,128,768]{1,0,2:T(2,128)S(1)}, u32[]{:S(2)}, u32[]{:S(2)}) async-start(f32[2,128,768]{1,0,2:T(2,128)} %copy.113), calls=%async_computation.7 | async-start | bytes 1572864 | tf_op jit(solution)/shard_map/all_to_all | solution.py:59
  279.9 0.9 copy-start.9
  280.8 24.1 %all-to-all-start.6 = ((f32[2,128,768]{1,0,2:T(2,128)}), f32[2,128,768]{1,0,2:T(2,128)S(1)}, u32[]{:S(2)}, u32[]{:S(2)}) async-start(f32[2,128,768]{1,0,2:T(2,128)} %copy.110), calls=%async_computation.6 | async-start | bytes 1572864 | tf_op jit(solution)/shard_map/all_to_all | solution.py:58
  285.7 0.9 copy-start.2
  304.8 3.7 copy-start.3
  316.2 29.5 %all-to-all-start.8 = ((f32[2,1024,96]{2,0,1:T(2,128)}), f32[2,1024,96]{2,0,1:T(2,128)S(1)}, u32[]{:S(2)}, u32[]{:S(2)}) async-start(f32[2,1024,96]{2,0,1:T(2,128)} %copy.119), calls=%async_computation.8 | async-start | bytes 2097152 | tf_op jit(solution)/shard_map/all_to_all | solution.py:62
  319.8 387.3 %reduce-scatter.8.cloned.1.call-start = ((), (), s32[]{:S(2)}) async-start(), calls=%async_computation.16 | async-start | bytes 21233664 | tf_op jit(solution)/shard_map/reduce_scatter | solution.py:208
  348.7 2.7 copy-start.5
  350.5 0.9 copy-start.13
  350.6 3.1 slice-start
  351.4 2.9 slice-start.1
  351.4 3.1 slice-start.2
  361.2 662.1 %reduce-scatter.6.cloned.1.call-start = ((), (), s32[]{:S(2)}) async-start(), calls=%async_computation.15 | async-start | bytes 21233664 | tf_op jit(solution)/shard_map/reduce_scatter | solution.py:206
  361.3 3.2 copy-start.6
  369.6 1.6 copy-start.18
  378.4 1.1 copy-start.14
  397.6 46.1 %all-to-all-start.10 = ((f32[2,128,768]{1,0,2:T(2,128)}), f32[2,128,768]{1,0,2:T(2,128)S(1)}, u32[]{:S(2)}, u32[]{:S(2)}) async-start(f32[2,128,768]{1,0,2:T(2,128)} %copy.126), calls=%async_computation.10 | async-start | bytes 1572864 | tf_op jit(solution)/shard_map/all_to_all | solution.py:59
  443.7 42.8 %all-to-all-start.9 = ((f32[2,128,768]{1,0,2:T(2,128)}), f32[2,128,768]{1,0,2:T(2,128)S(1)}, u32[]{:S(2)}, u32[]{:S(2)}) async-start(f32[2,128,768]{1,0,2:T(2,128)} %copy.123), calls=%async_computation.9 | async-start | bytes 1572864 | tf_op jit(solution)/shard_map/all_to_all | solution.py:58
  447.2 657.8 %reduce-scatter.10.cloned.1.call-start = ((), (), s32[]{:S(2)}) async-start(), calls=%async_computation.17 | async-start | bytes 1769472
  449.0 753.1 %all-reduce.4.cloned.1.call-start = ((), (), s32[]{:S(2)}) async-start(), calls=%async_computation.18 | async-start | bytes 9437184 | tf_op jit(solution)/shard_map/psum | solution.py:204
  489.8 533.5 %copy-start.15 = (f32[2,8,128,96]{2,1,3,0:T(8,128)S(1)}, f32[2,8,128,96]{2,1,3,0:T(8,128)}, u32[]{:S(2)}) copy-start(f32[2,8,128,96]{2,1,3,0:T(8,128)} %fusion.69) | copy-start | bytes 2359300
  1029.0 83.3 %all-to-all-start.11 = ((f32[2,1024,96]{2,0,1:T(2,128)}), f32[2,1024,96]{2,0,1:T(2,128)S(1)}, u32[]{:S(2)}, u32[]{:S(2)}) async-start(f32[2,1024,96]{2,0,1:T(2,128)} %copy.132), calls=%async_computation.11 | async-start | bytes 2097152 | tf_op jit(solution)/shard_map/all_to_all | solution.py:62
  1032.8 80.5 %copy-start.24 = (s32[2,128]{1,0:T(2,128)S(1)}, s32[2,128]{1,0:T(2,128)}, u32[]{:S(2)}) copy-start(s32[2,128]{1,0:T(2,128)} %param.12) | copy-start | bytes 3076
  1113.2 93.6 %copy-start.11 = (f32[2,128,768]{2,1,0:T(8,128)}, f32[2,128,768]{2,1,0:T(8,128)S(1)}, u32[]{:S(2)}) copy-start(f32[2,128,768]{2,1,0:T(8,128)S(1)} %multiply_add_fusion) | copy-start | bytes 2359300
  1202.1 3.4 copy-start.16
  1202.1 4.8 copy-start.1
  (1 other events, 0.7 us)
Sparse Core Ops, SparseCore 0:
  361.3 345.6 reduce-scatter.7
  710.9 312.3 reduce-scatter.5
  1027.3 77.6 reduce-scatter.9
  1107.4 94.6 all-reduce.3
where the time goes:
time: 1230 us; the launch traced here: 1210 us
  waiting for transfers between devices  833 us (68%)
  matrix products  180 us (15%)
  blocking collectives  77.9 us (6%)
  starting transfers between devices  44.3 us (4%)
  local copies, waits for them, and re-layouts  40.6 us (3%)
  other arithmetic  23 us (2%)
  between operations  15.1 us (1%)
    reduce_scatter x1, waiting for transfers between devices, local(): lax.psum_scatter(dense_sums[0], 'seq', scatter_dimension=2, tiled=True)  316 us
    reduce_scatter x1, waiting for transfers between devices, local(): lax.psum_scatter(dense_sums[2], 'seq', scatter_dimension=1, tiled=True)  217 us
    dot_general x34, matrix products, precise(): return jnp.einsum(form, left, right, precision=lax.Precision.HIGHEST)  131 us
    all_to_all x4, waiting for transfers between devices, mixer(): lax.all_to_all(real_part, 'seq', split_axis=2, concat_axis=1, tiled=True)  87.7 us
    unnamed x5, waiting for transfers between devices  72.1 us
    all_to_all x4, waiting for transfers between devices, mixer(): lax.all_to_all(imag_part, 'seq', split_axis=2, concat_axis=1, tiled=True)  49.8 us
    psum x1, waiting for transfers between devices, local(): dense_sums = lax.psum((up_mat_local, up_vec_local, down_mat_local), 'dp')  46.4 us
    all_to_all x3, waiting for transfers between devices, mixer(): lax.all_to_all(spec_real, 'seq', split_axis=1, concat_axis=2, tiled=True)  43.9 us
  transfers between devices with their start and end apart: 15, of which 14 were waited for; matrix products, arithmetic and copies ran while one was open for 10% of the time, Pallas kernels for 0%

commit v1 on v0

v1 whole, which is shorter than its diff:
```python
import math

import jax
import jax.numpy as jnp
import numpy as np
from jax import lax
from jax.experimental import pallas as pl
from jax.experimental.pallas import tpu as pltpu
from jax.sharding import Mesh
from jax.sharding import PartitionSpec as P

EPSILON = 1e-05
DP = ("do", "dy", "core")
SEQ = ("zh", "zl", "x")
ROW = ("zl", "x")
PLANE = ("dy", "core", "x")
ALL = DP + SEQ


def owned(count, part, seq, at):
    step = 2 * count
    second = step - at if at else count
    pos = np.arange(seq * part).reshape(seq, part // step, step)
    return np.stack([pos[:, :, at], pos[:, :, second]], 1).reshape(-1)


def feature_table(width):
    half = width // 2
    angle = np.outer(np.arange(width), np.arange(width)) % width * (2.0 * math.pi / width)
    cos, sin = np.cos(angle) / math.sqrt(width), np.sin(angle) / math.sqrt(width)
    return np.concatenate([cos[:, :half], cos[:, half : half + 1], sin[:, 1:half]], 1)


def position_tables(count, part, seq):
    length = seq * part
    step = 2 * count
    span = length // step
    keep = span // step
    w = 2.0 * math.pi / length
    own = [owned(count, part, seq, i) for i in range(count)]
    local = length // count
    send = np.zeros((2, count, count, 2 * keep, local))
    recv = np.zeros((2, count, count, local, 2 * keep))
    block = np.zeros((2, count, local, local))
    scale = 1.0 / math.sqrt(length)

    def kept(i):
        if i:
            return [(i + step * s, 2) for s in range(keep)]
        ends = [(step * s, 1 if s in (0, keep // 2) else 2) for s in range(keep // 2 + 1)]
        return ends + [(count + step * s, 2) for s in range(keep // 2)]

    for j in range(count):
        n = own[j]
        first = n % step == j
        theta = 2.0 * math.pi * j / step
        for i in range(count):
            if i == j:
                angle = w * (np.outer(n, n) % length)
                block[0, i], block[1, i] = np.cos(angle) * scale, np.sin(angle) * scale
                continue
            at = 0
            slots = {}
            for kap, kinds in kept(i):
                cos, sin = np.cos(w * (kap * n % length)), np.sin(w * (kap * n % length))
                if j:
                    sign = np.where(first, 1.0, -1.0)
                    rows = (cos, sign * sin, sign * cos, sin)
                else:
                    rows = (cos * first, cos * ~first, sin * first, sin * ~first)
                if kinds == 2:
                    send[0, j, i, at], send[0, j, i, at + 1] = rows[:2]
                    send[1, j, i, at], send[1, j, i, at + 1] = rows[2:]
                    slots[kap] = (at, at + 1, 0.0)
                else:
                    phi = w * (kap * j % length)
                    send[0, j, i, at] = math.cos(phi) * rows[0] + math.sin(phi) * rows[1]
                    send[1, j, i, at] = math.cos(phi) * rows[2] + math.sin(phi) * rows[3]
                    slots[kap] = (at, at, phi)
                at += kinds
            for index, k in enumerate(own[i]):
                kap, turn = k % span, k // span
                mirrored = kap not in slots
                p_at, q_at, phi = slots[(span - kap) % span if mirrored else kap]
                pair = np.zeros((2, 2 * keep))
                if p_at == q_at:
                    pair[0, p_at], pair[1, p_at] = math.cos(phi), math.sin(phi)
                else:
                    pair[0, p_at], pair[1, q_at] = 1.0, 1.0
                even, odd = pair, pair
                if j:
                    if mirrored:
                        c, s = math.cos(theta), math.sin(theta)
                        even = odd = np.stack([c * pair[0] + s * pair[1], s * pair[0] - c * pair[1]])
                    c, s = math.cos(theta * turn), math.sin(theta * turn)
                    recv[0, i, j, index] = c * even[0] - s * even[1]
                    recv[1, i, j, index] = s * odd[0] + c * odd[1]
                else:
                    flip = (-1.0) ** turn
                    if mirrored:
                        even, odd = pair * np.array([[1.0], [-1.0]]), pair * np.array([[-1.0], [1.0]])
                    recv[0, i, j, index] = even[0] + flip * even[1]
                    recv[1, i, j, index] = odd[0] + flip * odd[1]
    rows = count * 2 * keep
    send = send.reshape(2, count, rows, local)
    recv = np.moveaxis(recv, 2, 3).reshape(2, count, local, rows) * scale
    return tuple(np.asarray(t, np.float32) for t in (send, recv, block))


def precise(left, right):
    return jnp.matmul(left, right, precision=lax.Precision.HIGHEST)


def wide(left, right, contract):
    return lax.dot_general(left, right, ((contract[:1], contract[1:]), ((), ())), preferred_element_type=jnp.float32)


def normalize(values, gain, shift):
    average = jnp.mean(values, axis=-1, keepdims=True)
    centered = values - average
    variance = jnp.mean(centered * centered, axis=-1, keepdims=True)
    inverse = lax.rsqrt(variance + EPSILON)
    unit = centered * inverse
    return unit * gain + shift, unit, inverse


def norm_back(upstream, unit, inverse, gain):
    scaled = upstream * gain
    first_term = jnp.mean(scaled, axis=-1, keepdims=True)
    second_term = jnp.mean(scaled * unit, axis=-1, keepdims=True)
    return inverse * (scaled - first_term - unit * second_term)


def gelu(values):
    return jax.nn.gelu(values, approximate=True)


def gelu_parts(p):
    c = math.sqrt(2.0 / math.pi)
    square = p * p
    t = jnp.tanh(c * p * (1.0 + 0.044715 * square))
    halves = 0.5 * (1.0 + t)
    slope = halves + 0.5 * p * (1.0 - t * t) * (c + 3.0 * 0.044715 * c * square)
    return p * halves, slope


def grads_kernel(normed_ref, delta_ref, up_ref, bias_ref, down_ref, out_ref):
    planes, rows = out_ref.shape[0], out_ref.shape[1] // 2
    normed = normed_ref[...].astype(jnp.bfloat16)
    delta = delta_ref[...].astype(jnp.bfloat16)
    pre = wide(normed, up_ref[...], (1, 0)) + bias_ref[...]
    value, slope = gelu_parts(pre)
    back = (wide(delta, down_ref[...], (1, 1)) * slope).astype(jnp.bfloat16)
    up = wide(back, normed, (0, 0))
    down = wide(value.astype(jnp.bfloat16), delta, (0, 0))
    parts = [(z, h, a[z * rows : (z + 1) * rows]) for z in range(planes) for h, a in enumerate((up, down))]

    @pl.when(pl.program_id(0) == 0)
    def _():
        for z, h, value in parts:
            out_ref[z, h * rows : (h + 1) * rows] = value

    @pl.when(pl.program_id(0) > 0)
    def _():
        for z, h, value in parts:
            out_ref[z, h * rows : (h + 1) * rows] += value


def weight_grads(normed, delta, up, bias, down, planes):
    tokens, width = normed.shape
    units = up.shape[1]
    block = min(tokens, 512)
    return pl.pallas_call(
        grads_kernel,
        grid=(tokens // block,),
        in_specs=[
            pl.BlockSpec((block, width), lambda i: (i, 0)),
            pl.BlockSpec((block, width), lambda i: (i, 0)),
            pl.BlockSpec((width, units), lambda i: (0, 0)),
            pl.BlockSpec((1, units), lambda i: (0, 0)),
            pl.BlockSpec((units, width), lambda i: (0, 0)),
        ],
        out_specs=pl.BlockSpec((planes, 2 * units // planes, width), lambda i: (0, 0, 0)),
        out_shape=jax.ShapeDtypeStruct((planes, 2 * units // planes, width), jnp.float32),
        compiler_params=pltpu.CompilerParams(vmem_limit_bytes=48 * 2**20),
        cost_estimate=pl.CostEstimate(
            flops=8 * tokens * width * units, bytes_accessed=8 * tokens * width, transcendentals=tokens * units
        ),
        name="weight_grads",
    )(normed, delta, up, bias.reshape(1, units), down)


def local(inputs, segments, padding, type_table, ln_gain, ln_bias, up_weight, up_bias, down_weight, down_bias, out_grad):
    rows, part, width = inputs.shape
    layers = ln_gain.shape[0]
    types = type_table.shape[0]
    hidden_width = up_weight.shape[2]
    seq = lax.axis_size(SEQ)
    count = lax.axis_size(ROW)
    step = 2 * count
    units = part // step
    tokens = rows * part
    half = width // 2
    at = lax.axis_index(ROW)

    feature = jnp.asarray(feature_table(width).astype(np.float32))
    send_t, recv_t, own_t = position_tables(count, part, seq)
    send_t, recv_t, own_t = (lax.dynamic_index_in_dim(jnp.asarray(t), at, 1, False) for t in (send_t, recv_t, own_t))
    chunk = send_t.shape[1] // count
    classes = np.array([[i, step - i if i else count] for i in range(count)])

    def spread(values):
        shaped = values.reshape(rows, units, step, width).transpose(0, 2, 1, 3)
        shaped = shaped[:, classes.reshape(-1)].reshape(seq, 2 * units, width)
        return lax.all_to_all(shaped, SEQ, 0, 0, tiled=True).reshape(tokens, width)

    def gather_back(values):
        shaped = lax.all_to_all(values.reshape(seq, 2 * units, width), SEQ, 0, 0, tiled=True)
        back = np.argsort(classes.reshape(-1))
        shaped = shaped.reshape(rows, step, units, width)[:, back].transpose(0, 2, 1, 3)
        return shaped.reshape(rows, part, width)

    def mark(values):
        whole = lax.all_gather(values, SEQ)[:, lax.axis_index("zh")]
        whole = whole.reshape(seq, units, step)
        pick = lax.dynamic_index_in_dim(jnp.asarray(classes), at, 0, False)
        return jnp.take(whole, pick, axis=2).transpose(0, 2, 1).reshape(tokens, 1)

    def mixer(values):
        spectrum = precise(values, feature)
        lower, upper = spectrum[:, :half], spectrum[:, half:]
        first = lax.broadcasted_iota(jnp.int32, (1, half), 1) == 0

        def stage(tables, low_part, up_part):
            even = precise(tables[0], low_part)
            odd = precise(tables[1], up_part)
            middle = precise(tables[0], up_part[:, :1])
            return even, jnp.where(first, middle, odd)

        even, odd = stage(send_t, lower, upper)
        sent = jnp.concatenate([even, odd], 1).reshape(count, chunk, width)
        got = lax.all_to_all(sent, ROW, 0, 0, tiled=True).reshape(count * chunk, width)
        even, odd = stage(recv_t, got[:, :half], got[:, half:])
        own_even, own_odd = stage(own_t, lower, upper)
        even, odd = even + own_even, odd + own_odd
        sine = jnp.where(first, 0.0, odd)
        head = even - sine
        tail = even + sine
        return jnp.concatenate([head, odd[:, :1], jnp.flip(tail[:, 1:], 1)], 1)

    onehot = segments[..., None] == jnp.arange(types, dtype=jnp.int32)
    embedded = inputs + sum(onehot[..., t : t + 1].astype(jnp.float32) * type_table[t] for t in range(types))
    live = mark(padding).astype(jnp.float32)
    kind = mark(segments)
    carried = spread(embedded)
    upstream = spread(out_grad)

    shares = lax.axis_size(("dy", "core"))
    planes = lax.axis_size(("zh", "zl"))
    columns = lax.axis_size("x")
    unit_block = hidden_width // seq
    piece = unit_block // shares
    starts = [
        (z * columns + lax.axis_index("x")) * unit_block + lax.axis_index(("dy", "core")) * piece for z in range(planes)
    ]

    def cut(array, axis):
        return jnp.concatenate([lax.dynamic_slice_in_dim(array, s, piece, axis) for s in starts], axis)

    saved = []
    for layer in range(layers):
        entered = carried
        mixed = entered + mixer(entered * live)
        normed, unit_first, inverse_first = normalize(mixed, ln_gain[layer, 0], ln_bias[layer, 0])
        normed_low = normed.astype(jnp.bfloat16)
        preact = wide(normed_low, up_weight[layer], (1, 0)) + up_bias[layer]
        hidden = gelu(preact).astype(jnp.bfloat16)
        branch = wide(hidden, down_weight[layer], (1, 0)) + down_bias[layer]
        carried, unit_second, inverse_second = normalize(normed + branch, ln_gain[layer, 1], ln_bias[layer, 1])
        all_normed = lax.all_gather(normed, PLANE, tiled=True)
        saved.append((unit_first, inverse_first, preact, unit_second, inverse_second, all_normed))
    outputs = gather_back(carried)

    minor = [None] * layers
    ups = [None] * layers
    downs = [None] * layers
    for layer in reversed(range(layers)):
        unit_first, inverse_first, preact, unit_second, inverse_second, all_normed = saved[layer]
        gain_second = jnp.sum(upstream * unit_second, 0)
        shift_second = jnp.sum(upstream, 0)
        delta_out = norm_back(upstream, unit_second, inverse_second, ln_gain[layer, 1])
        all_delta = lax.all_gather(delta_out, PLANE, tiled=True)
        delta_branch = delta_out.astype(jnp.bfloat16)
        down_vec = jnp.sum(delta_branch.astype(jnp.float32), 0)
        delta_hidden = wide(delta_branch, down_weight[layer], (1, 1))
        puller = jax.vjp(gelu, preact)[1]
        delta_preact = puller(delta_hidden)[0].astype(jnp.bfloat16)
        up_vec = jnp.sum(delta_preact.astype(jnp.float32), 0)
        delta_normed = delta_out + wide(delta_preact, up_weight[layer], (1, 1))
        gain_first = jnp.sum(delta_normed * unit_first, 0)
        shift_first = jnp.sum(delta_normed, 0)
        delta_mixed = norm_back(delta_normed, unit_first, inverse_first, ln_gain[layer, 0])
        upstream = delta_mixed + live * mixer(delta_mixed)

        up_cut, down_cut = cut(up_weight[layer], 1), cut(down_weight[layer], 0)
        bias_cut = cut(up_bias[layer], 0)
        both = weight_grads(all_normed, all_delta, up_cut, bias_cut, down_cut, planes)
        summed = lax.psum_scatter(both.reshape(planes * 2 * piece, width), ("zh", "zl"), scatter_dimension=0, tiled=True)
        whole = lax.all_gather(summed, ("dy", "core"))
        if lax.axis_size("do") > 1:
            whole = lax.psum(whole, "do")
        ups[layer] = whole[:, :piece].reshape(unit_block, width)
        downs[layer] = whole[:, piece:].reshape(unit_block, width)
        minor[layer] = lax.psum(
            jnp.concatenate(
                [jnp.stack([gain_first, gain_second, shift_first, shift_second, down_vec]), up_vec.reshape(-1, width)]
            ),
            ALL,
        )
    table_grad = lax.psum(jnp.stack([jnp.sum(jnp.where(kind == t, upstream, 0.0), 0) for t in range(types)]), ALL)
    input_grad = gather_back(upstream)
    minor = jnp.stack(minor)
    up_vec = minor[:, 5:].reshape(layers, hidden_width)
    up_vec = lax.dynamic_slice_in_dim(up_vec, lax.axis_index(SEQ) * unit_block, unit_block, 1)
    return (
        outputs,
        input_grad,
        table_grad,
        minor[:, 0:2],
        minor[:, 2:4],
        jnp.stack(ups).transpose(0, 2, 1),
        up_vec,
        jnp.stack(downs),
        minor[:, 4],
    )


def solution(mesh):
    dp, seq = mesh.shape["dp"], mesh.shape["seq"]
    shape = (dp // 4, 2, 2, 2, 2, seq // 4)
    finer = Mesh(mesh.devices.reshape(shape), ALL)
    in_specs = (P(DP, SEQ, None), P(DP, SEQ), P(DP, SEQ)) + (P(),) * 7 + (P(DP, SEQ, None),)
    out_specs = (
        P(DP, SEQ, None),
        P(DP, SEQ, None),
        P(),
        P(),
        P(),
        P(None, None, SEQ),
        P(None, SEQ),
        P(None, SEQ, None),
        P(),
    )
    return jax.shard_map(local, mesh=finer, in_specs=in_specs, out_specs=out_specs, check_vma=False)
```

time: 1230 us -> 633 us (0.51)
  waiting for transfers between devices: 833 us -> 262 us
  matrix products: 180 us -> 110 us
  local copies, waits for them, and re-layouts: 40.6 us -> 66.4 us
  Pallas kernels: 0 us -> 22.6 us
  other arithmetic: 23 us -> 43.6 us
    reduce_scatter x2, waiting for transfers between devices: 533 us -> 53.9 us  [local(): lax.psum_scatter(both.reshape(planes * 2 * piece, width), ('zh', 'zl'), s...]
    all_to_all x11 -> x7, waiting for transfers between devices: 181 us -> 20.8 us  [the longest x4 13.6 us: mixer(): lax.all_to_all(sent, ROW, 0, 0, tiled=True).reshape(count * chunk, width)]
    all_gather x0 -> x6, waiting for transfers between devices: none -> 97.9 us  [the longest x2 50.6 us: local(): all_normed = lax.all_gather(normed, PLANE, tiled=True)]
    unnamed x5 -> x9, waiting for transfers between devices: 72.1 us -> 1.09 us
    dot_general x46 -> x48, matrix products: 180 us -> 110 us  [the longest x40 64.9 us: precise(): return jnp.matmul(left, right, precision=lax.Precision.HIGHEST)]
    psum x2 -> x0, blocking collectives: 48.2 us -> none  [the longest x1 42 us: local(): lax.psum((gain_local, shift_local, down_vec_local, table_local), ('dp', '...]
    all_gather x0 -> x2, blocking collectives: none -> 46.1 us  [mark(): whole = lax.all_gather(values, SEQ)[:, lax.axis_index('zh')]]
    psum x1, waiting for transfers between devices: 46.4 us -> 88.3 us  [local(): lax.psum(jnp.stack([jnp.sum(jnp.where(kind == t, upstream, 0.0), 0) for t...]
  transfers between devices with their start and end apart: 15 -> 16, of which waited for: 14 -> 9; matrix products, arithmetic and copies ran while one was open for 10% -> 22% of each run, Pallas kernels for 0% -> 4%
where the time goes in v1:
time: 633 us; the launch traced here: 624 us
  waiting for transfers between devices  262 us (41%)
  matrix products  110 us (17%)
  blocking collectives  70.3 us (11%)
  local copies, waits for them, and re-layouts  66.4 us (10%)
  other arithmetic  43.6 us (7%)
  starting transfers between devices  32.1 us (5%)
  Pallas kernels  22.6 us (4%)
  between operations  17.2 us (3%)
    psum x1, waiting for transfers between devices, local(): lax.psum(jnp.stack([jnp.sum(jnp.where(kind == t, upstream, 0.0), 0) for t...  88.3 us
    dot_general x40, matrix products, precise(): return jnp.matmul(left, right, precision=lax.Precision.HIGHEST)  64.9 us
    reduce_scatter x2, waiting for transfers between devices, local(): lax.psum_scatter(both.reshape(planes * 2 * piece, width), ('zh', 'zl'), s...  53.9 us
    all_gather x2, waiting for transfers between devices, local(): all_normed = lax.all_gather(normed, PLANE, tiled=True)  50.6 us
    all_gather x2, waiting for transfers between devices, local(): all_delta = lax.all_gather(delta_out, PLANE, tiled=True)  47.3 us
    all_gather x2, blocking collectives, mark(): whole = lax.all_gather(values, SEQ)[:, lax.axis_index('zh')]  46.1 us
    dot_general x8, matrix products, wide(): lax.dot_general(left, right, ((contract[:1], contract[1:]), ((), ())), pr...  45.3 us
    all_to_all x1, blocking collectives, gather_back(): lax.all_to_all(values.reshape(seq, 2 * units, width), SEQ, 0, 0, tiled=True)  24.1 us
  transfers between devices with their start and end apart: 16, of which 9 were waited for; matrix products, arithmetic and copies ran while one was open for 22% of the time, Pallas kernels for 4%

profile of v1, /device:TPU:0, one launch (start us, length us, event | category | flops | bytes accessed | tf_op | source)
XLA Modules:
  0.0 624.5 jit_solution(6350584785261161636)
XLA Ops:
  12.9 7.4 %all-to-all-start = ((f32[8,32,768]{2,1,0:T(8,128)}), f32[8,32,768]{2,1,0:T(8,128)S(1)}, u32[]{:S(2)}, u32[]{:S(2)}) async-start(f32[8,32,768]{2,1,0:T(8,128)} %bitcast.7), calls=%async_computation | async-start | bytes 1572864 | tf_op jit(solution)/shard_map/all_to_all | solution.py:215
  21.0 26.6 %all-gather.4 = s32[8,2,128]{2,1,0:T(2,128)S(1)} all-gather(s32[1,2,128]{2,1,0:T(2,128)S(1)} %bitcast.380), channel_id=2, replica_groups=mesh['do'=1,'dy'=2,'core'=2,'zh'=2,'zl'=2,'x'=2] {'zh','zl','x'}, dimensions={0}, use_global_device_ids=true | all-gather | bytes 9216 | tf_op jit(solution)/shard_map/all_gather | solution.py:224
  47.6 19.5 %all-gather.5 = s32[8,2,128]{2,1,0:T(2,128)S(1)} all-gather(s32[1,2,128]{2,1,0:T(2,128)S(1)} %bitcast.375), channel_id=3, replica_groups=mesh['do'=1,'dy'=2,'core'=2,'zh'=2,'zl'=2,'x'=2] {'zh','zl','x'}, dimensions={0}, use_global_device_ids=true | all-gather | bytes 9216 | tf_op jit(solution)/shard_map/all_gather | solution.py:224
  69.8 2.8 gather_fusion.2
  76.5 4.2 all-to-all-start.4
  87.9 7.2 %all-to-all-done.4 = f32[8,32,768]{2,1,0:T(8,128)} async-done(((f32[8,32,768]{2,1,0:T(8,128)}), f32[8,32,768]{2,1,0:T(8,128)}, u32[]{:S(2)}, u32[]{:S(2)}) %all-to-all-start.4) | async-done | bytes 786464 | tf_op jit(solution)/shard_map/all_to_all | solution.py:215
  95.1 3.6 all-to-all-start.1
  102.5 2.4 fusion.103
  109.9 2.3 fusion.211
  112.5 2.3 reverse
  124.7 5.5 fusion.16
  131.6 5.5 fusion.217
  137.4 2.3 fusion.75
  144.5 4.2 all-to-all-start.2
  152.6 2.4 fusion.97
  160.0 2.3 fusion.208
  163.3 2.9 reverse.1
  169.8 4.0 fusion.19
  173.9 5.5 fusion.218
  181.6 3.2 convert_reduce_fusion.2
  186.4 7.0 %convert_reduce_fusion = (f32[3072]{0:T(1024)}, bf16[256,3072]{1,0:T(8,128)(2,1)S(1)}) fusion(f32[256,3072]{1,0:T(8,128)} %copy-done.63, bf16[2,3072,768]{2,1,0:T(8,128)(2,1)} %param.34, f32[256,768]{1,0:T(8,128)} %get-tuple-element.86), kind=kOutput, calls=%fused_computation.42 | convolution fusion | flops 1225454592 | bytes 10235904 | tf_op jit(solution)/shard_map/dot_general | solution.py:115
  193.4 4.7 multiply_reduce_fusion
  205.4 4.2 all-to-all-start.5
  211.5 2.4 fusion.91
  213.9 3.5 all-to-all-done.5
  222.4 2.3 fusion.206
  225.7 2.9 reverse.2
  228.8 2.5 multiply_reduce_fusion.1
  234.9 6.5 %fusion.212 = (bf16[1,3072,768]{2,1,0:T(8,128)(2,1)S(1)}, bf16[1,3072,768]{2,1,0:T(8,128)(2,1)}) fusion(bf16[2,3072,768]{2,1,0:T(8,128)(2,1)} %param.34), kind=kLoop, calls=%fused_computation.382 | loop fusion | bytes 18874368 | tf_op jit(solution)/shard_map/slice | solution.py:278
  243.6 6.8 %fusion.213 = (bf16[1,768,3072]{2,1,0:T(8,128)(2,1)S(1)}, bf16[1,768,3072]{2,1,0:T(8,128)(2,1)}) fusion(bf16[2,768,3072]{2,1,0:T(8,128)(2,1)} %param.32), kind=kLoop, calls=%fused_computation.383 | loop fusion | bytes 18874368 | tf_op jit(solution)/shard_map/slice | solution.py:276
  250.4 2.8 dynamic-slice_bitcast_fusion.17
  253.6 26.6 %all-gather.17.cloned.1.call-done.normed_ref = f32[2048,768]{1,0:T(8,128)} async-done(((f32[256,768]{1,0:T(8,128)}), f32[2048,768]{1,0:T(8,128)}) %all-gather.17.cloned.1.call-update) | async-done | bytes 6291472 | tf_op jit(solution)/shard_map/all_gather | solution.py:280
  280.2 11.3 %weight_grads.3 = f32[4,192,768]{2,1,0:T(8,128)} custom-call(f32[2048,768]{1,0:T(8,128)} %all-gather.17.cloned.1.call-done.normed_ref, f32[2048,768]{1,0:T(8,128)} %all-gather.19.cloned.1.call-done.delta_ref, bf16[768,384]{1,0:T(8,128)(2,1)S(1)} %pad_maximum_fusion.3.up_ref, f32[1,384]{1,0:T(1,128)S(1)} %reshape.429.bias_ref, ...), custom_call_target="tpu_custom_call" | custom-call | flops 4831838208 | bytes 12582912 | tf_op jit(solution)/shard_map/weight_grads/pallas_call | solution.py:173
  296.0 8.2 %convert_reduce_fusion.1 = (f32[3072]{0:T(1024)}, bf16[256,3072]{1,0:T(8,128)(2,1)}) fusion(f32[256,3072]{1,0:T(8,128)} %fusion.16, bf16[2,3072,768]{2,1,0:T(8,128)(2,1)} %param.34, f32[256,768]{1,0:T(8,128)} %get-tuple-element.84), kind=kOutput, calls=%fused_computation.43 | convolution fusion | flops 1225454592 | bytes 10235904 | tf_op jit(solution)/shard_map/dot_general | solution.py:115
  304.2 24.0 %all-gather.13.cloned.1.call-done.normed_ref = f32[2048,768]{1,0:T(8,128)} async-done(((f32[256,768]{1,0:T(8,128)}), f32[2048,768]{1,0:T(8,128)}) %all-gather.13.cloned.1.call-update) | async-done | bytes 6291472 | tf_op jit(solution)/shard_map/all_gather | solution.py:280
  328.2 47.3 %all-gather.15.cloned.1.call-done.delta_ref = f32[2048,768]{1,0:T(8,128)} async-done(((f32[256,768]{1,0:T(8,128)}), f32[2048,768]{1,0:T(8,128)}) %all-gather.15.cloned.1.call-update) | async-done | bytes 6291472 | tf_op jit(solution)/shard_map/all_gather | solution.py:292
  375.5 11.3 %weight_grads.2 = f32[4,192,768]{2,1,0:T(8,128)} custom-call(f32[2048,768]{1,0:T(8,128)} %all-gather.13.cloned.1.call-done.normed_ref, f32[2048,768]{1,0:T(8,128)} %all-gather.15.cloned.1.call-done.delta_ref, bf16[768,384]{1,0:T(8,128)(2,1)S(1)} %pad_maximum_fusion.1.up_ref, f32[1,384]{1,0:T(1,128)S(1)} %reshape.427.bias_ref, ...), custom_call_target="tpu_custom_call" | custom-call | flops 4831838208 | bytes 12582912 | tf_op jit(solution)/shard_map/weight_grads/pallas_call | solution.py:173
  386.9 4.9 multiply_reduce_fusion.2
  399.0 3.7 all-to-all-start.6
  408.0 10.1 %all-to-all-done.6 = f32[4,32,768]{2,1,0:T(8,128)S(1)} async-done(((f32[4,32,768]{2,1,0:T(8,128)}), f32[4,32,768]{2,1,0:T(8,128)S(1)}, u32[]{:S(2)}, u32[]{:S(2)}) %all-to-all-start.6) | async-done | bytes 393248 | tf_op jit(solution)/shard_map/all_to_all | solution.py:242
  426.8 3.4 reduce-scatter.5.cloned.1.call-done
  430.4 50.5 %reduce-scatter.3.cloned.1.call-done = f32[192,768]{1,0:T(8,128)} async-done(((f32[768,768]{1,0:T(8,128)}), f32[192,768]{1,0:T(8,128)}) %reduce-scatter.3.cloned.1.call-update) | async-done | bytes 589840 | tf_op jit(solution)/shard_map/reduce_scatter | solution.py:308
  480.9 24.1 %all_to_all.40 = f32[8,32,768]{2,1,0:T(8,128)S(1)} all-to-all(f32[8,32,768]{2,1,0:T(8,128)S(1)} %bitcast.333), channel_id=1, replica_groups=mesh['do'=1,'dy'=2,'core'=2,'zh'=2,'zl'=2,'x'=2] {'zh','zl','x'}, dimensions={0} | all-to-all | bytes 1572864 | tf_op jit(solution)/shard_map/all_to_all | solution.py:218
  505.0 3.6 all-to-all-start.7
  508.6 88.3 %all-reduce.3.cloned.1.call-done = (f32[4,768]{1,0:T(4,128)}, f32[1,9,768]{2,0,1:T(1,128)}, f32[1,9,768]{2,0,1:T(1,128)}) async-done(((f32[4,768]{1,0:T(4,128)}, f32[1,9,768]{2,0,1:T(1,128)}, f32[1,9,768]{2,0,1:T(1,128)}), (f32[4,768]{1,0:T(4,128)}, f32[1,9,768]{2,0,1:T(1,128)}, f32[1,9,768]{2,0,1:T(1,128)})) %all-reduce.3.cloned.1.call-update) | async-done | bytes 67600 | tf_op jit(solution)/shard_map/psum | solution.py:320
  605.5 2.9 fusion.215
  608.3 2.9 fusion.214
  613.3 2.8 pad_maximum_fusion
  (326 shorter events, 119.6 us)
Async XLA Ops:
  11.0 10.0 %copy-start.60 = (s32[2,128]{1,0:T(2,128)S(1)}, s32[2,128]{1,0:T(2,128)}, u32[]{:S(2)}) copy-start(s32[2,128]{1,0:T(2,128)} %param.28) | copy-start | bytes 3076
  11.1 36.6 %copy-start.57 = (s32[2,128]{1,0:T(2,128)S(1)}, s32[2,128]{1,0:T(2,128)}, u32[]{:S(2)}) copy-start(s32[2,128]{1,0:T(2,128)} %param.27) | copy-start | bytes 3076
  11.1 57.6 %copy-start.16 = (f32[2,128,768]{2,1,0:T(8,128)S(1)}, f32[2,128,768]{2,1,0:T(8,128)}, u32[]{:S(2)}) copy-start(f32[2,128,768]{2,1,0:T(8,128)} %param.36) | copy-start | bytes 2359300
  12.9 61.8 %copy-start.51 = (f32[2,768]{1,0:T(2,128)S(1)}, f32[2,768]{1,0:T(2,128)}, u32[]{:S(2)}) copy-start(f32[2,768]{1,0:T(2,128)} %param.35) | copy-start | bytes 18436
  12.9 62.4 %copy-start.41 = (f32[2,2,768]{2,1,0:T(2,128)S(1)}, f32[2,2,768]{2,1,0:T(2,128)}, u32[]{:S(2)}) copy-start(f32[2,2,768]{2,1,0:T(2,128)} %param.31) | copy-start | bytes 36868
  12.9 62.4 %copy-start.42 = (f32[2,2,768]{2,1,0:T(2,128)S(1)}, f32[2,2,768]{2,1,0:T(2,128)}, u32[]{:S(2)}) copy-start(f32[2,2,768]{2,1,0:T(2,128)} %param.30) | copy-start | bytes 36868
  12.9 63.0 %copy-start.29 = (f32[2,3072]{1,0:T(2,128)S(1)}, f32[2,3072]{1,0:T(2,128)}, u32[]{:S(2)}) copy-start(f32[2,3072]{1,0:T(2,128)} %param.33) | copy-start | bytes 73732
  12.9 63.7 %all-to-all-start = ((f32[8,32,768]{2,1,0:T(8,128)}), f32[8,32,768]{2,1,0:T(8,128)S(1)}, u32[]{:S(2)}, u32[]{:S(2)}) async-start(f32[8,32,768]{2,1,0:T(8,128)} %bitcast.7), calls=%async_computation | async-start | bytes 1572864 | tf_op jit(solution)/shard_map/all_to_all | solution.py:215
  21.0 48.8 %copy-start.52 = (pred[2]{0:T(512)(128)(4,1)}, pred[2]{0:T(512)(128)(4,1)S(1)}, u32[]{:S(2)}) copy-start(pred[2]{0:T(512)(128)(4,1)S(1)} %get-tuple-element.103) | copy-start | bytes 10
  68.7 12.1 %copy-start.26 = (f32[256]{0:T(256)}, f32[256]{0:T(256)S(1)}, u32[]{:S(2)}) copy-start(f32[256]{0:T(256)S(1)} %convert_element_type.59) | copy-start | bytes 3076
  69.8 11.1 %copy-start = (f32[768,768]{1,0:T(8,128)S(1)}, f32[768,768]{1,0:T(8,128)}, u32[]{:S(2)}) copy-start(f32[768,768]{1,0:T(8,128)} %constant.144.clone) | copy-start | bytes 7077892
  75.9 54.2 %copy-start.17 = (f32[768]{0:T(1024)}, f32[768]{0:T(1024)S(1)}, u32[]{:S(2)}) copy-start(f32[768]{0:T(1024)S(1)} %get-tuple-element.167) | copy-start | bytes 9220
  76.5 18.6 %all-to-all-start.4 = ((f32[8,32,768]{2,1,0:T(8,128)}), f32[8,32,768]{2,1,0:T(8,128)}, u32[]{:S(2)}, u32[]{:S(2)}) async-start(f32[8,32,768]{2,1,0:T(8,128)} %bitcast.326), calls=%async_computation.4 | async-start | bytes 1572864 | tf_op jit(solution)/shard_map/all_to_all | solution.py:215
  83.2 11.9 %copy-start.48 = (f32[256]{0:T(256)}, f32[256]{0:T(256)S(1)}, u32[]{:S(2)}) copy-start(f32[256]{0:T(256)S(1)} %slice_reduce_fusion.3) | copy-start | bytes 3076
  95.1 9.8 %all-to-all-start.1 = ((f32[4,32,768]{2,1,0:T(8,128)}), f32[4,32,768]{2,1,0:T(8,128)S(1)}, u32[]{:S(2)}, u32[]{:S(2)}) async-start(f32[4,32,768]{2,1,0:T(8,128)} %bitcast.348), calls=%async_computation.1 | async-start | bytes 786432 | tf_op jit(solution)/shard_map/all_to_all | solution.py:242
  137.3 7.2 %copy-start.24 = (f32[256]{0:T(256)}, f32[256]{0:T(256)S(1)}, u32[]{:S(2)}) copy-start(f32[256]{0:T(256)S(1)} %add_rsqrt_fusion.3) | copy-start | bytes 3076
  139.7 9.2 %copy-start.39 = (f32[8,32]{1,0:T(8,128)S(1)}, f32[8,32]{1,0:T(8,128)}, u32[]{:S(2)}) copy-start(f32[8,32]{1,0:T(8,128)} %get-tuple-element.60) | copy-start | bytes 3076
  144.5 10.6 %all-to-all-start.2 = ((f32[4,32,768]{2,1,0:T(8,128)}), f32[4,32,768]{2,1,0:T(8,128)S(1)}, u32[]{:S(2)}, u32[]{:S(2)}) async-start(f32[4,32,768]{2,1,0:T(8,128)} %bitcast.349), calls=%async_computation.2 | async-start | bytes 786432 | tf_op jit(solution)/shard_map/all_to_all | solution.py:242
  148.7 105.0 %all-gather.19.cloned.1.call-start = ((), (), s32[]{:S(2)}) async-start(), calls=%async_computation.14 | async-start | bytes 7077888 | tf_op jit(solution)/shard_map/all_gather | solution.py:292
  173.8 7.8 %copy-start.31 = (f32[768]{0:T(1024)S(1)}, f32[768]{0:T(1024)}, u32[]{:S(2)}) copy-start(f32[768]{0:T(1024)} %get-tuple-element.70) | copy-start | bytes 9220
  173.8 7.8 %copy-start.54 = (f32[256]{0:T(256)S(1)}, f32[256]{0:T(256)}, u32[]{:S(2)}) copy-start(f32[256]{0:T(256)} %div.62) | copy-start | bytes 3076
  184.9 95.3 %all-gather.17.cloned.1.call-start = ((), (), s32[]{:S(2)}) async-start(), calls=%async_computation.13 | async-start | bytes 7077888 | tf_op jit(solution)/shard_map/all_gather | solution.py:280
  185.6 142.6 %all-gather.13.cloned.1.call-start = ((), (), s32[]{:S(2)}) async-start(), calls=%async_computation.10 | async-start | bytes 7077888 | tf_op jit(solution)/shard_map/all_gather | solution.py:280
  205.4 12.0 %all-to-all-start.5 = ((f32[4,32,768]{2,1,0:T(8,128)}), f32[4,32,768]{2,1,0:T(8,128)S(1)}, u32[]{:S(2)}, u32[]{:S(2)}) async-start(f32[4,32,768]{2,1,0:T(8,128)} %bitcast.350), calls=%async_computation.5 | async-start | bytes 786432 | tf_op jit(solution)/shard_map/all_to_all | solution.py:242
  209.5 165.9 %all-gather.15.cloned.1.call-start = ((), (), s32[]{:S(2)}) async-start(), calls=%async_computation.11 | async-start | bytes 7077888 | tf_op jit(solution)/shard_map/all_gather | solution.py:292
  220.0 8.7 %copy-start.23 = (f32[256]{0:T(256)S(1)}, f32[256]{0:T(256)}, u32[]{:S(2)}) copy-start(f32[256]{0:T(256)} %copy-done.22) | copy-start | bytes 3076
  220.1 8.7 %copy-start.25 = (f32[256]{0:T(256)S(1)}, f32[256]{0:T(256)}, u32[]{:S(2)}) copy-start(f32[256]{0:T(256)} %copy-done.24) | copy-start | bytes 3076
  233.1 197.2 %reduce-scatter.5.cloned.1.call-start = ((), (), s32[]{:S(2)}) async-start(), calls=%async_computation.15 | async-start | bytes 2949120 | tf_op jit(solution)/shard_map/reduce_scatter | solution.py:308
  253.6 38.0 %copy-start.40 = (s32[8,128]{1,0:T(8,128)S(1)}, s32[8,128]{1,0:T(8,128)}, u32[]{:S(2)}) copy-start(s32[8,128]{1,0:T(8,128)} %get-tuple-element.165) | copy-start | bytes 12292
  291.5 189.3 %reduce-scatter.3.cloned.1.call-start = ((), (), s32[]{:S(2)}) async-start(), calls=%async_computation.12 | async-start | bytes 2949120 | tf_op jit(solution)/shard_map/reduce_scatter | solution.py:308
  392.1 10.8 %copy-start.53 = (pred[2]{0:T(512)(128)(4,1)S(1)}, pred[2]{0:T(512)(128)(4,1)}, u32[]{:S(2)}) copy-start(pred[2]{0:T(512)(128)(4,1)} %copy-done.52) | copy-start | bytes 10
  392.1 11.3 %copy-start.33 = (f32[768]{0:T(1024)S(1)}, f32[768]{0:T(1024)}, u32[]{:S(2)}) copy-start(f32[768]{0:T(1024)} %get-tuple-element.59) | copy-start | bytes 9220
  392.1 11.3 %copy-start.59 = (f32[768]{0:T(1024)S(1)}, f32[768]{0:T(1024)}, u32[]{:S(2)}) copy-start(f32[768]{0:T(1024)} %get-tuple-element.50) | copy-start | bytes 9220
  392.1 11.3 %copy-start.58 = (f32[768]{0:T(1024)S(1)}, f32[768]{0:T(1024)}, u32[]{:S(2)}) copy-start(f32[768]{0:T(1024)} %get-tuple-element.61) | copy-start | bytes 9220
  392.1 11.3 %copy-start.43 = (f32[3072]{0:T(1024)S(1)}, f32[3072]{0:T(1024)}, u32[]{:S(2)}) copy-start(f32[3072]{0:T(1024)} %get-tuple-element.160) | copy-start | bytes 36868
  392.1 11.3 %copy-start.35 = (f32[768]{0:T(1024)S(1)}, f32[768]{0:T(1024)}, u32[]{:S(2)}) copy-start(f32[768]{0:T(1024)} %get-tuple-element.85) | copy-start | bytes 9220
  392.1 11.3 %copy-start.34 = (f32[768]{0:T(1024)S(1)}, f32[768]{0:T(1024)}, u32[]{:S(2)}) copy-start(f32[768]{0:T(1024)} %get-tuple-element.48) | copy-start | bytes 9220
  392.2 12.1 %copy-start.45 = (f32[3072]{0:T(1024)S(1)}, f32[3072]{0:T(1024)}, u32[]{:S(2)}) copy-start(f32[3072]{0:T(1024)} %get-tuple-element.162) | copy-start | bytes 36868
  392.2 12.1 %copy-start.38 = (f32[768]{0:T(1024)S(1)}, f32[768]{0:T(1024)}, u32[]{:S(2)}) copy-start(f32[768]{0:T(1024)} %get-tuple-element.83) | copy-start | bytes 9220
  392.2 12.1 %copy-start.37 = (f32[768]{0:T(1024)S(1)}, f32[768]{0:T(1024)}, u32[]{:S(2)}) copy-start(f32[768]{0:T(1024)} %get-tuple-element.46) | copy-start | bytes 9220
  392.2 12.2 %copy-start.36 = (f32[768]{0:T(1024)S(1)}, f32[768]{0:T(1024)}, u32[]{:S(2)}) copy-start(f32[768]{0:T(1024)} %get-tuple-element.57) | copy-start | bytes 9220
  399.0 19.1 %all-to-all-start.6 = ((f32[4,32,768]{2,1,0:T(8,128)}), f32[4,32,768]{2,1,0:T(8,128)S(1)}, u32[]{:S(2)}, u32[]{:S(2)}) async-start(f32[4,32,768]{2,1,0:T(8,128)} %bitcast.54), calls=%async_computation.6 | async-start | bytes 786432 | tf_op jit(solution)/shard_map/all_to_all | solution.py:242
  402.6 194.3 %all-reduce.3.cloned.1.call-start = ((), (), s32[]{:S(2)}) async-start(), calls=%async_computation.18 | async-start | bytes 135168 | tf_op jit(solution)/shard_map/psum | solution.py:320
  423.8 57.1 %copy-start.13 = (f32[256,768]{1,0:T(8,128)S(1)}, f32[256,768]{1,0:T(8,128)}, u32[]{:S(2)}) copy-start(f32[256,768]{1,0:T(8,128)} %get-tuple-element.129) | copy-start | bytes 2359300
  424.8 83.8 %copy-start.61 = (s32[8]{0:T(128)S(1)}, s32[8]{0:T(128)}, u32[]{:S(2)}) copy-start(s32[8]{0:T(128)} %constant.159) | copy-start | bytes 100
  426.8 178.7 %all-gather.23.cloned.1.call-start = ((), (), s32[]{:S(2)}) async-start(), calls=%async_computation.17 | async-start | bytes 2949120 | tf_op jit(solution)/shard_map/all_gather | solution.py:309
  430.3 178.0 %all-gather.21.cloned.1.call-start = ((), (), s32[]{:S(2)}) async-start(), calls=%async_computation.16 | async-start | bytes 2949120 | tf_op jit(solution)/shard_map/all_gather | solution.py:309
  505.0 98.5 %all-to-all-start.7 = ((f32[8,32,768]{2,1,0:T(8,128)}), f32[8,32,768]{2,1,0:T(8,128)S(1)}, u32[]{:S(2)}, u32[]{:S(2)}) async-start(f32[8,32,768]{2,1,0:T(8,128)} %bitcast.58), calls=%async_computation.7 | async-start | bytes 1572864 | tf_op jit(solution)/shard_map/all_to_all | solution.py:218
  (32 other events, 144.7 us)
Sparse Core Ops, SparseCore 0:
  185.0 47.1 all-gather.18
  234.6 45.5 all-gather.16
  282.6 45.5 all-gather.12
  329.9 45.5 all-gather.14
  378.2 52.0 reduce-scatter.4
  433.0 47.7 reduce-scatter.2
  482.4 23.6 all-gather.22
  507.7 24.1 all-gather.20
Sparse Core Ops, SparseCore 1:
  426.9 170.0 all-reduce.2

commit v2 on v1

v2 whole, which is shorter than its diff:
```python
import functools
import math

import jax
import jax.numpy as jnp
import ml_dtypes
import numpy as np
from jax import lax
from jax.experimental import pallas as pl
from jax.experimental.pallas import tpu as pltpu
from jax.sharding import Mesh
from jax.sharding import PartitionSpec as P

EPSILON = 1e-05
DP = ("do", "dy", "core")
SEQ = ("zh", "zl", "x")
ROW = ("zl", "x")
PLANES = ("zh", "zl")
SHARES = ("dy", "core")
PLANE = ("dy", "core", "x")
ALL = DP + SEQ
MARK = 128
LOW = jnp.bfloat16
HIGH = jnp.float32
VMEM = pl.BlockSpec(memory_space=pltpu.VMEM)
SMEM = pl.BlockSpec(memory_space=pltpu.SMEM)


def split_table(values):
    head = values.astype(ml_dtypes.bfloat16)
    return np.stack([head, (values - head.astype(np.float64)).astype(ml_dtypes.bfloat16)])


def feature_table(width):
    half = width // 2
    angle = np.outer(np.arange(width), np.arange(width)) % width * (2.0 * math.pi / width)
    cos, sin = np.cos(angle) / math.sqrt(width), np.sin(angle) / math.sqrt(width)
    return split_table(np.concatenate([cos[:, :half], cos[:, half : half + 1], sin[:, 1:half]], 1))


def mirror_table(half):
    table = np.zeros((half, half), ml_dtypes.bfloat16)
    table[half - np.arange(1, half), np.arange(1, half)] = 1.0
    return table


def pair_of(count, at):
    return at, 2 * count - at if at else count


def owned(count, part, seq, at):
    first, second = pair_of(count, at)
    pos = np.arange(seq * part).reshape(seq, part // (2 * count), 2 * count)
    return np.stack([pos[:, :, first], pos[:, :, second]], 1).reshape(-1)


def position_tables(count, part, seq):
    length = seq * part
    step = 2 * count
    span = length // step
    keep = span // step
    w = 2.0 * math.pi / length
    own = [owned(count, part, seq, i) for i in range(count)]
    local = length // count
    send = np.zeros((2, count, count, 2 * keep, local))
    recv = np.zeros((2, count, count, local, 2 * keep))
    block = np.zeros((2, count, local, local))
    scale = 1.0 / math.sqrt(length)

    def kept(i):
        if i:
            return [(i + step * s, 2) for s in range(keep)]
        ends = [(step * s, 1 if s in (0, keep // 2) else 2) for s in range(keep // 2 + 1)]
        return ends + [(count + step * s, 2) for s in range(keep // 2)]

    for j in range(count):
        n = own[j]
        first = n % step == j
        theta = 2.0 * math.pi * j / step
        for i in range(count):
            if i == j:
                angle = w * (np.outer(n, n) % length)
                block[0, i], block[1, i] = np.cos(angle) * scale, np.sin(angle) * scale
                continue
            at = 0
            slots = {}
            for kap, kinds in kept(i):
                cos, sin = np.cos(w * (kap * n % length)), np.sin(w * (kap * n % length))
                if j:
                    sign = np.where(first, 1.0, -1.0)
                    rows = (cos, sign * sin, sign * cos, sin)
                else:
                    rows = (cos * first, cos * ~first, sin * first, sin * ~first)
                if kinds == 2:
                    send[0, j, i, at], send[0, j, i, at + 1] = rows[:2]
                    send[1, j, i, at], send[1, j, i, at + 1] = rows[2:]
                    slots[kap] = (at, at + 1, 0.0)
                else:
                    phi = w * (kap * j % length)
                    send[0, j, i, at] = math.cos(phi) * rows[0] + math.sin(phi) * rows[1]
                    send[1, j, i, at] = math.cos(phi) * rows[2] + math.sin(phi) * rows[3]
                    slots[kap] = (at, at, phi)
                at += kinds
            for index, k in enumerate(own[i]):
                kap, turn = k % span, k // span
                mirrored = kap not in slots
                p_at, q_at, phi = slots[(span - kap) % span if mirrored else kap]
                pair = np.zeros((2, 2 * keep))
                if p_at == q_at:
                    pair[0, p_at], pair[1, p_at] = math.cos(phi), math.sin(phi)
                else:
                    pair[0, p_at], pair[1, q_at] = 1.0, 1.0
                even, odd = pair, pair
                if j:
                    if mirrored:
                        c, s = math.cos(theta), math.sin(theta)
                        even = odd = np.stack([c * pair[0] + s * pair[1], s * pair[0] - c * pair[1]])
                    c, s = math.cos(theta * turn), math.sin(theta * turn)
                    recv[0, i, j, index] = c * even[0] - s * even[1]
                    recv[1, i, j, index] = s * odd[0] + c * odd[1]
                else:
                    flip = (-1.0) ** turn
                    if mirrored:
                        even, odd = pair * np.array([[1.0], [-1.0]]), pair * np.array([[-1.0], [1.0]])
                    recv[0, i, j, index] = even[0] + flip * even[1]
                    recv[1, i, j, index] = odd[0] + flip * odd[1]
    recv = recv * scale
    sends, recvs, blocks = [], [], []
    for at in range(seq):
        i = at % count
        order = np.arange(local).reshape(seq, -1)[[at ^ k for k in range(seq)]].reshape(-1)
        others = [i ^ k for k in range(1, count)]
        sends.append(send[:, i, others].reshape(2, -1, local)[:, :, order])
        cos = np.concatenate([recv[0, i, j] for j in others], 1)[order]
        sin = np.concatenate([recv[1, i, j] for j in others], 1)[order]
        recvs.append(np.stack([np.concatenate([cos, -sin], 1), np.concatenate([cos, sin], 1)]))
        cos, sin = (block[h, i][order][:, order] for h in range(2))
        blocks.append(np.stack([np.concatenate([cos, -sin], 1), np.concatenate([cos, sin], 1)]))
    return tuple(np.moveaxis(split_table(np.stack(t)), 0, 1) for t in (sends, recvs, blocks))


def wide(left, right, contract=(1, 0)):
    return lax.dot_general(left, right, ((contract[:1], contract[1:]), ((), ())), preferred_element_type=HIGH)


def split(values):
    head = values.astype(LOW)
    return head, (values - head.astype(HIGH)).astype(LOW)


def triple(left, right):
    return wide(left[0], right[0]) + wide(left[0], right[1]) + wide(left[1], right[0])


def first_lane(values):
    return lax.broadcasted_iota(jnp.int32, values.shape, 1) == 0


def mean(values):
    return jnp.mean(values, axis=-1, keepdims=True)


def normalize(values):
    centered = values - mean(values)
    inverse = lax.rsqrt(mean(centered * centered) + EPSILON)
    return centered * inverse, inverse


def norm_back(upstream, unit, inverse, gain):
    scaled = upstream * gain
    return inverse * (scaled - mean(scaled) - unit * mean(scaled * unit))


def gelu_parts(p):
    c = math.sqrt(2.0 / math.pi)
    square = p * p
    t = jnp.tanh(p * (c + 0.044715 * c * square))
    halves = 0.5 + 0.5 * t
    slope = halves + p * (0.5 - 0.5 * (t * t)) * (c + 3.0 * 0.044715 * c * square)
    return p * halves, slope


def stage_one(values, feature_ref, send_ref, spectrum_ref, sent_refs):
    half = values.shape[1] // 2
    parts = split(values)
    spectrum = triple(parts, (feature_ref[0], feature_ref[1]))
    spectrum_ref[...] = spectrum
    head, tail = split(spectrum)
    lanes = half + 128
    even = triple((send_ref[0, 0], send_ref[1, 0]), (head[:, :lanes], tail[:, :lanes]))
    odd = triple((send_ref[0, 1], send_ref[1, 1]), (head[:, half:], tail[:, half:]))
    middle = jnp.where(first_lane(even[:, half:]), even[:, half:], odd[:, :128])
    rows = sent_refs[0].shape[0]
    for k, ref in enumerate(sent_refs):
        at = slice(k * rows, (k + 1) * rows)
        ref[:, :half] = even[at, :half]
        ref[:, half:lanes] = middle[at]
        ref[:, lanes:] = odd[at, 128:]


def unpack(packed, mirror, table_ref):
    half = packed.shape[1] // 2
    head, tail = split(packed)

    def stack(part):
        low, high = part[:, :half], part[:, half:]
        back = wide(jnp.concatenate([low, high], 0), mirror).astype(LOW)
        count = low.shape[0]
        turned = back[:count]
        middle = jnp.where(first_lane(turned[:, :128]), high[:, :128].astype(HIGH), turned[:, :128].astype(HIGH))
        turned = jnp.concatenate([middle.astype(LOW), turned[:, 128:]], 1)
        edge = jnp.where(first_lane(high[:, :128]), 0.0, high[:, :128].astype(HIGH)).astype(LOW)
        high = jnp.concatenate([edge, high[:, 128:]], 1)
        return jnp.concatenate([low, high], 0), jnp.concatenate([turned, back[count:]], 0)

    head_pair, tail_pair = stack(head), stack(tail)
    sides = [
        triple((table_ref[0, side], table_ref[1, side]), (head_pair[side], tail_pair[side])) for side in range(2)
    ]
    return jnp.concatenate(sides, 1)


def stage_two(got_refs, mirror_ref, recv_ref):
    got = jnp.concatenate([ref[...] for ref in got_refs], 0)
    return unpack(got, mirror_ref[...], recv_ref)


def call(kernel, name, inputs, outs, flops=0, **more):
    size = sum(math.prod(a.shape) * a.dtype.itemsize for a in list(inputs) + list(outs))
    more.setdefault("in_specs", [SMEM if a.dtype == jnp.int32 and a.shape == (1,) else VMEM for a in inputs])
    more.setdefault("out_specs", [VMEM] * len(outs))
    results = pl.pallas_call(
        kernel,
        out_shape=list(outs),
        compiler_params=pltpu.CompilerParams(vmem_limit_bytes=32 * 2**20),
        cost_estimate=pl.CostEstimate(flops=flops, bytes_accessed=size, transcendentals=0),
        name=name,
        **more,
    )(*inputs)
    return list(results)


def array(*shape, dtype=HIGH):
    return jax.ShapeDtypeStruct(shape, dtype)


def class_rows(count, units, dest):
    row, i = dest // count, dest % count
    second = jnp.where(i == 0, count, 2 * count - i)
    return row, (i, second)


def spread_body(count, marked, at_ref, refs):
    if marked:
        values_ref, segments_ref, padding_ref, table_ref, *outs, held = refs
    else:
        values_ref, *outs, held = refs
    rows, part, width = values_ref.shape
    units = part // (2 * count)
    for row in range(rows):
        values = values_ref[row]
        if marked:
            kind = segments_ref[row]
            for t in range(table_ref.shape[0]):
                values = values + jnp.where(kind == t, table_ref[t : t + 1, :], 0.0)
            lane = lax.broadcasted_iota(jnp.int32, (part, MARK), 1)
            live = padding_ref[row].astype(HIGH)
            held[row, :, :, width:] = jnp.where(
                lane == 0, live, jnp.where(lane == 1, kind.astype(HIGH), 0.0)
            ).reshape(units, 2 * count, MARK)
        held[row, :, :, :width] = values.reshape(units, 2 * count, width)
    for k, out in enumerate(outs):
        row, classes = class_rows(count, units, at_ref[0] ^ k)
        for h, at in enumerate(classes):
            out[h * units : (h + 1) * units, :] = held[row, :, at, :]


def collect_kernel(count, at_ref, *refs):
    *blocks, out = refs
    rows, units, step, width = out.shape
    for k, ref in enumerate(blocks):
        row, classes = class_rows(count, units, at_ref[0] ^ k)
        for h, at in enumerate(classes):
            out[row, :, at, :] = ref[h * units : (h + 1) * units, :]


def enter_kernel(blocks, *refs):
    held = refs[:blocks]
    feature_ref, send_ref, carried_ref, marks_ref, spectrum_ref, *sent_refs = refs[blocks:]
    width = carried_ref.shape[1]
    values = jnp.concatenate([ref[...] for ref in held], 0)
    carried_ref[...] = values[:, :width]
    marks_ref[...] = values[:, width:]
    stage_one(values[:, :width] * values[:, width : width + 1], feature_ref, send_ref, spectrum_ref, sent_refs)


def own_kernel(masked, *refs):
    if masked:
        spectrum_ref, carried_ref, mirror_ref, block_ref, marks_ref, out_ref = refs
    else:
        spectrum_ref, carried_ref, mirror_ref, block_ref, out_ref = refs
    mixed = unpack(spectrum_ref[...], mirror_ref[...], block_ref)
    if masked:
        mixed = mixed * marks_ref[:, :1]
    out_ref[...] = carried_ref[...] + mixed


def forward_kernel(layer, last, got, *refs):
    got_refs, refs = refs[:got], refs[got:]
    base_ref, mirror_ref, recv_ref, up_ref, up_bias_ref, down_ref, down_bias_ref, gain_ref, shift_ref, *refs = refs
    if last:
        upstream_ref, *refs = refs
    else:
        marks_ref, feature_ref, send_ref, *refs = refs
    normed_ref, unit_ref, inverse_ref, slope_ref, *refs = refs
    *refs, low_ref, total_ref = refs
    chunk = pl.program_id(0)

    @pl.when(chunk == 0)
    def _():
        mixed = base_ref[...] + stage_two(got_refs, mirror_ref, recv_ref)
        unit, inverse = normalize(mixed)
        unit_ref[...] = unit
        inverse_ref[...] = inverse
        normed = unit * gain_ref[layer, 0:1, :] + shift_ref[layer, 0:1, :]
        normed_ref[...] = normed
        low_ref[...] = normed.astype(LOW)
        total_ref[...] = normed + down_bias_ref[layer : layer + 1, :]

    preact = wide(low_ref[...], up_ref[0]) + up_bias_ref[layer : layer + 1, :]
    value, slope = gelu_parts(preact)
    slope_ref[...] = slope
    total_ref[...] += wide(value.astype(LOW), down_ref[0])

    @pl.when(chunk == pl.num_programs(0) - 1)
    def _():
        unit, inverse = normalize(total_ref[...])
        gain = gain_ref[layer, 1:2, :]
        carried = unit * gain + shift_ref[layer, 1:2, :]
        if last:
            carried_ref, delta_ref, minor_ref = refs
            carried_ref[...] = carried
            delta_out(upstream_ref[...], unit, inverse, gain, delta_ref, minor_ref)
        else:
            unit_two_ref, inverse_two_ref, carried_ref, spectrum_ref, *sent_refs = refs
            unit_two_ref[...] = unit
            inverse_two_ref[...] = inverse
            carried_ref[...] = carried
            stage_one(carried * marks_ref[:, :1], feature_ref, send_ref, spectrum_ref, sent_refs)


def delta_out(upstream, unit, inverse, gain, delta_ref, minor_ref):
    delta = norm_back(upstream, unit, inverse, gain)
    delta_ref[...] = delta
    rows = [upstream * unit, upstream, delta.astype(LOW).astype(HIGH)]
    for at, value in enumerate(rows):
        minor_ref[at : at + 1, :] = jnp.sum(value, 0, keepdims=True)
    minor_ref[len(rows) :, :] = jnp.zeros_like(minor_ref[len(rows) :, :])


def delta_kernel(layer, got, *refs):
    got_refs, refs = refs[:got], refs[got:]
    base_ref, marks_ref, mirror_ref, recv_ref, unit_ref, inverse_ref, gain_ref, delta_ref, minor_ref = refs
    upstream = base_ref[...] + marks_ref[:, :1] * stage_two(got_refs, mirror_ref, recv_ref)
    delta_out(upstream, unit_ref[...], inverse_ref[...], gain_ref[layer, 1:2, :], delta_ref, minor_ref)


def backward_kernel(layer, *refs):
    delta_ref, slope_ref, up_ref, down_ref, unit_ref, inverse_ref, gain_ref, feature_ref, send_ref, *refs = refs
    mixed_ref, minor_ref, spectrum_ref, *sent_refs, low_ref, total_ref = refs
    chunk = pl.program_id(0)

    @pl.when(chunk == 0)
    def _():
        low_ref[...] = delta_ref[...].astype(LOW)
        total_ref[...] = delta_ref[...]
        minor_ref[...] = jnp.zeros_like(minor_ref)

    slope = (wide(low_ref[...], down_ref[0], (1, 1)) * slope_ref[...]).astype(LOW)
    minor_ref[pl.ds(2 + chunk, 1), :] = jnp.sum(slope.astype(HIGH), 0, keepdims=True)
    total_ref[...] += wide(slope, up_ref[0], (1, 1))

    @pl.when(chunk == pl.num_programs(0) - 1)
    def _():
        upstream = total_ref[...]
        unit = unit_ref[...]
        minor_ref[0:1, :] = jnp.sum(upstream * unit, 0, keepdims=True)
        minor_ref[1:2, :] = jnp.sum(upstream, 0, keepdims=True)
        mixed = norm_back(upstream, unit, inverse_ref[...], gain_ref[layer, 0:1, :])
        mixed_ref[...] = mixed
        stage_one(mixed, feature_ref, send_ref, spectrum_ref, sent_refs)


def leave_kernel(types, got, *refs):
    got_refs, refs = refs[:got], refs[got:]
    base_ref, marks_ref, mirror_ref, recv_ref, minor_ref, *outs = refs
    upstream = base_ref[...] + marks_ref[:, :1] * stage_two(got_refs, mirror_ref, recv_ref)
    kind = marks_ref[:, 1:2]
    for t in range(types):
        minor_ref[t : t + 1, :] = jnp.sum(jnp.where(kind == float(t), upstream, 0.0), 0, keepdims=True)
    minor_ref[types:, :] = jnp.zeros_like(minor_ref[types:, :])
    rows = outs[0].shape[0]
    for k, ref in enumerate(outs):
        ref[...] = upstream[k * rows : (k + 1) * rows]


def grads_kernel(normed_ref, delta_ref, up_ref, bias_ref, down_ref, out_ref):
    planes, rows = out_ref.shape[0], out_ref.shape[1] // 2
    normed = normed_ref[...].astype(LOW)
    delta = delta_ref[...].astype(LOW)
    pre = wide(normed, up_ref[...]) + bias_ref[...]
    value, slope = gelu_parts(pre)
    back = (wide(delta, down_ref[...], (1, 1)) * slope).astype(LOW)
    up = wide(back, normed, (0, 0))
    down = wide(value.astype(LOW), delta, (0, 0))
    parts = [(z, h, a[z * rows : (z + 1) * rows]) for z in range(planes) for h, a in enumerate((up, down))]

    @pl.when(pl.program_id(0) == 0)
    def _():
        for z, h, value in parts:
            out_ref[z, h * rows : (h + 1) * rows] = value

    @pl.when(pl.program_id(0) > 0)
    def _():
        for z, h, value in parts:
            out_ref[z, h * rows : (h + 1) * rows] += value


def finish_kernel(layer, at_ref, *refs):
    *pieces, up_ref, down_ref, turned = refs[: len(refs)]
    rows = pieces[0].shape[0] // 2
    for k, ref in enumerate(pieces):
        at = pl.multiple_of((at_ref[0] ^ k) * rows, 8)
        turned[pl.ds(at, rows), :] = ref[:rows, :]
        down_ref[0, pl.ds(at, rows), :] = ref[rows:, :]
    up_ref[0] = turned[...].T


def swap(values, axes, k):
    count = lax.axis_size(axes)
    return lax.ppermute(values, axes, [(i, i ^ k) for i in range(count)])


def exchange(blocks, axes, first=0):
    return [b if k == 0 else swap(b, axes, k) for k, b in enumerate(blocks, first)]


def all_sum(values):
    for axes in (("core",), ("dy", "x"), PLANES, ("do",)):
        moved = [swap(values, axes, k) for k in range(1, lax.axis_size(axes))]
        values = sum(moved, values)
    return values


def plane_gather(values):
    if lax.axis_size("x") > 2:
        return [lax.all_gather(values, PLANE, tiled=True)]
    rows = values.shape[0] // 2
    along_x, along_y = swap(values, "x", 1), swap(values, "dy", 1)
    head, tail = swap(along_x[:rows], "dy", 1), swap(along_y[rows:], "x", 1)
    found = [along_x, along_y, head, tail]
    return [values, swap(values, "core", 1)] + found + [swap(f, "core", 1) for f in found]


def local(inputs, segments, padding, type_table, ln_gain, ln_bias, up_weight, up_bias, down_weight, down_bias, out_grad):
    rows, part, width = inputs.shape
    layers, _, hidden_width = up_weight.shape
    types = type_table.shape[0]
    seq, count = lax.axis_size(SEQ), lax.axis_size(ROW)
    step = 2 * count
    units = part // step
    tokens = rows * part
    block = tokens // seq
    half = width // 2
    place = lax.axis_index(SEQ).reshape(1)

    feature = jnp.asarray(feature_table(width))
    mirror = jnp.asarray(mirror_table(half))
    send_t, recv_t, block_t = (
        lax.dynamic_index_in_dim(jnp.asarray(t), place[0], 0, False) for t in position_tables(count, part, seq)
    )
    chunk = send_t.shape[2] // (count - 1)
    sent_outs = [array(chunk, width)] * (count - 1)
    whole = array(tokens, width)
    thin = array(tokens, 1)
    minor_out = array(8, width)
    steps = hidden_width // width

    def spread(values, *marks):
        span = width + (MARK if marks else 0)
        blocks = call(
            lambda at_ref, *refs: spread_body(count, bool(marks), at_ref, refs),
            "spread",
            (place, values) + marks,
            [array(block, span)] * seq,
            scratch_shapes=[pltpu.VMEM((rows, units, step, span), HIGH)],
        )
        return exchange(blocks, SEQ)

    def collect(blocks):
        got = exchange(blocks, SEQ)
        out = call(
            functools.partial(collect_kernel, count),
            "collect",
            [place] + got,
            [array(rows, units, step, width)],
        )[0]
        return out.reshape(rows, part, width)

    def own(spectrum, carried, marks=None):
        inputs = [spectrum, carried, mirror, block_t] + ([] if marks is None else [marks])
        return call(functools.partial(own_kernel, marks is not None), "own_part", inputs, [whole])[0]

    def weights(layer):
        return [
            pl.BlockSpec((1, width, width), lambda c: (layer, 0, c)),
            pl.BlockSpec((2, width), lambda c: (0, c)),
            pl.BlockSpec((1, width, width), lambda c: (layer, c, 0)),
        ]

    column = pl.BlockSpec((tokens, width), lambda c: (0, c))
    slope_out = array(tokens, hidden_width)
    scratch = [pltpu.VMEM((tokens, width), LOW), pltpu.VMEM((tokens, width), HIGH)]
    flops = 4 * tokens * width * hidden_width

    def forward(layer, got, base, *more):
        last = layer == layers - 1
        inputs = got + [base, mirror, recv_t, up_weight, up_bias, down_weight, down_bias, ln_gain, ln_bias] + list(more)
        outs = [whole, whole, thin, slope_out]
        outs += [whole, whole, minor_out] if last else [whole, thin, whole, whole] + sent_outs
        at = len(got) + 3
        in_specs = [VMEM] * at + weights(layer) + [VMEM] * (len(inputs) - at - 3)
        out_specs = [VMEM] * 3 + [column] + [VMEM] * (len(outs) - 4)
        return call(
            functools.partial(forward_kernel, layer, last, len(got)),
            "layer_forward",
            inputs,
            outs,
            flops,
            grid=(steps,),
            in_specs=in_specs,
            out_specs=out_specs,
            scratch_shapes=scratch,
        )

    def backward(layer, delta, slope, unit, inverse):
        inputs = [delta, slope, up_weight, down_weight, unit, inverse, ln_gain, feature, send_t]
        outs = [whole, minor_out, whole] + sent_outs
        up_spec, _, down_spec = weights(layer)
        return call(
            functools.partial(backward_kernel, layer),
            "layer_backward",
            inputs,
            outs,
            flops,
            grid=(steps,),
            in_specs=[VMEM, column, up_spec, down_spec] + [VMEM] * 5,
            out_specs=[VMEM] * len(outs),
            scratch_shapes=scratch,
        )

    def delta(layer, got, base, marks, unit, inverse):
        inputs = got + [base, marks, mirror, recv_t, unit, inverse, ln_gain]
        return call(functools.partial(delta_kernel, layer, len(got)), "delta", inputs, [whole, minor_out])

    shares, planes, columns = lax.axis_size(SHARES), lax.axis_size(PLANES), lax.axis_size("x")
    unit_block = hidden_width // seq
    piece = unit_block // shares
    share = lax.axis_index(SHARES)
    starts = [(z * columns + lax.axis_index("x")) * unit_block + share * piece for z in range(planes)]

    def cut(values, axis):
        return jnp.concatenate([lax.dynamic_slice_in_dim(values, s, piece, axis) for s in starts], axis)

    cuts = [(cut(up_weight[l], 1), cut(up_bias[l : l + 1], 1), cut(down_weight[l], 0)) for l in range(layers)]

    def weight_grads(layer, normed, delta):
        normed, delta = jnp.concatenate(normed, 0), jnp.concatenate(delta, 0)
        total = normed.shape[0]
        size = min(total, 512)
        whole_of = lambda a: pl.BlockSpec(a.shape, lambda i: (0,) * len(a.shape))
        out = array(planes, 2 * piece, width)
        both = call(
            grads_kernel,
            "weight_grads",
            [normed, delta, *cuts[layer]],
            [out],
            8 * total * width * piece * planes,
            grid=(total // size,),
            in_specs=[pl.BlockSpec((size, width), lambda i: (i, 0))] * 2 + [whole_of(a) for a in cuts[layer]],
            out_specs=[whole_of(out)],
        )[0]
        summed = lax.psum_scatter(both.reshape(-1, width), PLANES, scatter_dimension=0, tiled=True)
        if lax.axis_size("do") > 1:
            summed = lax.psum(summed, "do")
        along = swap(summed, "dy", 1)
        return [summed, swap(summed, "core", 1), along, swap(along, "core", 1)]

    column_of = lambda a: a.reshape(rows, part, 1)
    held = spread(inputs, column_of(segments), column_of(padding), type_table)
    carried, marks, spectrum, *sent = call(
        functools.partial(enter_kernel, seq),
        "enter",
        held + [feature, send_t],
        [whole, array(tokens, MARK), whole] + sent_outs,
    )
    upstream = jnp.concatenate(spread(out_grad), 0)
    saved = []
    for layer in range(layers - 1):
        got = exchange(sent, ROW, 1)
        base = own(spectrum, carried)
        normed, unit, inverse, slope, unit_two, inverse_two, carried, spectrum, *sent = forward(
            layer, got, base, marks, feature, send_t
        )
        saved.append((plane_gather(normed), unit, inverse, slope, unit_two, inverse_two))
    got = exchange(sent, ROW, 1)
    base = own(spectrum, carried)
    normed, unit, inverse, slope, outputs, delta_two, minor_two = forward(layers - 1, got, base, upstream)
    saved.append((plane_gather(normed), unit, inverse, slope))
    outputs = collect([outputs[k * block : (k + 1) * block] for k in range(seq)])

    pieces = [None] * layers
    minors = []
    for layer in reversed(range(layers)):
        all_normed, unit, inverse, slope, *second = saved[layer]
        if second:
            delta_two, minor_two = delta(layer, got, base, marks, *second)
        pieces[layer] = weight_grads(layer, all_normed, plane_gather(delta_two))
        mixed, minor_one, spectrum, *sent = backward(layer, delta_two, slope, unit, inverse)
        minors += [minor_two, minor_one]
        got = exchange(sent, ROW, 1)
        base = own(spectrum, mixed, marks)
    minor_table, *blocks = call(
        functools.partial(leave_kernel, types, len(got)),
        "leave",
        got + [base, marks, mirror, recv_t],
        [minor_out] + [array(block, width)] * seq,
    )
    input_grad = collect(blocks)
    minor = all_sum(jnp.concatenate(minors + [minor_table], 0))
    ends = [minor[16 * (layers - 1 - l) :][:16] for l in range(layers)]
    table_grad = minor[16 * layers :][:types]
    gain_grad = jnp.stack([jnp.stack([e[8], e[0]]) for e in ends])
    shift_grad = jnp.stack([jnp.stack([e[9], e[1]]) for e in ends])
    down_vec = jnp.stack([e[2] for e in ends])
    up_vec = jnp.stack([e[10 : 10 + steps].reshape(-1) for e in ends])
    up_vec = lax.dynamic_slice_in_dim(up_vec, place[0] * unit_block, unit_block, 1)

    outs = [array(layers, width, unit_block), array(layers, unit_block, width)]
    grads = []
    for layer in reversed(range(layers)):
        at = len(pieces[layer]) + 1
        grads = call(
            functools.partial(finish_kernel if not grads else finish_more, layer),
            "finish",
            [share.reshape(1)] + pieces[layer] + grads,
            outs,
            in_specs=[SMEM] + [VMEM] * (at - 1) + [pl.BlockSpec(memory_space=pl.ANY)] * len(grads),
            out_specs=[
                pl.BlockSpec((1,) + o.shape[1:], functools.partial(lambda l, i: (l, 0, 0), layer)) for o in outs
            ],
            grid=(1,),
            input_output_aliases={at: 0, at + 1: 1} if grads else {},
            scratch_shapes=[pltpu.VMEM((unit_block, width), HIGH)],
        )
    up_grad, down_grad = grads
    return outputs, input_grad, table_grad, gain_grad, shift_grad, up_grad, up_vec, down_grad, down_vec


def finish_more(layer, at_ref, *refs):
    pieces = refs[:-5]
    finish_kernel(layer, at_ref, *pieces, *refs[-3:])


def solution(mesh):
    dp, seq = mesh.shape["dp"], mesh.shape["seq"]
    shape = (dp // 4, 2, 2, 2, 2, seq // 4)
    finer = Mesh(mesh.devices.reshape(shape), ALL)
    in_specs = (P(DP, SEQ, None), P(DP, SEQ), P(DP, SEQ)) + (P(),) * 7 + (P(DP, SEQ, None),)
    out_specs = (
        P(DP, SEQ, None),
        P(DP, SEQ, None),
        P(),
        P(),
        P(),
        P(None, None, SEQ),
        P(None, SEQ),
        P(None, SEQ, None),
        P(),
    )
    return jax.shard_map(local, mesh=finer, in_specs=in_specs, out_specs=out_specs, check_vma=False)
```

time: 633 us -> 460 us (0.73)
  the two profiles are of different devices: /device:TPU:0 before, /device:TPU:9 now
where the time goes in v2:
time: 460 us; the launch traced here: 453 us
  waiting for transfers between devices  173 us (38%)
  starting transfers between devices  110 us (24%)
  local copies, waits for them, and re-layouts  81 us (18%)
  Pallas kernels  70.5 us (15%)
  between operations  15.7 us (3%)
    ppermute x89, waiting for transfers between devices, swap(): return lax.ppermute(values, axes, [(i, i ^ k) for i in range(count)])  173 us
    ppermute x89, starting transfers between devices, swap(): return lax.ppermute(values, axes, [(i, i ^ k) for i in range(count)])  110 us
    pallas_call x19, Pallas kernels, call(): pl.pallas_call(kernel, out_shape=list(outs), compiler_params=pltpu.Compil...  70.5 us
    unnamed x211, local copies, waits for them, and re-layouts  50.6 us
  transfers between devices with their start and end apart: 91, of which 41 were waited for; matrix products, arithmetic and copies ran while one was open for 9% of the time, Pallas kernels for 11%

profile of v2, /device:TPU:9, one launch (start us, length us, event | category | flops | bytes accessed | tf_op | source)
XLA Modules:
  0.0 453.2 jit_solution(13318431818814732149)
XLA Ops:
  15.3 2.3 collective-permute-start.3
  30.4 8.4 %fusion.2 = (bf16[1,768,3072]{2,1,0:T(8,128)(2,1)}, bf16[1,768,3072]{2,1,0:T(8,128)(2,1)}) fusion(bf16[2,768,3072]{2,1,0:T(8,128)(2,1)} %refs_2_.7), kind=kLoop, calls=%fused_computation.101 | loop fusion | bytes 18874368 | tf_op jit(solution)/shard_map/slice | solution.py:575
  38.8 8.0 %fusion.1 = (bf16[1,3072,768]{2,1,0:T(8,128)(2,1)}, bf16[1,3072,768]{2,1,0:T(8,128)(2,1)}) fusion(bf16[2,3072,768]{2,1,0:T(8,128)(2,1)} %refs_3_.5), kind=kLoop, calls=%fused_computation.100 | loop fusion | bytes 18874368 | tf_op jit(solution)/shard_map/slice | solution.py:575
  48.0 2.6 collective-permute-done.14
  50.8 4.4 collective-permute-done.15
  55.3 4.6 %collective-permute-done.16 = f32[32,768]{1,0:T(8,128)S(1)} collective-permute-done((f32[32,768]{1,0:T(8,128)}, f32[32,768]{1,0:T(8,128)S(1)}, u32[]{:S(2)}, u32[]{:S(2)}) %collective-permute-start.16) | collective-permute-done | bytes 98336 | tf_op jit(solution)/shard_map/ppermute | solution.py:441
  60.7 5.7 %collective-permute-done.17 = f32[32,768]{1,0:T(8,128)S(1)} collective-permute-done((f32[32,768]{1,0:T(8,128)}, f32[32,768]{1,0:T(8,128)S(1)}, u32[]{:S(2)}, u32[]{:S(2)}) %collective-permute-start.17) | collective-permute-done | bytes 98336 | tf_op jit(solution)/shard_map/ppermute | solution.py:441
  72.6 5.1 %collective-permute-done.4.refs_5_ = f32[32,896]{1,0:T(8,128)S(1)} collective-permute-done((f32[32,896]{1,0:T(8,128)}, f32[32,896]{1,0:T(8,128)S(1)}, u32[]{:S(2)}, u32[]{:S(2)}) %collective-permute-start.4) | collective-permute-done | bytes 114720 | tf_op jit(solution)/shard_map/ppermute | solution.py:441
  78.8 3.6 collective-permute-done.6.refs_7_
  86.0 2.9 enter.1
  89.0 2.6 collective-permute-start.9
  95.2 10.4 %layer_forward.2 = (f32[256,768]{1,0:T(8,128)}, f32[256,768]{1,0:T(8,128)S(1)}, f32[256,1]{1,0:T(8,128)S(1)}, f32[256,3072]{1,0:T(8,128)S(1)}, f32[256,768]{1,0:...) custom-call(f32[32,768]{1,0:T(8,128)S(1)} %collective-permute-done.7, ...), custom_call_target="tpu_custom_call" | custom-call | flops 2415919104 | bytes 30760960 | tf_op jit(solution)/shard_map/layer_forward/pallas_call | solution.py:232
  112.8 8.9 %layer_forward.3 = (f32[256,768]{1,0:T(8,128)}, f32[256,768]{1,0:T(8,128)S(1)}, f32[256,1]{1,0:T(8,128)S(1)}, f32[256,3072]{1,0:T(8,128)S(1)}, f32[256,768]{1,0:...) custom-call(f32[32,768]{1,0:T(8,128)S(1)} %collective-permute-done.10.refs_0_, ...), custom_call_target="tpu_custom_call" | custom-call | flops 2415919104 | bytes 27802624 | tf_op jit(solution)/shard_map/layer_forward/pallas_call | solution.py:232
  127.7 15.3 %collective-permute-start.68 = (f32[256,768]{1,0:T(8,128)}, f32[256,768]{1,0:T(8,128)S(1)}, u32[]{:S(2)}, u32[]{:S(2)}) collective-permute-start(f32[256,768]{1,0:T(8,128)} %get-tuple-element.138), channel_id=1, source_target_pairs={{0,8},{8,0},{1,9},{9,1},{2,10},{10,2},{3,11},{11,3},{4,12},{12,4},... | collective-permute-start | bytes 2359304 | tf_op jit(solution)/shard_map/ppermute | solution.py:441
  145.2 3.4 dynamic-slice_bitcast_fusion.5
  156.0 12.0 %collective-permute-done.70 = f32[256,768]{1,0:T(8,128)S(1)} collective-permute-done((f32[256,768]{1,0:T(8,128)}, f32[256,768]{1,0:T(8,128)S(1)}, u32[]{:S(2)}, u32[]{:S(2)}) %collective-permute-start.70) | collective-permute-done | bytes 786464 | tf_op jit(solution)/shard_map/ppermute | solution.py:441
  172.0 12.8 %collective-permute-done.79 = f32[256,768]{1,0:T(8,128)S(1)} collective-permute-done((f32[256,768]{1,0:T(8,128)S(1)}, f32[256,768]{1,0:T(8,128)S(1)}, u32[]{:S(2)}, u32[]{:S(2)}) %collective-permute-start.79) | collective-permute-done | bytes 786464 | tf_op jit(solution)/shard_map/ppermute | solution.py:441
  187.6 5.6 %collective-permute-done.71 = f32[128,768]{1,0:T(8,128)S(1)} collective-permute-done((f32[128,768]{1,0:T(8,128)S(1)}, f32[128,768]{1,0:T(8,128)S(1)}, u32[]{:S(2)}, u32[]{:S(2)}) %collective-permute-start.71) | collective-permute-done | bytes 393248 | tf_op jit(solution)/shard_map/ppermute | solution.py:441
  194.8 6.9 %collective-permute-done.80 = f32[128,768]{1,0:T(8,128)S(1)} collective-permute-done((f32[128,768]{1,0:T(8,128)S(1)}, f32[128,768]{1,0:T(8,128)S(1)}, u32[]{:S(2)}, u32[]{:S(2)}) %collective-permute-start.80) | collective-permute-done | bytes 393248 | tf_op jit(solution)/shard_map/ppermute | solution.py:441
  206.7 8.1 %weight_grads.3 = f32[4,192,768]{2,1,0:T(8,128)S(1)} custom-call(f32[2048,768]{1,0:T(8,128)S(1)} %constant_dynamic-update-slice_fusion.33.normed_ref, f32[2048,768]{1,0:T(8,128)S(1)} %constant_dynamic-update-slice_fusion.43.delta_ref, bf16[768,384]{1,0:T(8,128)(2,1)S(1)} %pad_maximum_fusion.2.up_ref, f32[1,384]{1,0:T(1,128)S(1)} %pad_maximum_fusion.8.bias_ref, ...), custom_call_target="tpu_custom_call" | custom-call | flops 4831838208 | bytes 16123392 | tf_op jit(solution)/shard_map/weight_grads/pallas_call | solution.py:232
  219.9 4.1 copy-done
  230.1 8.2 %layer_backward.2 = (f32[256,768]{1,0:T(8,128)S(1)}, f32[8,768]{1,0:T(8,128)S(1)}, f32[256,768]{1,0:T(8,128)S(1)}, f32[32,768]{1,0:T(8,128)S(1)}, f32[32,768]{1,0:T(8,128)S(1)}, /*index=5*/f32[32,768]{1,0:T(8,128)S(1)}) custom-call(f32[256,768]{1,0:T(8,128)S(1)} %copy-done.22, f32[256,3072]{1,0:T(8,128)S(1)} %copy-done.26, ...), custom_call_target="tpu_custom_call" | custom-call | flops 2415919104 | bytes 28054528 | tf_op jit(solution)/shard_map/layer_backward/pallas_call | solution.py:232
  240.0 2.7 collective-permute-done.27.refs_0_
  245.9 7.3 %collective-permute-done.29.refs_2_ = f32[32,768]{1,0:T(8,128)S(1)} collective-permute-done((f32[32,768]{1,0:T(8,128)S(1)}, f32[32,768]{1,0:T(8,128)S(1)}, u32[]{:S(2)}, u32[]{:S(2)}) %collective-permute-start.29) | collective-permute-done | bytes 98336 | tf_op jit(solution)/shard_map/ppermute | solution.py:441
  260.7 13.5 %collective-permute-done.57 = f32[256,768]{1,0:T(8,128)S(1)} collective-permute-done((f32[256,768]{1,0:T(8,128)S(1)}, f32[256,768]{1,0:T(8,128)S(1)}, u32[]{:S(2)}, u32[]{:S(2)}) %collective-permute-start.57) | collective-permute-done | bytes 786464 | tf_op jit(solution)/shard_map/ppermute | solution.py:441
  276.4 6.8 %collective-permute-done.50 = f32[128,768]{1,0:T(8,128)S(1)} collective-permute-done((f32[128,768]{1,0:T(8,128)S(1)}, f32[128,768]{1,0:T(8,128)S(1)}, u32[]{:S(2)}, u32[]{:S(2)}) %collective-permute-start.50) | collective-permute-done | bytes 393248 | tf_op jit(solution)/shard_map/ppermute | solution.py:441
  286.3 5.4 %collective-permute-done.59 = f32[128,768]{1,0:T(8,128)S(1)} collective-permute-done((f32[128,768]{1,0:T(8,128)S(1)}, f32[128,768]{1,0:T(8,128)S(1)}, u32[]{:S(2)}, u32[]{:S(2)}) %collective-permute-start.59) | collective-permute-done | bytes 393248 | tf_op jit(solution)/shard_map/ppermute | solution.py:441
  297.8 7.9 %weight_grads.2 = f32[4,192,768]{2,1,0:T(8,128)S(1)} custom-call(f32[2048,768]{1,0:T(8,128)S(1)} %constant_dynamic-update-slice_fusion.13.normed_ref, f32[2048,768]{1,0:T(8,128)S(1)} %constant_dynamic-update-slice_fusion.23.delta_ref, bf16[768,384]{1,0:T(8,128)(2,1)S(1)} %pad_maximum_fusion.up_ref, f32[1,384]{1,0:T(1,128)S(1)} %pad_maximum_fusion.7.bias_ref, ...), custom_call_target="tpu_custom_call" | custom-call | flops 4831838208 | bytes 16123392 | tf_op jit(solution)/shard_map/weight_grads/pallas_call | solution.py:232
  308.7 3.7 copy-done.1
  318.4 8.1 %layer_backward.3 = (f32[256,768]{1,0:T(8,128)S(1)}, f32[8,768]{1,0:T(8,128)S(1)}, f32[256,768]{1,0:T(8,128)S(1)}, f32[32,768]{1,0:T(8,128)S(1)}, f32[32,768]{1,0:T(8,128)S(1)}, /*index=5*/f32[32,768]{1,0:T(8,128)S(1)}) custom-call(f32[256,768]{1,0:T(8,128)S(1)} %copy-done.19, f32[256,3072]{1,0:T(8,128)S(1)} %copy-done.24, ...), custom_call_target="tpu_custom_call" | custom-call | flops 2415919104 | bytes 28054528 | tf_op jit(solution)/shard_map/layer_backward/pallas_call | solution.py:232
  327.3 3.1 collective-permute-start.31
  332.6 4.0 collective-permute-done.31.refs_1_
  336.6 6.9 %collective-permute-done.32.refs_2_ = f32[32,768]{1,0:T(8,128)S(1)} collective-permute-done((f32[32,768]{1,0:T(8,128)S(1)}, f32[32,768]{1,0:T(8,128)S(1)}, u32[]{:S(2)}, u32[]{:S(2)}) %collective-permute-start.32) | collective-permute-done | bytes 98336 | tf_op jit(solution)/shard_map/ppermute | solution.py:441
  347.0 4.1 collective-permute-start.21
  351.9 2.5 collective-permute-start.24
  358.3 2.8 collective-permute-done.22.refs_3_
  362.9 2.7 collective-permute-start.25
  369.2 5.0 %collective-permute-done.26.refs_7_ = f32[32,768]{1,0:T(8,128)S(1)} collective-permute-done((f32[32,768]{1,0:T(8,128)S(1)}, f32[32,768]{1,0:T(8,128)S(1)}, u32[]{:S(2)}, u32[]{:S(2)}) %collective-permute-start.26) | collective-permute-done | bytes 98336 | tf_op jit(solution)/shard_map/ppermute | solution.py:441
  376.0 2.3 collective-permute-start.36
  379.7 2.3 collective-permute-start.45
  383.9 5.9 %collective-permute-done.37.refs_5_ = f32[32,768]{1,0:T(8,128)S(1)} collective-permute-done((f32[32,768]{1,0:T(8,128)S(1)}, f32[32,768]{1,0:T(8,128)S(1)}, u32[]{:S(2)}, u32[]{:S(2)}) %collective-permute-start.37) | collective-permute-done | bytes 98336 | tf_op jit(solution)/shard_map/ppermute | solution.py:441
  389.8 2.6 collective-permute-start.39
  393.5 8.2 %collective-permute-done.38.refs_6_ = f32[32,768]{1,0:T(8,128)S(1)} collective-permute-done((f32[32,768]{1,0:T(8,128)S(1)}, f32[32,768]{1,0:T(8,128)S(1)}, u32[]{:S(2)}, u32[]{:S(2)}) %collective-permute-start.38) | collective-permute-done | bytes 98336 | tf_op jit(solution)/shard_map/ppermute | solution.py:441
  401.7 6.1 %collective-permute-done.39.refs_7_ = f32[32,768]{1,0:T(8,128)S(1)} collective-permute-done((f32[32,768]{1,0:T(8,128)S(1)}, f32[32,768]{1,0:T(8,128)S(1)}, u32[]{:S(2)}, u32[]{:S(2)}) %collective-permute-start.39) | collective-permute-done | bytes 98336 | tf_op jit(solution)/shard_map/ppermute | solution.py:441
  413.3 9.4 %collective-permute-done.87.refs_2_ = f32[192,768]{1,0:T(8,128)S(1)} collective-permute-done((f32[192,768]{1,0:T(8,128)}, f32[192,768]{1,0:T(8,128)S(1)}, u32[]{:S(2)}, u32[]{:S(2)}) %collective-permute-start.87) | collective-permute-done | bytes 589856 | tf_op jit(solution)/shard_map/ppermute | solution.py:441
  422.7 4.2 collective-permute-start.88
  426.8 8.5 %collective-permute-done.66.refs_2_ = f32[192,768]{1,0:T(8,128)S(1)} collective-permute-done((f32[192,768]{1,0:T(8,128)}, f32[192,768]{1,0:T(8,128)S(1)}, u32[]{:S(2)}, u32[]{:S(2)}) %collective-permute-start.66) | collective-permute-done | bytes 589856 | tf_op jit(solution)/shard_map/ppermute | solution.py:441
  435.3 2.3 collective-permute-start.67
  (409 shorter events, 153.4 us)
Async XLA Ops:
  7.2 401.8 %reduce-scatter.5.cloned.1.call-start = ((), (), s32[]{:S(2)}) async-start(), calls=%async_computation.3 | async-start | bytes 2949120 | tf_op jit(solution)/shard_map/reduce_scatter | solution.py:593
  12.7 56.0 %collective-permute-start = (f32[32,896]{1,0:T(8,128)}, f32[32,896]{1,0:T(8,128)}, u32[]{:S(2)}, u32[]{:S(2)}) collective-permute-start(f32[32,896]{1,0:T(8,128)} %get-tuple-element.77), channel_id=1, source_target_pairs={{0,1},{1,0},{2,3},{3,2},{4,5},{5,4},{6,7},{7,6},{8,9},{9,8},{10,11... | collective-permute-start | bytes 344072 | tf_op jit(solution)/shard_map/ppermute | solution.py:441
  13.9 54.8 %collective-permute-start.1 = (f32[32,896]{1,0:T(8,128)}, f32[32,896]{1,0:T(8,128)}, u32[]{:S(2)}, u32[]{:S(2)}) collective-permute-start(f32[32,896]{1,0:T(8,128)} %get-tuple-element.78), channel_id=1, source_target_pairs={{0,2},{1,3},{2,0},{3,1},{4,6},{5,7},{6,4},{7,5},{8,10},{9,11},{10,... | collective-permute-start | bytes 344072 | tf_op jit(solution)/shard_map/ppermute | solution.py:441
  14.0 56.1 %collective-permute-start.2 = (f32[32,896]{1,0:T(8,128)}, f32[32,896]{1,0:T(8,128)}, u32[]{:S(2)}, u32[]{:S(2)}) collective-permute-start(f32[32,896]{1,0:T(8,128)} %get-tuple-element.79), channel_id=1, source_target_pairs={{0,3},{1,2},{2,1},{3,0},{4,7},{5,6},{6,5},{7,4},{8,11},{9,10},{10,... | collective-permute-start | bytes 344072 | tf_op jit(solution)/shard_map/ppermute | solution.py:441
  15.3 56.2 %collective-permute-start.3 = (f32[32,896]{1,0:T(8,128)}, f32[32,896]{1,0:T(8,128)}, u32[]{:S(2)}, u32[]{:S(2)}) collective-permute-start(f32[32,896]{1,0:T(8,128)} %get-tuple-element.80), channel_id=1, source_target_pairs={{0,4},{1,5},{2,6},{3,7},{4,0},{5,1},{6,2},{7,3},{8,12},{9,13},{10,... | collective-permute-start | bytes 344072 | tf_op jit(solution)/shard_map/ppermute | solution.py:441
  23.5 23.4 %collective-permute-start.13 = (f32[32,768]{1,0:T(8,128)}, f32[32,768]{1,0:T(8,128)}, u32[]{:S(2)}, u32[]{:S(2)}) collective-permute-start(f32[32,768]{1,0:T(8,128)} %get-tuple-element.96), channel_id=1, source_target_pairs={{0,1},{1,0},{2,3},{3,2},{4,5},{5,4},{6,7},{7,6},{8,9},{9,8},{10,11... | collective-permute-start | bytes 294920 | tf_op jit(solution)/shard_map/ppermute | solution.py:441
  68.7 13.8 %collective-permute-start.6 = (f32[32,896]{1,0:T(8,128)}, f32[32,896]{1,0:T(8,128)S(1)}, u32[]{:S(2)}, u32[]{:S(2)}) collective-permute-start(f32[32,896]{1,0:T(8,128)} %copy-done.58), channel_id=1, source_target_pairs={{0,7},{1,6},{2,5},{3,4},{4,3},{5,2},{6,1},{7,0},{8,15},{9,14},{10,... | collective-permute-start | bytes 344072 | tf_op jit(solution)/shard_map/ppermute | solution.py:441
  70.1 21.4 %collective-permute-start.18 = (f32[32,768]{1,0:T(8,128)}, f32[32,768]{1,0:T(8,128)S(1)}, u32[]{:S(2)}, u32[]{:S(2)}) collective-permute-start(f32[32,768]{1,0:T(8,128)} %copy-done.62), channel_id=1, source_target_pairs={{0,6},{1,7},{2,4},{3,5},{4,2},{5,3},{6,0},{7,1},{8,14},{9,15},{10,... | collective-permute-start | bytes 294920 | tf_op jit(solution)/shard_map/ppermute | solution.py:441
  71.5 37.7 %collective-permute-start.19 = (f32[32,768]{1,0:T(8,128)}, f32[32,768]{1,0:T(8,128)S(1)}, u32[]{:S(2)}, u32[]{:S(2)}) collective-permute-start(f32[32,768]{1,0:T(8,128)} %copy-done.61), channel_id=1, source_target_pairs={{0,7},{1,6},{2,5},{3,4},{4,3},{5,2},{6,1},{7,0},{8,15},{9,14},{10,... | collective-permute-start | bytes 294920 | tf_op jit(solution)/shard_map/ppermute | solution.py:441
  127.4 25.5 %collective-permute-start.69 = (f32[256,768]{1,0:T(8,128)}, f32[256,768]{1,0:T(8,128)S(1)}, u32[]{:S(2)}, u32[]{:S(2)}) collective-permute-start(f32[256,768]{1,0:T(8,128)} %get-tuple-element.138), channel_id=1, source_target_pairs={{0,1},{1,0},{2,3},{3,2},{4,5},{5,4},{6,7},{7,6},{8,9},{9,8},{10,11... | collective-permute-start | bytes 2359304 | tf_op jit(solution)/shard_map/ppermute | solution.py:441
  127.7 26.8 %collective-permute-start.68 = (f32[256,768]{1,0:T(8,128)}, f32[256,768]{1,0:T(8,128)S(1)}, u32[]{:S(2)}, u32[]{:S(2)}) collective-permute-start(f32[256,768]{1,0:T(8,128)} %get-tuple-element.138), channel_id=1, source_target_pairs={{0,8},{8,0},{1,9},{9,1},{2,10},{10,2},{3,11},{11,3},{4,12},{12,4},... | collective-permute-start | bytes 2359304 | tf_op jit(solution)/shard_map/ppermute | solution.py:441
  148.6 19.3 %collective-permute-start.70 = (f32[256,768]{1,0:T(8,128)}, f32[256,768]{1,0:T(8,128)S(1)}, u32[]{:S(2)}, u32[]{:S(2)}) collective-permute-start(f32[256,768]{1,0:T(8,128)} %get-tuple-element.138), channel_id=1, source_target_pairs={{0,16},{16,0},{1,17},{17,1},{2,18},{18,2},{3,19},{19,3},{4,20},{20... | collective-permute-start | bytes 2359304 | tf_op jit(solution)/shard_map/ppermute | solution.py:441
  150.8 35.2 %collective-permute-start.77 = (f32[256,768]{1,0:T(8,128)S(1)}, f32[256,768]{1,0:T(8,128)S(1)}, u32[]{:S(2)}, u32[]{:S(2)}) collective-permute-start(f32[256,768]{1,0:T(8,128)S(1)} %copy-done.21), channel_id=1, source_target_pairs={{0,8},{8,0},{1,9},{9,1},{2,10},{10,2},{3,11},{11,3},{4,12},{12,4},... | collective-permute-start | bytes 2359304 | tf_op jit(solution)/shard_map/ppermute | solution.py:441
  151.2 19.8 %collective-permute-start.78 = (f32[256,768]{1,0:T(8,128)S(1)}, f32[256,768]{1,0:T(8,128)S(1)}, u32[]{:S(2)}, u32[]{:S(2)}) collective-permute-start(f32[256,768]{1,0:T(8,128)S(1)} %copy-done.21), channel_id=1, source_target_pairs={{0,1},{1,0},{2,3},{3,2},{4,5},{5,4},{6,7},{7,6},{8,9},{9,8},{10,11... | collective-permute-start | bytes 2359304 | tf_op jit(solution)/shard_map/ppermute | solution.py:441
  152.9 31.9 %collective-permute-start.79 = (f32[256,768]{1,0:T(8,128)S(1)}, f32[256,768]{1,0:T(8,128)S(1)}, u32[]{:S(2)}, u32[]{:S(2)}) collective-permute-start(f32[256,768]{1,0:T(8,128)S(1)} %copy-done.21), channel_id=1, source_target_pairs={{0,16},{16,0},{1,17},{17,1},{2,18},{18,2},{3,19},{19,3},{4,20},{20... | collective-permute-start | bytes 2359304 | tf_op jit(solution)/shard_map/ppermute | solution.py:441
  154.5 38.8 %collective-permute-start.71 = (f32[128,768]{1,0:T(8,128)S(1)}, f32[128,768]{1,0:T(8,128)S(1)}, u32[]{:S(2)}, u32[]{:S(2)}) collective-permute-start(f32[128,768]{1,0:T(8,128)S(1)} %slice.171), channel_id=1, source_target_pairs={{0,16},{16,0},{1,17},{17,1},{2,18},{18,2},{3,19},{19,3},{4,20},{20... | collective-permute-start | bytes 1179656 | tf_op jit(solution)/shard_map/ppermute | solution.py:441
  168.0 34.6 %collective-permute-start.73 = (f32[256,768]{1,0:T(8,128)S(1)}, f32[256,768]{1,0:T(8,128)S(1)}, u32[]{:S(2)}, u32[]{:S(2)}) collective-permute-start(f32[256,768]{1,0:T(8,128)S(1)} %collective-permute-done.69), channel_id=1, source_target_pairs={{0,8},{8,0},{1,9},{9,1},{2,10},{10,2},{3,11},{11,3},{4,12},{12,4},... | collective-permute-start | bytes 2359304 | tf_op jit(solution)/shard_map/ppermute | solution.py:441
  171.0 23.6 %collective-permute-start.72 = (f32[128,768]{1,0:T(8,128)S(1)}, f32[128,768]{1,0:T(8,128)S(1)}, u32[]{:S(2)}, u32[]{:S(2)}) collective-permute-start(f32[128,768]{1,0:T(8,128)S(1)} %slice.172), channel_id=1, source_target_pairs={{0,1},{1,0},{2,3},{3,2},{4,5},{5,4},{6,7},{7,6},{8,9},{9,8},{10,11... | collective-permute-start | bytes 1179656 | tf_op jit(solution)/shard_map/ppermute | solution.py:441
  184.8 16.9 %collective-permute-start.80 = (f32[128,768]{1,0:T(8,128)S(1)}, f32[128,768]{1,0:T(8,128)S(1)}, u32[]{:S(2)}, u32[]{:S(2)}) collective-permute-start(f32[128,768]{1,0:T(8,128)S(1)} %slice.173), channel_id=1, source_target_pairs={{0,16},{16,0},{1,17},{17,1},{2,18},{18,2},{3,19},{19,3},{4,20},{20... | collective-permute-start | bytes 1179656 | tf_op jit(solution)/shard_map/ppermute | solution.py:441
  186.0 16.5 %collective-permute-start.81 = (f32[128,768]{1,0:T(8,128)S(1)}, f32[128,768]{1,0:T(8,128)S(1)}, u32[]{:S(2)}, u32[]{:S(2)}) collective-permute-start(f32[128,768]{1,0:T(8,128)S(1)} %slice.174), channel_id=1, source_target_pairs={{0,1},{1,0},{2,3},{3,2},{4,5},{5,4},{6,7},{7,6},{8,9},{9,8},{10,11... | collective-permute-start | bytes 1179656 | tf_op jit(solution)/shard_map/ppermute | solution.py:441
  216.3 192.7 %reduce-scatter.3.cloned.1.call-start = ((), (), s32[]{:S(2)}) async-start(), calls=%async_computation.2 | async-start | bytes 2949120 | tf_op jit(solution)/shard_map/reduce_scatter | solution.py:593
  216.4 39.6 %collective-permute-start.48 = (f32[256,768]{1,0:T(8,128)}, f32[256,768]{1,0:T(8,128)S(1)}, u32[]{:S(2)}, u32[]{:S(2)}) collective-permute-start(f32[256,768]{1,0:T(8,128)} %get-tuple-element.137), channel_id=1, source_target_pairs={{0,1},{1,0},{2,3},{3,2},{4,5},{5,4},{6,7},{7,6},{8,9},{9,8},{10,11... | collective-permute-start | bytes 2359304 | tf_op jit(solution)/shard_map/ppermute | solution.py:441
  218.1 39.2 %collective-permute-start.47 = (f32[256,768]{1,0:T(8,128)}, f32[256,768]{1,0:T(8,128)S(1)}, u32[]{:S(2)}, u32[]{:S(2)}) collective-permute-start(f32[256,768]{1,0:T(8,128)} %get-tuple-element.137), channel_id=1, source_target_pairs={{0,8},{8,0},{1,9},{9,1},{2,10},{10,2},{3,11},{11,3},{4,12},{12,4},... | collective-permute-start | bytes 2359304 | tf_op jit(solution)/shard_map/ppermute | solution.py:441
  218.7 40.2 %collective-permute-start.49 = (f32[256,768]{1,0:T(8,128)}, f32[256,768]{1,0:T(8,128)S(1)}, u32[]{:S(2)}, u32[]{:S(2)}) collective-permute-start(f32[256,768]{1,0:T(8,128)} %get-tuple-element.137), channel_id=1, source_target_pairs={{0,16},{16,0},{1,17},{17,1},{2,18},{18,2},{3,19},{19,3},{4,20},{20... | collective-permute-start | bytes 2359304 | tf_op jit(solution)/shard_map/ppermute | solution.py:441
  255.1 19.2 %collective-permute-start.57 = (f32[256,768]{1,0:T(8,128)S(1)}, f32[256,768]{1,0:T(8,128)S(1)}, u32[]{:S(2)}, u32[]{:S(2)}) collective-permute-start(f32[256,768]{1,0:T(8,128)S(1)} %get-tuple-element.115.refs_0_), channel_id=1, source_target_pairs={{0,1},{1,0},{2,3},{3,2},{4,5},{5,4},{6,7},{7,6},{8,9},{9,8},{10,11... | collective-permute-start | bytes 2359304 | tf_op jit(solution)/shard_map/ppermute | solution.py:441
  256.0 19.6 %collective-permute-start.58 = (f32[256,768]{1,0:T(8,128)S(1)}, f32[256,768]{1,0:T(8,128)S(1)}, u32[]{:S(2)}, u32[]{:S(2)}) collective-permute-start(f32[256,768]{1,0:T(8,128)S(1)} %get-tuple-element.115.refs_0_), channel_id=1, source_target_pairs={{0,16},{16,0},{1,17},{17,1},{2,18},{18,2},{3,19},{19,3},{4,20},{20... | collective-permute-start | bytes 2359304 | tf_op jit(solution)/shard_map/ppermute | solution.py:441
  257.3 25.9 %collective-permute-start.50 = (f32[128,768]{1,0:T(8,128)S(1)}, f32[128,768]{1,0:T(8,128)S(1)}, u32[]{:S(2)}, u32[]{:S(2)}) collective-permute-start(f32[128,768]{1,0:T(8,128)S(1)} %slice.167), channel_id=1, source_target_pairs={{0,16},{16,0},{1,17},{17,1},{2,18},{18,2},{3,19},{19,3},{4,20},{20... | collective-permute-start | bytes 1179656 | tf_op jit(solution)/shard_map/ppermute | solution.py:441
  258.9 35.8 %collective-permute-start.52 = (f32[256,768]{1,0:T(8,128)S(1)}, f32[256,768]{1,0:T(8,128)S(1)}, u32[]{:S(2)}, u32[]{:S(2)}) collective-permute-start(f32[256,768]{1,0:T(8,128)S(1)} %collective-permute-done.48), channel_id=1, source_target_pairs={{0,8},{8,0},{1,9},{9,1},{2,10},{10,2},{3,11},{11,3},{4,12},{12,4},... | collective-permute-start | bytes 2359304 | tf_op jit(solution)/shard_map/ppermute | solution.py:441
  260.0 24.0 %collective-permute-start.51 = (f32[128,768]{1,0:T(8,128)S(1)}, f32[128,768]{1,0:T(8,128)S(1)}, u32[]{:S(2)}, u32[]{:S(2)}) collective-permute-start(f32[128,768]{1,0:T(8,128)S(1)} %slice.168), channel_id=1, source_target_pairs={{0,1},{1,0},{2,3},{3,2},{4,5},{5,4},{6,7},{7,6},{8,9},{9,8},{10,11... | collective-permute-start | bytes 1179656 | tf_op jit(solution)/shard_map/ppermute | solution.py:441
  274.3 20.7 %collective-permute-start.53 = (f32[256,768]{1,0:T(8,128)S(1)}, f32[256,768]{1,0:T(8,128)S(1)}, u32[]{:S(2)}, u32[]{:S(2)}) collective-permute-start(f32[256,768]{1,0:T(8,128)S(1)} %collective-permute-done.49), channel_id=1, source_target_pairs={{0,8},{8,0},{1,9},{9,1},{2,10},{10,2},{3,11},{11,3},{4,12},{12,4},... | collective-permute-start | bytes 2359304 | tf_op jit(solution)/shard_map/ppermute | solution.py:441
  275.6 16.1 %collective-permute-start.59 = (f32[128,768]{1,0:T(8,128)S(1)}, f32[128,768]{1,0:T(8,128)S(1)}, u32[]{:S(2)}, u32[]{:S(2)}) collective-permute-start(f32[128,768]{1,0:T(8,128)S(1)} %slice.169), channel_id=1, source_target_pairs={{0,16},{16,0},{1,17},{17,1},{2,18},{18,2},{3,19},{19,3},{4,20},{20... | collective-permute-start | bytes 1179656 | tf_op jit(solution)/shard_map/ppermute | solution.py:441
  284.0 12.7 %collective-permute-start.61 = (f32[256,768]{1,0:T(8,128)S(1)}, f32[256,768]{1,0:T(8,128)S(1)}, u32[]{:S(2)}, u32[]{:S(2)}) collective-permute-start(f32[256,768]{1,0:T(8,128)S(1)} %collective-permute-done.57), channel_id=1, source_target_pairs={{0,8},{8,0},{1,9},{9,1},{2,10},{10,2},{3,11},{11,3},{4,12},{12,4},... | collective-permute-start | bytes 2359304 | tf_op jit(solution)/shard_map/ppermute | solution.py:441
  330.4 13.1 %collective-permute-start.32 = (f32[32,768]{1,0:T(8,128)S(1)}, f32[32,768]{1,0:T(8,128)S(1)}, u32[]{:S(2)}, u32[]{:S(2)}) collective-permute-start(f32[32,768]{1,0:T(8,128)S(1)} %get-tuple-element.121), channel_id=1, source_target_pairs={{0,3},{1,2},{2,1},{3,0},{4,7},{5,6},{6,5},{7,4},{8,11},{9,10},{10,... | collective-permute-start | bytes 294920 | tf_op jit(solution)/shard_map/ppermute | solution.py:441
  351.9 15.4 %collective-permute-start.24 = (f32[32,768]{1,0:T(8,128)S(1)}, f32[32,768]{1,0:T(8,128)S(1)}, u32[]{:S(2)}, u32[]{:S(2)}) collective-permute-start(f32[32,768]{1,0:T(8,128)S(1)} %get-tuple-element.165), channel_id=1, source_target_pairs={{0,5},{1,4},{2,7},{3,6},{4,1},{5,0},{6,3},{7,2},{8,13},{9,12},{10,... | collective-permute-start | bytes 294920 | tf_op jit(solution)/shard_map/ppermute | solution.py:441
  354.3 20.7 %collective-permute-start.43 = (f32[40,768]{1,0:T(8,128)S(1)}, f32[40,768]{1,0:T(8,128)S(1)}, u32[]{:S(2)}, u32[]{:S(2)}) collective-permute-start(f32[40,768]{1,0:T(8,128)S(1)} %add.98), channel_id=1, source_target_pairs={{0,17},{1,16},{16,1},{17,0},{2,19},{3,18},{18,3},{19,2},{4,21},{5,... | collective-permute-start | bytes 368648 | tf_op jit(solution)/shard_map/ppermute | solution.py:441
  356.5 19.5 %collective-permute-start.42 = (f32[40,768]{1,0:T(8,128)S(1)}, f32[40,768]{1,0:T(8,128)S(1)}, u32[]{:S(2)}, u32[]{:S(2)}) collective-permute-start(f32[40,768]{1,0:T(8,128)S(1)} %add.98), channel_id=1, source_target_pairs={{0,16},{1,17},{16,0},{17,1},{2,18},{3,19},{18,2},{19,3},{4,20},{5,... | collective-permute-start | bytes 368648 | tf_op jit(solution)/shard_map/ppermute | solution.py:441
  361.2 17.1 %collective-permute-start.41 = (f32[40,768]{1,0:T(8,128)S(1)}, f32[40,768]{1,0:T(8,128)S(1)}, u32[]{:S(2)}, u32[]{:S(2)}) collective-permute-start(f32[40,768]{1,0:T(8,128)S(1)} %add.98), channel_id=1, source_target_pairs={{0,1},{1,0},{16,17},{17,16},{2,3},{3,2},{18,19},{19,18},{4,5},{5,4... | collective-permute-start | bytes 368648 | tf_op jit(solution)/shard_map/ppermute | solution.py:441
  378.3 11.5 %collective-permute-start.37 = (f32[32,768]{1,0:T(8,128)S(1)}, f32[32,768]{1,0:T(8,128)S(1)}, u32[]{:S(2)}, u32[]{:S(2)}) collective-permute-start(f32[32,768]{1,0:T(8,128)S(1)} %get-tuple-element.129), channel_id=1, source_target_pairs={{0,5},{1,4},{2,7},{3,6},{4,1},{5,0},{6,3},{7,2},{8,13},{9,12},{10,... | collective-permute-start | bytes 294920 | tf_op jit(solution)/shard_map/ppermute | solution.py:441
  378.9 31.5 %collective-permute-start.46 = (f32[40,768]{1,0:T(8,128)S(1)}, f32[40,768]{1,0:T(8,128)S(1)}, u32[]{:S(2)}, u32[]{:S(2)}) collective-permute-start(f32[40,768]{1,0:T(8,128)S(1)} %add_add_fusion.1), channel_id=1, source_target_pairs={{0,6},{2,4},{4,2},{6,0},{1,7},{3,5},{5,3},{7,1},{8,14},{10,12},{12... | collective-permute-start | bytes 368648 | tf_op jit(solution)/shard_map/ppermute | solution.py:441
  379.7 30.8 %collective-permute-start.45 = (f32[40,768]{1,0:T(8,128)S(1)}, f32[40,768]{1,0:T(8,128)S(1)}, u32[]{:S(2)}, u32[]{:S(2)}) collective-permute-start(f32[40,768]{1,0:T(8,128)S(1)} %add_add_fusion.1), channel_id=1, source_target_pairs={{0,4},{2,6},{4,0},{6,2},{1,5},{3,7},{5,1},{7,3},{8,12},{10,14},{12... | collective-permute-start | bytes 368648 | tf_op jit(solution)/shard_map/ppermute | solution.py:441
  382.0 28.5 %collective-permute-start.44 = (f32[40,768]{1,0:T(8,128)S(1)}, f32[40,768]{1,0:T(8,128)S(1)}, u32[]{:S(2)}, u32[]{:S(2)}) collective-permute-start(f32[40,768]{1,0:T(8,128)S(1)} %add_add_fusion.1), channel_id=1, source_target_pairs={{0,2},{2,0},{4,6},{6,4},{1,3},{3,1},{5,7},{7,5},{8,10},{10,8},{12,... | collective-permute-start | bytes 368648 | tf_op jit(solution)/shard_map/ppermute | solution.py:441
  383.2 18.6 %collective-permute-start.38 = (f32[32,768]{1,0:T(8,128)S(1)}, f32[32,768]{1,0:T(8,128)S(1)}, u32[]{:S(2)}, u32[]{:S(2)}) collective-permute-start(f32[32,768]{1,0:T(8,128)S(1)} %get-tuple-element.130), channel_id=1, source_target_pairs={{0,6},{1,7},{2,4},{3,5},{4,2},{5,3},{6,0},{7,1},{8,14},{9,15},{10,... | collective-permute-start | bytes 294920 | tf_op jit(solution)/shard_map/ppermute | solution.py:441
  389.8 18.0 %collective-permute-start.39 = (f32[32,768]{1,0:T(8,128)S(1)}, f32[32,768]{1,0:T(8,128)S(1)}, u32[]{:S(2)}, u32[]{:S(2)}) collective-permute-start(f32[32,768]{1,0:T(8,128)S(1)} %get-tuple-element.131), channel_id=1, source_target_pairs={{0,7},{1,6},{2,5},{3,4},{4,3},{5,2},{6,1},{7,0},{8,15},{9,14},{10,... | collective-permute-start | bytes 294920 | tf_op jit(solution)/shard_map/ppermute | solution.py:441
  409.0 13.7 %collective-permute-start.87 = (f32[192,768]{1,0:T(8,128)}, f32[192,768]{1,0:T(8,128)S(1)}, u32[]{:S(2)}, u32[]{:S(2)}) collective-permute-start(f32[192,768]{1,0:T(8,128)} %reduce-scatter.5.cloned.1.call-done.refs_0_), channel_id=1, source_target_pairs={{0,16},{16,0},{1,17},{17,1},{2,18},{18,2},{3,19},{19,3},{4,20},{20... | collective-permute-start | bytes 1769480 | tf_op jit(solution)/shard_map/ppermute | solution.py:441
  409.0 26.3 %collective-permute-start.66 = (f32[192,768]{1,0:T(8,128)}, f32[192,768]{1,0:T(8,128)S(1)}, u32[]{:S(2)}, u32[]{:S(2)}) collective-permute-start(f32[192,768]{1,0:T(8,128)} %reduce-scatter.3.cloned.1.call-done.refs_0_), channel_id=1, source_target_pairs={{0,16},{16,0},{1,17},{17,1},{2,18},{18,2},{3,19},{19,3},{4,20},{20... | collective-permute-start | bytes 1769480 | tf_op jit(solution)/shard_map/ppermute | solution.py:441
  411.2 28.9 %collective-permute-start.86 = (f32[192,768]{1,0:T(8,128)}, f32[192,768]{1,0:T(8,128)S(1)}, u32[]{:S(2)}, u32[]{:S(2)}) collective-permute-start(f32[192,768]{1,0:T(8,128)} %reduce-scatter.5.cloned.1.call-done.refs_0_), channel_id=1, source_target_pairs={{0,8},{8,0},{1,9},{9,1},{2,10},{10,2},{3,11},{11,3},{4,12},{12,4},... | collective-permute-start | bytes 1769480 | tf_op jit(solution)/shard_map/ppermute | solution.py:441
  413.2 29.8 %collective-permute-start.65 = (f32[192,768]{1,0:T(8,128)}, f32[192,768]{1,0:T(8,128)S(1)}, u32[]{:S(2)}, u32[]{:S(2)}) collective-permute-start(f32[192,768]{1,0:T(8,128)} %reduce-scatter.3.cloned.1.call-done.refs_0_), channel_id=1, source_target_pairs={{0,8},{8,0},{1,9},{9,1},{2,10},{10,2},{3,11},{11,3},{4,12},{12,4},... | collective-permute-start | bytes 1769480 | tf_op jit(solution)/shard_map/ppermute | solution.py:441
  422.7 17.4 %collective-permute-start.88 = (f32[192,768]{1,0:T(8,128)S(1)}, f32[192,768]{1,0:T(8,128)S(1)}, u32[]{:S(2)}, u32[]{:S(2)}) collective-permute-start(f32[192,768]{1,0:T(8,128)S(1)} %collective-permute-done.87.refs_2_), channel_id=1, source_target_pairs={{0,8},{8,0},{1,9},{9,1},{2,10},{10,2},{3,11},{11,3},{4,12},{12,4},... | collective-permute-start | bytes 1769480 | tf_op jit(solution)/shard_map/ppermute | solution.py:441
  (124 other events, 1347.5 us)
Sparse Core Ops, SparseCore 0:
  216.4 48.1 reduce-scatter.4
  307.3 49.7 reduce-scatter.2

commit v3 on v2

v3 whole, which is shorter than its diff:
```python
import functools
import math

import jax
import jax.numpy as jnp
import ml_dtypes
import numpy as np
from jax import lax
from jax.experimental import pallas as pl
from jax.experimental.pallas import tpu as pltpu
from jax.sharding import Mesh
from jax.sharding import PartitionSpec as P

EPSILON = 1e-05
DP = ("do", "dy", "core")
SEQ = ("zh", "zl", "x")
ROW = ("zl", "x")
PLANES = ("zh", "zl")
SHARES = ("dy", "core")
PLANE = ("dy", "core", "x")
ALL = DP + SEQ
MARK = 128
LOW = jnp.bfloat16
HIGH = jnp.float32
VMEM = pl.BlockSpec(memory_space=pltpu.VMEM)
NEAR = pl.BlockSpec(memory_space=pltpu.VMEM)
SMEM = pl.BlockSpec(memory_space=pltpu.SMEM)
ANY = pl.BlockSpec(memory_space=pl.ANY)
HBM = pl.BlockSpec(memory_space=pltpu.HBM)


MICROSECONDS = {
    "spread_marked": 2.0,
    "pick": 1.5,
    "cut": 5.9,
    "enter": 1.7,
    "spread": 1.0,
    "own_part": 1.5,
    "own_fetch": 5.5,
    "mix": 2.2,
    "layer_forward": 12.0,
    "layer_backward": 7.5,
    "layer_feed": 7.5,
    "layer_stream": 12.0,
    "delta": 2.8,
    "weight_grads": 12.0,
    "leave": 0.9,
    "collect": 2.2,
    "finish": 3.3,
}


def split_table(values):
    head = values.astype(ml_dtypes.bfloat16)
    return np.stack([head, (values - head.astype(np.float64)).astype(ml_dtypes.bfloat16)])


def feature_table(width):
    half = width // 2
    angle = np.outer(np.arange(width), np.arange(width)) % width * (2.0 * math.pi / width)
    cos, sin = np.cos(angle) / math.sqrt(width), np.sin(angle) / math.sqrt(width)
    return split_table(np.concatenate([cos[:, :half], cos[:, half : half + 1], sin[:, 1:half]], 1))


def mirror_table(half):
    table = np.zeros((half, half), ml_dtypes.bfloat16)
    table[half - np.arange(1, half), np.arange(1, half)] = 1.0
    return table


def pair_of(count, at):
    return at, 2 * count - at if at else count


def owned(count, part, seq, at):
    first, second = pair_of(count, at)
    pos = np.arange(seq * part).reshape(seq, part // (2 * count), 2 * count)
    return np.stack([pos[:, :, first], pos[:, :, second]], 1).reshape(-1)


def position_tables(count, part, seq):
    length = seq * part
    step = 2 * count
    span = length // step
    keep = span // step
    w = 2.0 * math.pi / length
    own = [owned(count, part, seq, i) for i in range(count)]
    local = length // count
    send = np.zeros((2, count, count, 2 * keep, local))
    recv = np.zeros((2, count, count, local, 2 * keep))
    block = np.zeros((2, count, local, local))
    scale = 1.0 / math.sqrt(length)

    def kept(i):
        if i:
            return [(i + step * s, 2) for s in range(keep)]
        ends = [(step * s, 1 if s in (0, keep // 2) else 2) for s in range(keep // 2 + 1)]
        return ends + [(count + step * s, 2) for s in range(keep // 2)]

    for j in range(count):
        n = own[j]
        first = n % step == j
        theta = 2.0 * math.pi * j / step
        for i in range(count):
            if i == j:
                angle = w * (np.outer(n, n) % length)
                block[0, i], block[1, i] = np.cos(angle) * scale, np.sin(angle) * scale
                continue
            at = 0
            slots = {}
            for kap, kinds in kept(i):
                cos, sin = np.cos(w * (kap * n % length)), np.sin(w * (kap * n % length))
                if j:
                    sign = np.where(first, 1.0, -1.0)
                    rows = (cos, sign * sin, sign * cos, sin)
                else:
                    rows = (cos * first, cos * ~first, sin * first, sin * ~first)
                if kinds == 2:
                    send[0, j, i, at], send[0, j, i, at + 1] = rows[:2]
                    send[1, j, i, at], send[1, j, i, at + 1] = rows[2:]
                    slots[kap] = (at, at + 1, 0.0)
                else:
                    phi = w * (kap * j % length)
                    send[0, j, i, at] = math.cos(phi) * rows[0] + math.sin(phi) * rows[1]
                    send[1, j, i, at] = math.cos(phi) * rows[2] + math.sin(phi) * rows[3]
                    slots[kap] = (at, at, phi)
                at += kinds
            for index, k in enumerate(own[i]):
                kap, turn = k % span, k // span
                mirrored = kap not in slots
                p_at, q_at, phi = slots[(span - kap) % span if mirrored else kap]
                pair = np.zeros((2, 2 * keep))
                if p_at == q_at:
                    pair[0, p_at], pair[1, p_at] = math.cos(phi), math.sin(phi)
                else:
                    pair[0, p_at], pair[1, q_at] = 1.0, 1.0
                even, odd = pair, pair
                if j:
                    if mirrored:
                        c, s = math.cos(theta), math.sin(theta)
                        even = odd = np.stack([c * pair[0] + s * pair[1], s * pair[0] - c * pair[1]])
                    c, s = math.cos(theta * turn), math.sin(theta * turn)
                    recv[0, i, j, index] = c * even[0] - s * even[1]
                    recv[1, i, j, index] = s * odd[0] + c * odd[1]
                else:
                    flip = (-1.0) ** turn
                    if mirrored:
                        even, odd = pair * np.array([[1.0], [-1.0]]), pair * np.array([[-1.0], [1.0]])
                    recv[0, i, j, index] = even[0] + flip * even[1]
                    recv[1, i, j, index] = odd[0] + flip * odd[1]
    recv = recv * scale
    sends, recvs, blocks = [], [], []
    for at in range(seq):
        i = at % count
        order = np.arange(local).reshape(seq, -1)[[at ^ k for k in range(seq)]].reshape(-1)
        others = [i ^ k for k in range(1, count)]
        sends.append(send[:, i, others].reshape(2, -1, local)[:, :, order])
        cos = np.concatenate([recv[0, i, j] for j in others], 1)[order]
        sin = np.concatenate([recv[1, i, j] for j in others], 1)[order]
        recvs.append(np.stack([np.concatenate([cos, -sin], 1), np.concatenate([cos, sin], 1)]))
        cos, sin = (block[h, i][order][:, order] for h in range(2))
        blocks.append(np.stack([np.concatenate([cos, -sin], 1), np.concatenate([cos, sin], 1)]))
    return tuple(np.moveaxis(split_table(np.stack(t)), 0, 1) for t in (sends, recvs, blocks))


def wide(left, right, contract=(1, 0)):
    return lax.dot_general(left, right, ((contract[:1], contract[1:]), ((), ())), preferred_element_type=HIGH)


def split(values):
    head = values.astype(LOW)
    return head, (values - head.astype(HIGH)).astype(LOW)


def triple(left, right):
    return wide(left[0], right[0]) + wide(left[0], right[1]) + wide(left[1], right[0])


def first_lane(values):
    return lax.broadcasted_iota(jnp.int32, values.shape, 1) == 0


def mean(values):
    return jnp.mean(values, axis=-1, keepdims=True)


def normalize(values):
    centered = values - mean(values)
    inverse = lax.rsqrt(mean(centered * centered) + EPSILON)
    return centered * inverse, inverse


def norm_back(upstream, unit, inverse, gain):
    scaled = upstream * gain
    return inverse * (scaled - mean(scaled) - unit * mean(scaled * unit))


def gelu_parts(p):
    c = math.sqrt(2.0 / math.pi)
    square = p * p
    t = jnp.tanh(p * (c + 0.044715 * c * square))
    halves = 0.5 + 0.5 * t
    slope = halves + p * (0.5 - 0.5 * (t * t)) * (c + 3.0 * 0.044715 * c * square)
    return p * halves, slope


def stage_one(values, feature_ref, send_ref, spectrum_ref, sent_refs):
    half = values.shape[1] // 2
    parts = split(values)
    spectrum = triple(parts, (feature_ref[0], feature_ref[1]))
    spectrum_ref[...] = spectrum
    head, tail = split(spectrum)
    lanes = half + 128
    even = triple((send_ref[0, 0], send_ref[1, 0]), (head[:, :lanes], tail[:, :lanes]))
    odd = triple((send_ref[0, 1], send_ref[1, 1]), (head[:, half:], tail[:, half:]))
    middle = jnp.where(first_lane(even[:, half:]), even[:, half:], odd[:, :128])
    rows = sent_refs[0].shape[0]
    for k, ref in enumerate(sent_refs):
        at = slice(k * rows, (k + 1) * rows)
        ref[:, :half] = even[at, :half]
        ref[:, half:lanes] = middle[at]
        ref[:, lanes:] = odd[at, 128:]


def unpack(packed, mirror, table_ref):
    half = packed.shape[1] // 2
    head, tail = split(packed)

    def stack(part):
        low, high = part[:, :half], part[:, half:]
        back = wide(jnp.concatenate([low, high], 0), mirror).astype(LOW)
        count = low.shape[0]
        turned = back[:count]
        middle = jnp.where(first_lane(turned[:, :128]), high[:, :128].astype(HIGH), turned[:, :128].astype(HIGH))
        turned = jnp.concatenate([middle.astype(LOW), turned[:, 128:]], 1)
        edge = jnp.where(first_lane(high[:, :128]), 0.0, high[:, :128].astype(HIGH)).astype(LOW)
        high = jnp.concatenate([edge, high[:, 128:]], 1)
        return jnp.concatenate([low, high], 0), jnp.concatenate([turned, back[count:]], 0)

    head_pair, tail_pair = stack(head), stack(tail)
    sides = [
        triple((table_ref[0, side], table_ref[1, side]), (head_pair[side], tail_pair[side])) for side in range(2)
    ]
    return jnp.concatenate(sides, 1)


def stage_two(got_refs, mirror_ref, recv_ref):
    got = jnp.concatenate([ref[...] for ref in got_refs], 0)
    return unpack(got, mirror_ref[...], recv_ref)


def call(kernel, name, inputs, outs, after=(), limit=24, token=False, near=False, **more):
    count, end = len(after), len(after) + len(inputs) + len(outs)

    def body(*refs):
        if token:
            kernel(*refs[count:end], *refs[end + 1 :])
            refs[end][...] = jnp.zeros_like(refs[end])
        else:
            kernel(*refs[count:])

    in_specs = more.pop("in_specs", None)
    if in_specs is None:
        in_specs = [SMEM if a.dtype == jnp.int32 and len(a.shape) == 1 else VMEM for a in inputs]
    out_specs = list(more.pop("out_specs", [VMEM] * len(outs)))
    far = lambda s: s is HBM or s.block_shape is not None and not near
    place = lambda s: pltpu.HBM if far(s) else pltpu.VMEM if s is NEAR else None
    inputs = [pltpu.with_memory_space_constraint(a, place(s)) if place(s) else a for a, s in zip(inputs, in_specs)]
    out_shape = [place(s)(o.shape, o.dtype) if place(s) else o for o, s in zip(outs, out_specs)]
    results = pl.pallas_call(
        body,
        in_specs=[ANY] * count + list(in_specs),
        out_specs=out_specs + [VMEM] * token,
        out_shape=out_shape + [array(8, 128)] * token,
        compiler_params=pltpu.CompilerParams(vmem_limit_bytes=limit * 2**20),
        cost_estimate=pl.CostEstimate(flops=int(MICROSECONDS[name] * 1.15e+09), bytes_accessed=0, transcendentals=0),
        name=name,
        **more,
    )(*after, *inputs)
    return list(results)


def hold(values, after):
    count = len(after)
    after = [pltpu.with_memory_space_constraint(a, pltpu.HBM) if math.prod(a.shape) > 8192 else a for a in after]
    return pl.pallas_call(
        lambda *refs: None,
        in_specs=[ANY] * (count + 1),
        out_specs=ANY,
        out_shape=array(*values.shape),
        input_output_aliases={count: 0},
        compiler_params=pltpu.CompilerParams(vmem_limit_bytes=2**20),
        name="hold",
    )(*after, values)


def array(*shape, dtype=HIGH):
    return jax.ShapeDtypeStruct(shape, dtype)


def pick_kernel(at_ref, *refs):
    *refs, sems = refs
    half = len(refs) // 2
    wait_all(start_all([(source.at[at_ref[0]], target) for source, target in zip(refs[:half], refs[half:])], sems))


def cut_kernel(layer, order, piece, blocks_ref, shares_ref, up_ref, down_ref, up_out, down_out, held, chosen_up, chosen_down, sems, down_sems):
    count, _, block = held.shape
    copies = []
    for b in range(count):
        start = pl.multiple_of(blocks_ref[b] * block, 128)
        copies.append(start_all([(up_ref.at[layer, :, pl.ds(start, block)], held.at[b])], sems.at[pl.ds(b, 1)]))
    downs = []
    for p, (b, h) in enumerate(order):
        start = pl.multiple_of(blocks_ref[b] * block + shares_ref[h] * piece, 16)
        target = chosen_down.at[p * piece : (p + 1) * piece]
        downs.append(pltpu.make_async_copy(down_ref.at[layer, pl.ds(start, piece), :], target, down_sems.at[p]))
        downs[-1].start()
    row = lax.broadcasted_iota(jnp.int32, (piece, block), 0)
    lane = lax.broadcasted_iota(jnp.int32, (piece, block), 1)
    chosen = [(lane == row + share * piece).astype(HIGH).astype(LOW) for share in (shares_ref[0], shares_ref[1])]
    wait_all(downs)
    outs = start_all([(chosen_down, down_out)], sems.at[pl.ds(count, 1)])
    for b in range(count):
        wait_all(copies[b])
        for p, (of, h) in enumerate(order):
            if of == b:
                chosen_up[p * piece : (p + 1) * piece] = wide(chosen[h], held[b], (1, 1)).astype(LOW)
    wait_all(outs + start_all([(chosen_up, up_out)], sems.at[pl.ds(0, 1)]))


def class_rows(count, dest):
    row, i = dest // count, dest % count
    if isinstance(dest, int):
        return row, pair_of(count, i)
    return row, (i, jnp.where(i == 0, count, 2 * count - i))


def spread_marked_kernel(count, at_ref, *rest):
    sources, (*outs, held), targets, sems = rest[:4], rest[4:-5], rest[-5:-1], rest[-1]
    wait_all(start_all(zip(sources, targets), sems))
    values_ref, segments_ref, padding_ref, table_ref = targets
    rows, part, width = values_ref.shape
    units = part // (2 * count)
    flags = jnp.concatenate([padding_ref[...], segments_ref[...], jnp.zeros((8 - 2 * rows, part), jnp.int32)], 0)
    flags = flags.astype(HIGH).astype(LOW)
    at = lax.broadcasted_iota(jnp.int32, (8, MARK), 0)
    lane = lax.broadcasted_iota(jnp.int32, (8, MARK), 1)
    for row in range(rows):
        pick = ((at == row) & (lane == 0)) | ((at == rows + row) & (lane == 1))
        marks = wide(flags, pick.astype(HIGH).astype(LOW), (0, 0))
        kind = marks[:, 1:2]
        values = values_ref[row]
        for t in range(table_ref.shape[0]):
            values = values + jnp.where(kind == float(t), table_ref[t : t + 1, :], 0.0)
        held[row, :, :, :width] = values.reshape(units, 2 * count, width)
        held[row, :, :, width:] = marks.reshape(units, 2 * count, MARK)
    for k, out in enumerate(outs):
        row, classes = class_rows(count, at_ref[0] ^ k)
        for h, at in enumerate(classes):
            out[h * units : (h + 1) * units, :] = held[row, :, at, :]


def spread_kernel(count, values_ref, out):
    rows, units, step, width = values_ref.shape
    for dest in range(rows * count):
        row, classes = class_rows(count, dest)
        for h, at in enumerate(classes):
            out[dest, h * units : (h + 1) * units, :] = values_ref[row, :, at, :]


def collect_kernel(count, blocks, *outs):
    rows, units, step, width = outs[0].shape
    part = blocks.shape[1] // len(outs)
    for source in range(rows * count):
        row, classes = class_rows(count, source)
        for n, out in enumerate(outs):
            for h, at in enumerate(classes):
                first = n * part + h * units
                out[row, :, at, :] = blocks[source, first : first + units, :]


def turned(at_ref, blocks):
    return [at_ref[0] ^ k for k in range(blocks)]


def enter_kernel(blocks, *refs):
    sources = refs[:blocks]
    feature_ref, send_ref, carried_ref, marks_ref, spectrum_ref, *sent_refs, held, sems = refs[blocks:]
    width = carried_ref.shape[1]
    rows = held.shape[0] // blocks
    wait_all(start_all([(ref, held.at[k * rows : (k + 1) * rows]) for k, ref in enumerate(sources)], sems))
    values = held[:, :width]
    carried_ref[...] = values
    marks_ref[...] = held[:, width:]
    stage_one(values * held[:, width : width + 1], feature_ref, send_ref, spectrum_ref, sent_refs)


def own_kernel(masked, layer, *refs):
    if layer is not None:
        *refs, up_in, down_in, out_ref, up_out, down_out, sems = refs
        copies = start_all([(up_in.at[layer], up_out), (down_in.at[layer], down_out)], sems)
    else:
        *refs, out_ref = refs
        copies = []
    spectrum_ref, carried_ref, mirror_ref, block_ref, *marks = refs
    mixed = unpack(spectrum_ref[...], mirror_ref[...], block_ref)
    if masked:
        mixed = mixed * marks[0][:, :1]
    out_ref[...] = carried_ref[...] + mixed
    wait_all(copies)


LANES = 4


def copies_of(pairs, sems):
    found = []
    for k, (source, target) in enumerate(pairs):
        rows = source.shape[0]
        parts = LANES if rows % (16 * LANES) == 0 else 1
        for part in range(parts):
            at = pl.ds(part * (rows // parts), rows // parts)
            found.append(pltpu.make_async_copy(source.at[at], target.at[at], sems.at[k, part]))
    return found


def start_all(pairs, sems):
    copies = copies_of(pairs, sems)
    for copy in copies:
        copy.start()
    return copies


def wait_all(copies):
    for copy in copies:
        copy.wait()


def keep(unit, inverse, held):
    width = unit.shape[1]
    held[:, :width] = unit
    held[:, width:] = jnp.broadcast_to(inverse, (unit.shape[0], held.shape[1] - width))


def weight_copies(layer, up_ref, down_ref, up_held, down_held, sems, chunk):
    width = up_held.shape[1]
    at = pl.ds(pl.multiple_of(chunk * width, 128), width)
    return (
        pltpu.make_async_copy(up_ref.at[layer, :, at], up_held.at[chunk], sems.at[0, chunk]),
        pltpu.make_async_copy(down_ref.at[layer, at, :], down_held.at[chunk], sems.at[1, chunk]),
    )


def next_weights(layer, refs, chunk):
    wait_all(weight_copies(layer, *refs, chunk))

    @pl.when(chunk + 1 < pl.num_programs(0))
    def _():
        for copy in weight_copies(layer, *refs, chunk + 1):
            copy.start()


def mix_kernel(layer, got, *refs):
    got_refs, refs = refs[:got], refs[got:]
    base_ref, mirror_ref, recv_ref, gain_ref, shift_ref, normed_out, unit_out, held_normed, held, sems = refs
    mixed = base_ref[...] + stage_two(got_refs, mirror_ref, recv_ref)
    unit, inverse = normalize(mixed)
    held_normed[...] = unit * gain_ref[layer, 0:1, :] + shift_ref[layer, 0:1, :]
    copies = start_all([(held_normed, normed_out)], sems)
    keep(unit, inverse, held)
    wait_all(copies + start_all([(held, unit_out)], sems.at[pl.ds(1, 1)]))


def chunk_of(chunk, width):
    return pl.ds(pl.multiple_of(chunk * width, 128), width)


def feed_kernel(layer, last, *refs):
    if last:
        *refs, held, delta_ref, low_ref, total_ref, more_sems, out_sems = refs
    else:
        *refs, held, low_ref, total_ref, up_held, down_held, feature_ref, send_ref, sems, more_sems, out_sems = refs
    normed_in, up_ref, up_bias_ref, down_ref, down_bias_ref, gain_ref, shift_ref, *refs = refs
    chunk = pl.program_id(0)
    width = low_ref.shape[1]
    if last:
        at_ref, upstream_ref, slope_ref, minor_ref, delta_far, carried_out = refs
        fetched = [(normed_in, total_ref)]
    else:
        marks_ref, feature_in, send_in, slope_ref, carried_ref, spectrum_ref, *sent_refs, unit_out = refs
        fetched = [(normed_in, total_ref), (feature_in, feature_ref), (send_in, send_ref)]
        weights = (up_ref, down_ref, up_held, down_held, sems)

    @pl.when(chunk == 0)
    def _():
        copies = start_all(fetched[:1], more_sems)
        if not last:
            for copy in weight_copies(layer, *weights, 0):
                copy.start()
        wait_all(copies)
        normed = total_ref[...]
        low_ref[...] = normed.astype(LOW)
        total_ref[...] = normed + down_bias_ref[layer : layer + 1, :]

    if last:
        at = chunk_of(chunk, width)
        up, down = up_ref[:, at], down_ref[at, :]
    else:
        next_weights(layer, weights, chunk)
        up, down = up_held[chunk], down_held[chunk]

        @pl.when(chunk == 1)
        def _():
            start_all(fetched[1:], more_sems.at[pl.ds(1, 2)])

    preact = wide(low_ref[...], up) + up_bias_ref[layer : layer + 1, :]
    value, slope = gelu_parts(preact)
    slope_ref[...] = slope.astype(slope_ref.dtype)
    total_ref[...] += wide(value.astype(LOW), down)

    @pl.when(chunk == pl.num_programs(0) - 1)
    def _():
        unit, inverse = normalize(total_ref[...])
        gain = gain_ref[layer, 1:2, :]
        carried = unit * gain + shift_ref[layer, 1:2, :]
        if last:
            blocks, rows, _ = upstream_ref.shape
            order = turned(at_ref, blocks)
            upstream = jnp.concatenate([upstream_ref[at] for at in order], 0)
            delta_out(upstream, unit, inverse, gain, delta_ref, minor_ref)
            copies = start_all([(delta_ref, delta_far)], out_sems)
            for k, at in enumerate(order):
                held[at] = carried[k * rows : (k + 1) * rows]
            wait_all(copies + start_all([(held, carried_out)], out_sems.at[pl.ds(1, 1)]))
        else:
            keep(unit, inverse, held)
            copies = start_all([(held, unit_out)], out_sems)
            carried_ref[...] = carried
            wait_all(copies_of(fetched[1:], more_sems.at[pl.ds(1, 2)]))
            stage_one(carried * marks_ref[:, :1], feature_ref, send_ref, spectrum_ref, sent_refs)
            wait_all(copies)


def delta_out(upstream, unit, inverse, gain, delta_ref, minor_ref):
    delta = norm_back(upstream, unit, inverse, gain)
    delta_ref[...] = delta
    rows = [upstream * unit, upstream, delta.astype(LOW).astype(HIGH)]
    for at, value in enumerate(rows):
        minor_ref[at : at + 1, :] = jnp.sum(value, 0, keepdims=True)
    minor_ref[len(rows) :, :] = jnp.zeros_like(minor_ref[len(rows) :, :])


def delta_kernel(layer, got, *refs):
    got_refs, refs = refs[:got], refs[got:]
    base_ref, marks_ref, mirror_ref, recv_ref, unit_in, gain_ref, minor_ref, delta_far, delta_ref, held, sems = refs
    copies = start_all([(unit_in, held)], sems)
    upstream = base_ref[...] + marks_ref[:, :1] * stage_two(got_refs, mirror_ref, recv_ref)
    wait_all(copies)
    width = upstream.shape[1]
    unit, inverse = held[:, :width], held[:, width : width + 1]
    delta_out(upstream, unit, inverse, gain_ref[layer, 1:2, :], delta_ref, minor_ref)
    wait_all(start_all([(delta_ref, delta_far)], sems))


def backward_kernel(layer, near, *refs):
    if near:
        *refs, low_ref, total_ref, held_unit, feature_ref, send_ref, more_sems = refs
    else:
        *refs, low_ref, total_ref, held_unit, feature_ref, send_ref, more_sems, up_held, down_held, sems = refs
    delta_in, slope_ref, up_ref, down_ref, unit_in, gain_ref, feature_in, send_in, *refs = refs
    mixed_ref, minor_ref, spectrum_ref, *sent_refs = refs
    chunk = pl.program_id(0)
    width = low_ref.shape[1]
    fetched = [(unit_in, held_unit), (feature_in, feature_ref), (send_in, send_ref)]

    @pl.when(chunk == 0)
    def _():
        copies = start_all([(delta_in, total_ref)], more_sems)
        if not near:
            for copy in weight_copies(layer, up_ref, down_ref, up_held, down_held, sems, 0):
                copy.start()
        wait_all(copies)
        low_ref[...] = total_ref[...].astype(LOW)
        minor_ref[...] = jnp.zeros_like(minor_ref)

    if near:
        at = chunk_of(chunk, width)
        up, down = up_ref[:, at], down_ref[at, :]
    else:
        next_weights(layer, (up_ref, down_ref, up_held, down_held, sems), chunk)
        up, down = up_held[chunk], down_held[chunk]

    @pl.when(chunk == 1)
    def _():
        start_all(fetched, more_sems.at[pl.ds(1, 3)])

    slope = (wide(low_ref[...], down, (1, 1)) * slope_ref[...].astype(HIGH)).astype(LOW)
    minor_ref[pl.ds(2 + chunk, 1), :] = jnp.sum(slope.astype(HIGH), 0, keepdims=True)
    total_ref[...] += wide(slope, up, (1, 1))

    @pl.when(chunk == pl.num_programs(0) - 1)
    def _():
        upstream = total_ref[...]
        wait_all(copies_of(fetched, more_sems.at[pl.ds(1, 3)]))
        unit, inverse = held_unit[:, :width], held_unit[:, width : width + 1]
        minor_ref[0:1, :] = jnp.sum(upstream * unit, 0, keepdims=True)
        minor_ref[1:2, :] = jnp.sum(upstream, 0, keepdims=True)
        mixed = norm_back(upstream, unit, inverse, gain_ref[layer, 0:1, :])
        mixed_ref[...] = mixed
        stage_one(mixed, feature_ref, send_ref, spectrum_ref, sent_refs)


def leave_kernel(types, got, *refs):
    got_refs, refs = refs[:got], refs[got:]
    at_ref, base_ref, marks_ref, mirror_ref, recv_ref, minor_ref, out, held, sems = refs
    upstream = base_ref[...] + marks_ref[:, :1] * stage_two(got_refs, mirror_ref, recv_ref)
    kind = marks_ref[:, 1:2]
    for t in range(types):
        minor_ref[t : t + 1, :] = jnp.sum(jnp.where(kind == float(t), upstream, 0.0), 0, keepdims=True)
    minor_ref[types:, :] = jnp.zeros_like(minor_ref[types:, :])
    blocks, rows, _ = held.shape
    for k, at in enumerate(turned(at_ref, blocks)):
        held[at] = upstream[k * rows : (k + 1) * rows]
    wait_all(start_all([(held, out)], sems))


def grads_kernel(plan, places, counts, *refs):
    starts_ref, refs = refs[0], refs[1:]
    normed_refs, refs = refs[: counts[0]], refs[counts[0] :]
    delta_refs, refs = refs[: counts[1]], refs[counts[1] :]
    up_in, bias_ref, down_in, *refs = refs
    *refs, normed_held, delta_held, up_ref, down_ref, normed_low, delta_low, hidden, back, sems, more_sems, out_sems = refs
    results, outs = refs[: len(refs) // 2], refs[len(refs) // 2 :]
    step = pl.program_id(0)
    blocks = len(plan)
    rows = normed_held.shape[1]
    units = up_ref.shape[0]
    piece = units // len(places)
    share = units // (pl.num_programs(0) - blocks)

    def copies(b):
        found = []
        for refs, held, parts in ((normed_refs, normed_held, plan[b][0]), (delta_refs, delta_held, plan[b][1])):
            at = 0
            for index, start, count in parts:
                source = refs[index]
                if start is not None:
                    source = source.at[pl.ds(pl.multiple_of(starts_ref[start], 8), count)]
                target = held.at[b % 2, at : at + count]
                found.append(pltpu.make_async_copy(source, target, sems.at[b, len(found)]))
                at += count
        return found

    def start(b):
        for copy in copies(b):
            copy.start()

    for b in range(blocks):

        @pl.when(step == b)
        def _():
            if b == 0:
                start(0)
                fetched = start_all([(up_in, up_ref), (down_in, down_ref)], more_sems)
            wait_all(copies(b))
            if b + 1 < blocks:
                start(b + 1)
            if b == 0:
                wait_all(fetched)
            at = slice(b * rows, (b + 1) * rows)
            normed = normed_held[b % 2].astype(LOW)
            delta = delta_held[b % 2].astype(LOW)
            normed_low[at] = normed
            delta_low[at] = delta
            value, slope = gelu_parts(wide(normed, up_ref[...], (1, 1)) + bias_ref[...])
            hidden[at] = value.astype(LOW)
            back[at] = (wide(delta, down_ref[...], (1, 1)) * slope).astype(LOW)

    def sent(c):
        found = []
        for p in range(c * share // piece, (c + 1) * share // piece):
            for h, (out, slot, first) in enumerate(places[p]):
                at = (slot, pl.ds(first, piece))
                found.append(pltpu.make_async_copy(outs[out].at[at], results[out].at[at], out_sems.at[p, h]))
        return found

    chunks = units // share
    for c in range(chunks):

        @pl.when(step == blocks + c)
        def _():
            at = slice(c * share, (c + 1) * share)
            both = (wide(back[:, at], normed_low[...], (0, 0)), wide(hidden[:, at], delta_low[...], (0, 0)))
            for p in range(c * share // piece, (c + 1) * share // piece):
                first_row = p * piece - c * share
                for (out, slot, first), a in zip(places[p], both):
                    outs[out][slot, first : first + piece] = a[first_row : first_row + piece]
            for copy in sent(c):
                copy.start()
            if c == chunks - 1:
                for k in range(chunks):
                    wait_all(sent(k))


def finish_kernel(layer, at_ref, *refs):
    *pieces, up_ref, down_ref, turned_ref = refs
    rows = pieces[0].shape[0] // 2
    for k, ref in enumerate(pieces[:4]):
        at = pl.multiple_of((at_ref[0] ^ k) * rows, 8)
        turned_ref[pl.ds(at, rows), :] = ref[:rows, :]
        down_ref[0, pl.ds(at, rows), :] = ref[rows:, :]
    up_ref[0] = turned_ref[...].T


def swap(values, axes, k):
    count = lax.axis_size(axes)
    return lax.ppermute(values, axes, [(i, i ^ k) for i in range(count)])


def exchange(blocks, axes, first=0):
    return [b if k == 0 else swap(b, axes, k) for k, b in enumerate(blocks, first)]


def sum_over(values, groups):
    for axes in groups:
        moved = [swap(values, axes, k) for k in range(1, lax.axis_size(axes))]
        values = sum(moved, values)
    return values


def local(inputs, segments, padding, type_table, ln_gain, ln_bias, up_weight, up_bias, down_weight, down_bias, out_grad):
    rows, part, width = inputs.shape
    layers, _, hidden_width = up_weight.shape
    types = type_table.shape[0]
    seq, count = lax.axis_size(SEQ), lax.axis_size(ROW)
    step = 2 * count
    units = part // step
    tokens = rows * part
    block = tokens // seq
    half = width // 2
    place = lax.axis_index(SEQ).reshape(1)

    feature = jnp.asarray(feature_table(width))
    mirror = jnp.asarray(mirror_table(half))
    tables = position_tables(count, part, seq)
    chunk = tables[0].shape[3] // (count - 1)
    sent_outs = [array(chunk, width)] * (count - 1)
    whole = array(tokens, width)
    kept = array(tokens, width + MARK)
    blocks_out = array(seq, block, width)
    minor_out = array(8, width)
    steps = hidden_width // width

    def spread(values, after):
        shaped = values.reshape(rows, units, step, width)
        out, token = call(functools.partial(spread_kernel, count), "spread", [shaped], [blocks_out], after, token=True)
        return lax.all_to_all(out, SEQ, 0, 0, tiled=True), token

    def collect(got, after):
        out = array(rows, units, step, width)
        *back, token = call(functools.partial(collect_kernel, count), "collect", [got], [out], after, token=True)
        return [b.reshape(inputs.shape) for b in back] + [token]

    weight_outs = [array(width, hidden_width, dtype=LOW), array(hidden_width, width, dtype=LOW)]

    def own(spectrum, carried, marks=None, after=(), token=False, layer=None):
        inputs = [spectrum, carried, mirror, block_t] + ([] if marks is None else [marks])
        kernel = functools.partial(own_kernel, marks is not None, layer)
        if layer is None:
            return call(kernel, "own_part", inputs, [whole], after, token=token)
        return call(
            kernel,
            "own_fetch",
            inputs + [up_weight, down_weight],
            [whole] + weight_outs,
            after,
            token=token,
            limit=8,
            in_specs=[VMEM] * len(inputs) + [HBM] * 2,
            out_specs=[VMEM, NEAR, NEAR],
            scratch_shapes=[pltpu.SemaphoreType.DMA((2, LANES))],
        )

    column = pl.BlockSpec((tokens, width), lambda c: (0, c))
    slope_out = array(tokens, hidden_width)
    scratch = [pltpu.VMEM((tokens, width), LOW), pltpu.VMEM((tokens, width), HIGH)]
    scratch += [pltpu.VMEM((steps, width, width), LOW)] * 2
    bias_spec = pl.BlockSpec((layers, width), lambda c: (0, c))

    held_kept = pltpu.VMEM(kept.shape, HIGH)
    dma = lambda n: pltpu.SemaphoreType.DMA((n, LANES))

    held_whole = pltpu.VMEM(whole.shape, HIGH)
    held_tables = [pltpu.VMEM(t, LOW) for t in (feature.shape, tables[0].shape[1:])]

    def mix(layer, got, base, after=()):
        inputs = got + [base, mirror, recv_t, ln_gain, ln_bias]
        return call(
            functools.partial(mix_kernel, layer, len(got)),
            "mix",
            inputs,
            [whole, kept],
            after,
            out_specs=[ANY, ANY] if layer == layers - 1 else [HBM, HBM],
            scratch_shapes=[held_whole, held_kept, dma(2)],
        )

    def feed(layer, normed, up, down, *more, after=(), token=False):
        last = layer == layers - 1
        inputs = [normed, up, up_bias, down, down_bias, ln_gain, ln_bias] + list(more)
        outs = [slope_out]
        outs += [minor_out, whole, blocks_out] if last else [whole, whole] + sent_outs + [kept]
        far = 2 if last else 1
        held = [pltpu.VMEM(blocks_out.shape, HIGH), held_whole] if last else [held_kept]
        fetches = [] if last else scratch[2:] + held_tables + [pltpu.SemaphoreType.DMA((2, steps))]
        weights = NEAR if last else HBM
        return call(
            functools.partial(feed_kernel, layer, last),
            "layer_feed" if last else "layer_forward",
            inputs,
            outs,
            after,
            near=last,
            token=token,
            grid=(steps,),
            in_specs=[ANY if last else HBM, weights, bias_spec, weights]
            + [VMEM] * 3
            + ([SMEM, VMEM] if last else [VMEM, HBM, HBM]),
            out_specs=[column] + [VMEM] * (len(outs) - 1 - far) + ([ANY, HBM] if last else [HBM]),
            scratch_shapes=held + scratch[:2] + fetches + [dma(3), dma(2)],
        )

    def backward(layer, delta, slope, up, down, kept, after=(), token=False):
        inputs = [delta, slope, up, down, kept, ln_gain, feature, send_t]
        outs = [whole, minor_out, whole] + sent_outs
        last = layer == layers - 1
        return call(
            functools.partial(backward_kernel, layer, last),
            "layer_backward" if last else "layer_stream",
            inputs,
            outs,
            after,
            near=last,
            token=token,
            grid=(steps,),
            in_specs=[ANY, column, NEAR, NEAR, ANY, VMEM, HBM, HBM]
            if last
            else [HBM, column, HBM, HBM, HBM, VMEM, HBM, HBM],
            out_specs=[VMEM] * len(outs),
            scratch_shapes=scratch[:2]
            + [held_kept]
            + held_tables
            + [dma(4)]
            + ([] if last else scratch[2:] + [pltpu.SemaphoreType.DMA((2, steps))]),
        )

    def delta(layer, got, base, marks, kept, after=()):
        inputs = got + [base, marks, mirror, recv_t, kept, ln_gain]
        return call(
            functools.partial(delta_kernel, layer, len(got)),
            "delta",
            inputs,
            [minor_out, whole],
            after,
            in_specs=[VMEM] * (len(got) + 4) + [HBM, VMEM],
            out_specs=[VMEM, HBM],
            scratch_shapes=[held_whole, held_kept, dma(1)],
        )

    columns = lax.axis_size("x")
    planes, shares = lax.axis_size(PLANES), lax.axis_size(SHARES)
    unit_block = hidden_width // seq
    piece = unit_block // shares
    x, dy, core, zh, zl = (lax.axis_index(a) for a in ("x", "dy", "core", "zh", "zl"))
    swapped = columns == 2

    def pair_pieces():
        nearby = [0, 1] if swapped else list(range(columns))
        own_x, own_dy, own_zh = (x, dy, zh) if swapped else (0, 0, 0)
        blocks = [((own_zh ^ b) * 2 + zl) * columns + (own_x ^ a) for a in nearby for b in (0, 1)]
        order = [(a * 2 + b, c) for a in nearby for c in (0, 1) for b in (0, 1)]
        return blocks, [(own_dy ^ c) * 2 + core for c in (0, 1)], order

    def plane_pieces():
        blocks = [z * columns + x for z in range(planes)]
        return blocks, [dy * 2 + (core ^ c) for c in (1, 0)], [(z, c) for c in (0, 1) for z in range(planes)]

    def cut(layer, after):
        blocks, shared, order = pair_pieces() if layer == layers - 1 else plane_pieces()
        starts = [blocks[b] * unit_block + shared[h] * piece for b, h in order]
        bias = jnp.concatenate([lax.dynamic_slice(up_bias, (layer, s), (1, piece)) for s in starts], 1)
        if unit_block % 128:
            up = [lax.dynamic_slice_in_dim(up_weight[layer], s, piece, 1).T for s in starts]
            down = [lax.dynamic_slice_in_dim(down_weight[layer], s, piece, 0) for s in starts]
            return jnp.concatenate(up, 0), bias, jnp.concatenate(down, 0), bias
        out = array(piece * len(order), width, dtype=LOW)
        up, down, token = call(
            functools.partial(cut_kernel, layer, order, piece),
            "cut",
            [jnp.stack(blocks).astype(jnp.int32), jnp.stack(shared).astype(jnp.int32), up_weight, down_weight],
            [out, out],
            after,
            token=True,
            in_specs=[SMEM, SMEM, HBM, HBM],
            out_specs=[HBM, HBM],
            scratch_shapes=[
                pltpu.VMEM((len(blocks), width, unit_block), LOW),
                pltpu.VMEM(out.shape, LOW),
                pltpu.VMEM(out.shape, LOW),
                dma(len(blocks) + 1),
                pltpu.SemaphoreType.DMA((len(order),)),
            ],
        )
        return up, bias, down, token

    def weight_grads(normed, starts, deltas, plan, cuts, places, outs, after=()):
        size = sum(r for _, _, r in plan[0][0])
        chosen = cuts[0].shape[0]
        share = max(384 // piece, 1) * piece
        total = len(plan) * size
        inputs = [jnp.stack(starts).astype(jnp.int32)] + normed + deltas + list(cuts[:3])
        return call(
            functools.partial(grads_kernel, plan, places, (len(normed), len(deltas))),
            "weight_grads",
            inputs,
            outs,
            after,
            token=True,
            limit=56,
            grid=(len(plan) + chosen // share,),
            in_specs=[SMEM] + [HBM] * (len(normed) + len(deltas)) + [HBM, VMEM, HBM],
            out_specs=[HBM] * len(outs),
            scratch_shapes=[pltpu.VMEM(o.shape, HIGH) for o in outs]
            + [pltpu.VMEM((2, size, width), HIGH)] * 2
            + [pltpu.VMEM(cuts[0].shape, LOW)] * 2
            + [pltpu.VMEM((total, width), LOW)] * 2
            + [pltpu.VMEM((total, chosen), LOW)] * 2
            + [pltpu.SemaphoreType.DMA((len(plan), 4)), dma(2), pltpu.SemaphoreType.DMA((len(places), 2))],
        )

    def shared_out(summed):
        along = swap(summed, "dy", 1)
        return [summed, swap(summed, "core", 1), along, swap(along, "core", 1)]

    def pair_grads(normed, deltas, cuts, after):
        plan = [([(b, None, tokens)], [(b, None, tokens)]) for b in range(4)]
        order = [(a, c, b) for a in range(columns) for c in (0, 1) for b in (0, 1)]
        if not swapped:
            places = [((0, p, 0), (0, p, piece)) for p in range(len(order))]
            out = array(len(order), 2 * piece, width)
            return weight_grads(normed, [0], deltas, plan, cuts, places, [out], after)
        places = [((a, 2 * c + b, 0), (2 + c, 2 * a + b, 0)) for a, c, b in order]
        return weight_grads(normed, [0], deltas, plan, cuts, places, [array(4, piece, width)] * 4, after)

    def pair_first(sums):
        if not swapped:
            return [lax.psum_scatter(sums[0], ("x", "dy", "zh"), scatter_dimension=0, tiled=True)], []
        up, up_far, down, down_far = sums
        got_up, got_down = swap(up_far, "x", 1), swap(down_far, "dy", 1)
        return [up[2:] + got_up[2:], down[2:] + got_down[2:]], [up[:2] + got_up[:2], down[:2] + got_down[:2]]

    def pair_step(far, near):
        if not swapped:
            return far, near
        got_up, got_down = swap(far[0], "dy", 1), swap(far[1], "x", 1)
        up, down = near
        far = jnp.concatenate([up[1] + got_up[1], down[1] + got_down[1]], 0)
        return [far], [jnp.concatenate([up[0] + got_up[0], down[0] + got_down[0]], 0)]

    def pair_last(far, near):
        if not swapped:
            summed = far[0].reshape(2 * piece, width)
            return lax.psum(summed, "do") if lax.axis_size("do") > 1 else summed
        return near[0] + swap(far[0], "zh", 1)

    def plane_first(values):
        if not swapped:
            return [lax.all_gather(values, ("dy", "x"), tiled=True)]
        return [swap(values, "x", 1), swap(values, "dy", 1)]

    def plane_rest(found):
        if not swapped:
            return []
        rows = tokens // 2
        return [swap(found[0][:rows], "dy", 1), swap(found[1][rows:], "x", 1)]

    def plane_grads(normed, deltas, cuts, after):
        group = lax.axis_size(("dy", "x"))
        out = array(planes, 2 * piece, width)
        places = [((h, z, 0), (h, z, piece)) for h in range(2) for z in range(planes)]
        rows = tokens // 2
        parts = [[(0, None, tokens)], [(1, None, tokens)], [(2, None, tokens)], [(3, None, rows), (4, None, rows)]]
        starts = [((dy ^ a) * columns + (x ^ b)) * tokens for a, b in ((0, 0), (0, 1), (1, 0), (1, 1))]
        if not swapped:
            parts = [[(0, b, tokens)] for b in range(group)]
            starts = [b * tokens for b in range(group)]
        starts = [jnp.asarray(s, jnp.int32) for s in starts]
        plan = [([(0, b, tokens)], parts[b]) for b in range(group)]
        return weight_grads([normed], starts, deltas, plan, cuts, places, [out, out], after)

    def plane_sum(both):
        summed = lax.psum_scatter(both.reshape(-1, width), PLANES, scatter_dimension=0, tiled=True)
        return lax.psum(summed, "do") if lax.axis_size("do") > 1 else summed

    def alone(stage, *operands):
        shapes = jax.eval_shape(stage, *operands)
        blank = lambda *_: jax.tree.map(lambda a: jnp.zeros(a.shape, a.dtype), shapes)
        return lax.cond(place[0] < 1000000, stage, blank, *operands)

    def send_and_own(sent, spectrum, mixed, marks):
        return exchange(sent, ROW, 1), own(spectrum, mixed, marks, token=True)

    held = call(
        functools.partial(spread_marked_kernel, count),
        "spread_marked",
        [place, inputs, segments, padding, type_table],
        [array(block, width + MARK)] * seq,
        in_specs=[SMEM] + [HBM] * 4,
        scratch_shapes=[pltpu.VMEM((rows, units, step, width + MARK), HIGH)]
        + [pltpu.VMEM(a.shape, a.dtype) for a in (inputs, segments, padding, type_table)]
        + [dma(4)],
    )
    held = exchange(held, SEQ)
    send_t, recv_t, block_t = call(
        pick_kernel,
        "pick",
        [place] + [jnp.asarray(t) for t in tables],
        [array(*t.shape[1:], dtype=LOW) for t in tables],
        held[1:4],
        in_specs=[SMEM] + [HBM] * 3,
        scratch_shapes=[dma(3)],
    )
    cuts = [None] * (layers - 1) + [cut(layers - 1, held[1:4])]
    carried, marks, spectrum, *sent = call(
        functools.partial(enter_kernel, seq),
        "enter",
        held + [feature, send_t],
        [whole, array(tokens, MARK), whole] + sent_outs,
        [cuts[-1][3]],
        in_specs=[HBM] * seq + [VMEM] * 2,
        scratch_shapes=[pltpu.VMEM((tokens, width + MARK), HIGH), dma(seq)],
    )
    upstream, made = spread(out_grad, sent[:1])
    saved = []
    for layer in range(layers - 1):
        got = exchange(sent, ROW, 1)
        base = own(spectrum, carried, after=[made])[0]
        normed, kept_one = mix(layer, got, base)
        all_normed = lax.all_gather(normed, ("dy", "x"), tiled=True)
        slope, carried, spectrum, *sent, kept_two = feed(layer, normed, up_weight, down_weight, marks, feature, send_t)
        saved.append((all_normed, kept_one, slope, kept_two))
    got = exchange(sent, ROW, 1)
    base, up, down = own(spectrum, carried, after=[upstream], layer=layers - 1)
    normed, kept_one = mix(layers - 1, got, base)

    def feed_stage(normed, kept, up, down, upstream):
        moved = swap(normed, "core", 1), swap(normed, "zl", 1)
        slope, minor_two, delta, outputs = feed(layers - 1, normed, up, down, place, upstream)
        return moved, minor_two, delta, outputs, backward(layers - 1, delta, slope, up, down, kept)

    moved_normed, minor_two, delta_two, outputs, (mixed, minor_one, spectrum, *sent) = alone(
        feed_stage, normed, kept_one, up, down, upstream
    )
    minors = [minor_two, minor_one]

    def send_and_swap(sent, spectrum, mixed, marks, normed_far, delta_two):
        got = exchange(sent, ROW, 1)
        return got, own(spectrum, mixed, marks)[0], swap(normed_far, "core", 1), swap(delta_two, "core", 1)

    got, base, *moved_delta = alone(send_and_swap, sent, spectrum, mixed, marks, moved_normed[1], delta_two)
    there, kept_one, slope, kept_two = saved[0]

    minor_two, delta_one = delta(0, got, base, marks, kept_two)

    def back_stage(delta_two, delta_one, kept_one, slope):
        cuts = cut(0, [delta_one])
        back = backward(0, delta_one, slope, up_weight, down_weight, kept_one, [cuts[3]])
        return swap(delta_two, "zl", 1), plane_first(delta_one), cuts, back

    delta_far, found, cuts[0], (mixed, minor_one, spectrum, *sent) = alone(
        back_stage, delta_two, delta_one, kept_one, slope
    )
    minors += [minor_two, minor_one]

    def send_and_rest(sent, spectrum, mixed, marks, found):
        return exchange(sent, ROW, 1), own(spectrum, mixed, marks)[0], plane_rest(found)

    got, base, rest = alone(send_and_rest, sent, spectrum, mixed, marks, found)
    found = ([delta_one] if swapped else []) + found + rest

    def grads_stage(normed, delta_two, delta_far, there, found, cuts, outputs):
        deltas = delta_two + [delta_far, swap(delta_far, "core", 1)]
        outputs = lax.all_to_all(outputs, SEQ, 0, 0, tiled=True)
        far, near, token = plane_grads(there, found, cuts[0], [])
        far = swap(far, "core", 1)
        *sums, token = pair_grads(normed, deltas, cuts[1], [token])
        return near + far, sums, outputs

    both, sums, outputs = alone(
        grads_stage,
        [normed, moved_normed[0], moved_normed[1], moved_delta[0]],
        [delta_two, moved_delta[1]],
        delta_far,
        there,
        found,
        cuts,
        outputs,
    )
    whole_sum = plane_sum(both)

    def first_stage(sums, got, base, marks):
        left = call(
            functools.partial(leave_kernel, types, len(got)),
            "leave",
            got + [place, base, marks, mirror, recv_t],
            [minor_out, blocks_out],
            out_specs=[VMEM, HBM],
            scratch_shapes=[pltpu.VMEM(blocks_out.shape, HIGH), dma(1)],
        )
        return pair_first(sums), left

    (far, near), (minor_table, blocks) = alone(first_stage, sums, got, base, marks)

    def middle_stage(far, near, outputs, minors):
        minor = sum_over(jnp.concatenate(minors, 0), [("core",)])
        return pair_step(far, near), minor, collect(outputs, [])[0]

    (far, near), minor, outputs = alone(middle_stage, far, near, outputs, minors + [minor_table])

    share = lax.axis_index(SHARES).reshape(1)
    outs = [array(layers, width, unit_block), array(layers, unit_block, width)]

    def finish(layer, pieces, grads):
        return call(
            functools.partial(finish_kernel, layer),
            "finish",
            [share] + pieces + grads,
            outs,
            in_specs=[SMEM] + [VMEM] * len(pieces) + [ANY] * len(grads),
            out_specs=[
                pl.BlockSpec((1,) + o.shape[1:], functools.partial(lambda l, i: (l, 0, 0), layer)) for o in outs
            ],
            grid=(1,),
            input_output_aliases={5: 0, 6: 1} if grads else {},
            scratch_shapes=[pltpu.VMEM((unit_block, width), HIGH)],
        )

    def last_stage(far, near, minor, whole_sum):
        grads = finish(0, shared_out(whole_sum), [])
        return pair_last(far, near), sum_over(minor, [("dy", "x"), ("do",)]), grads

    summed, minor, grads = alone(last_stage, far, near, minor, whole_sum)

    pieces = shared_out(summed)
    blocks = lax.all_to_all(hold(blocks, [summed]), SEQ, 0, 0, tiled=True)
    minor = sum_over(minor, [PLANES])
    input_grad, _ = collect(blocks, [])
    up_grad, down_grad = finish(1, pieces, grads)
    ends = [minor[16 * (layers - 1 - l) :][:16] for l in range(layers)]
    table_grad = minor[16 * layers :][:types]
    gain_grad = jnp.stack([jnp.stack([e[8], e[0]]) for e in ends])
    shift_grad = jnp.stack([jnp.stack([e[9], e[1]]) for e in ends])
    down_vec = jnp.stack([e[2] for e in ends])
    up_vec = jnp.stack([e[10 : 10 + steps].reshape(-1) for e in ends])
    up_vec = lax.dynamic_slice_in_dim(up_vec, place[0] * unit_block, unit_block, 1)

    return outputs, input_grad, table_grad, gain_grad, shift_grad, up_grad, up_vec, down_grad, down_vec


def solution(mesh):
    dp, seq = mesh.shape["dp"], mesh.shape["seq"]
    shape = (dp // 4, 2, 2, 2, 2, seq // 4)
    finer = Mesh(mesh.devices.reshape(shape), ALL)
    in_specs = (P(DP, SEQ, None), P(DP, SEQ), P(DP, SEQ)) + (P(),) * 7 + (P(DP, SEQ, None),)
    out_specs = (
        P(DP, SEQ, None),
        P(DP, SEQ, None),
        P(),
        P(),
        P(),
        P(None, None, SEQ),
        P(None, SEQ),
        P(None, SEQ, None),
        P(),
    )
    return jax.shard_map(local, mesh=finer, in_specs=in_specs, out_specs=out_specs, check_vma=False)
```

time: 460 us -> 325 us (0.71)
  the two profiles are of different devices: /device:TPU:9 before, /device:TPU:0 now
where the time goes in v3:
time: 325 us; the launch traced here: 318 us
  Pallas kernels  123 us (38%)
  waiting for transfers between devices  89.1 us (27%)
  starting transfers between devices  69.9 us (22%)
  between operations  15 us (5%)
  other arithmetic  10.6 us (3%)
  local copies, waits for them, and re-layouts  9.97 us (3%)
    pallas_call x24, Pallas kernels, call(): pl.pallas_call(body, in_specs=[ANY] * count + list(in_specs), out_specs=o...  123 us
    ppermute x48, waiting for transfers between devices, swap(): return lax.ppermute(values, axes, [(i, i ^ k) for i in range(count)])  76.3 us
    ppermute x48, starting transfers between devices, swap(): return lax.ppermute(values, axes, [(i, i ^ k) for i in range(count)])  55.2 us
    all_to_all x1, waiting for transfers between devices, local(): blocks = lax.all_to_all(hold(blocks, [summed]), SEQ, 0, 0, tiled=True)  6.75 us
  transfers between devices with their start and end apart: 53, of which 22 were waited for; matrix products, arithmetic and copies ran while one was open for 4% of the time, Pallas kernels for 31%

profile of v3, /device:TPU:0, one launch (start us, length us, event | category | flops | bytes accessed | tf_op | source)
XLA Modules:
  0.0 318.1 jit_solution(17247909405330143040)
XLA Ops:
  7.2 2.1 spread_marked.1
  9.9 2.9 collective-permute-start.29
  14.5 3.0 collective-permute-start.32
  18.9 3.6 %collective-permute-start.34 = (f32[32,896]{1,0:T(8,128)S(1)}, f32[32,896]{1,0:T(8,128)S(1)}, u32[]{:S(2)}, u32[]{:S(2)}) collective-permute-start(f32[32,896]{1,0:T(8,128)S(1)} %get-tuple-element.425), channel_id=1, source_target_pairs={{0,6},{1,7},{2,4},{3,5},{4,2},{5,3},{6,0},{7,1},{8,14},{9,15},{10,... | collective-permute-start | bytes 344072 | tf_op jit(solution)/shard_map/ppermute | solution.py:718
  22.7 6.0 %cut.3 = (bf16[768,768]{1,0:T(8,128)(2,1)}, bf16[768,768]{1,0:T(8,128)(2,1)}, f32[8,128]{1,0:T(8,128)S(1)}) custom-call(f32[32,896]{1,0:T(8,128)S(1)} %collective-permute-done.29.refs_0_.refs_2_, f32[32,896]{1,0:T(8,128)S(1)} %collective-permute-done.30.refs_1_.refs_3_, f32[32,896]{1,0:T(8,128)S(1)} %collective-permute-done.31.refs_2_.refs_4_, ...), custom_call_target="tpu_custom_call" | custom-call | flops 6784999936 | tf_op jit(solution)/shard_map/cut/pallas_call | solution.py:270
  30.5 4.2 %collective-permute-done.33.refs_6_ = f32[32,896]{1,0:T(8,128)S(1)} collective-permute-done((f32[32,896]{1,0:T(8,128)S(1)}, f32[32,896]{1,0:T(8,128)S(1)}, u32[]{:S(2)}, u32[]{:S(2)}) %collective-permute-start.33) | collective-permute-done | bytes 114720 | tf_op jit(solution)/shard_map/ppermute | solution.py:718
  35.5 3.9 %enter.1 = (f32[256,768]{1,0:T(8,128)S(1)}, f32[256,128]{1,0:T(8,128)}, f32[256,768]{1,0:T(8,128)S(1)}, f32[32,768]{1,0:T(8,128)S(1)}, f32[32,768]{1,0:T(8,128)S(1)}, /*index=5*/f32[32,768]{1,0:T(8,128)S(1)}) custom-call(f32[8,128]{1,0:T(8,128)S(1)} %get-tuple-element.421.refs_0_, f32[32,896]{1,0:T(8,128)} %copy-done.4, f32[32,896]{1,0:T(8,128)} %copy-done, ...), custom_call_target="tpu_custom_call" | custom-call | flops 1955000064 | tf_op jit(solution)/shard_map/enter/pallas_call | solution.py:270
  41.4 4.2 %collective-permute-start.37 = (f32[32,768]{1,0:T(8,128)S(1)}, f32[32,768]{1,0:T(8,128)S(1)}, u32[]{:S(2)}, u32[]{:S(2)}) collective-permute-start(f32[32,768]{1,0:T(8,128)S(1)} %get-tuple-element.429), channel_id=1, source_target_pairs={{0,2},{1,3},{2,0},{3,1},{4,6},{5,7},{6,4},{7,5},{8,10},{9,11},{10,... | collective-permute-start | bytes 294920 | tf_op jit(solution)/shard_map/ppermute | solution.py:718
  48.7 2.4 collective-permute-done.38.refs_2_
  51.1 2.2 mix.2
  53.4 5.0 %all-to-all-start.1 = ((f32[8,32,768]{2,1,0:T(8,128)}), f32[8,32,768]{2,1,0:T(8,128)S(1)}, u32[]{:S(2)}, u32[]{:S(2)}) async-start(f32[8,32,768]{2,1,0:T(8,128)} %get-tuple-element.441), calls=%async_computation.1 | async-start | bytes 1572864 | tf_op jit(solution)/shard_map/all_to_all | solution.py:758
  59.6 12.7 %layer_forward.1 = (f32[256,3072]{1,0:T(8,128)}, f32[256,768]{1,0:T(8,128)S(1)}, f32[256,768]{1,0:T(8,128)S(1)}, f32[32,768]{1,0:T(8,128)S(1)}, f32[32,768]{1,0:...) custom-call(f32[256,768]{1,0:T(8,128)} %get-tuple-element.436.refs_0_, bf16[2,768,3072]{2,1,0:T(8,128)(2,1)} %refs_5_.7, ...), custom_call_target="tpu_custom_call" | custom-call | flops 13799999488 | tf_op jit(solution)/shard_map/layer_forward/pallas_call | solution.py:270
  76.9 5.3 %own_fetch.1 = (f32[256,768]{1,0:T(8,128)S(1)}, bf16[768,3072]{1,0:T(8,128)(2,1)S(1)}, bf16[3072,768]{1,0:T(8,128)(2,1)S(1)}) custom-call(f32[8,32,768]{2,1,0:T(8,128)S(1)} %all-to-all-done.1.refs_0_, f32[256,768]{1,0:T(8,128)S(1)} %get-tuple-element.442.refs_1_, f32[256,768]{1,0:T(8,128)S(1)} %get-tuple-element.443.refs_2_, ...), custom_call_target="tpu_custom_call" | custom-call | flops 6325000192 | tf_op jit(solution)/shard_map/own_fetch/pallas_call | solution.py:270
  82.2 3.3 %mix.3 = (f32[256,768]{1,0:T(8,128)S(1)}, f32[256,896]{1,0:T(8,128)S(1)}) custom-call(f32[32,768]{1,0:T(8,128)S(1)} %collective-permute-done.39.refs_0_, f32[32,768]{1,0:T(8,128)S(1)} %collective-permute-done.40.refs_1_, f32[32,768]{1,0:T(8,128)S(1)} %collective-permute-done.41.refs_2_, f32[256,768]{1,0:T(8,128)S(1)} %get-tuple-element.444.refs_3_, ...), custom_call_target="tpu_custom_call" | custom-call | flops 2529999872 | tf_op jit(solution)/shard_map/mix/pallas_call | solution.py:270
  86.5 20.1 %conditional.8 = (f32[256,768]{1,0:T(8,128)}, f32[256,768]{1,0:T(8,128)}, f32[8,768]{1,0:T(8,128)}, f32[256,768]{1,0:T(8,128)}, f32[8,32,768]{2,1,0:T(8,128)}, /...) conditional(s32[]{:T(128)} %convert_element_type.2, () %tuple.76, ...), branch_computations={%region_0.0_spmd, %region_1.0_spmd} | conditional | flops 17250000896 | bytes 6291624 | solution.py:1009
  87.4 8.9 %layer_feed.1 = (f32[256,3072]{1,0:T(8,128)S(1)}, f32[8,768]{1,0:T(8,128)}, f32[256,768]{1,0:T(8,128)}, f32[8,32,768]{2,1,0:T(8,128)}) custom-call(f32[256,768]{1,0:T(8,128)S(1)} %get-tuple-element.188.refs_0_, bf16[768,3072]{1,0:T(8,128)(2,1)S(1)} %get-tuple-element.189.refs_1_.refs_2_, f32[2,3072]{1,0:T(2,128)S(1)} %get-tuple-element.190.refs_2_, ...), custom_call_target="tpu_custom_call" | custom-call | flops 8625000448 | tf_op jit(solution)/shard_map/cond/branch_1_fun/layer_feed/pallas_call | solution.py:270
  96.4 10.0 %layer_backward.1 = (f32[256,768]{1,0:T(8,128)S(1)}, f32[8,768]{1,0:T(8,128)}, f32[256,768]{1,0:T(8,128)S(1)}, f32[32,768]{1,0:T(8,128)S(1)}, f32[32,768]{1,0:T(8,128)S(1)}, /*index=5*/f32[32,768]{1,0:T(8,128)S(1)}) custom-call(f32[256,768]{1,0:T(8,128)} %get-tuple-element.571.refs_0_, f32[256,3072]{1,0:T(8,128)S(1)} %get-tuple-element.200.refs_1_, ...), custom_call_target="tpu_custom_call" | custom-call | flops 8625000448 | tf_op jit(solution)/shard_map/cond/branch_1_fun/layer_backward/pallas_call | solution.py:270
  106.5 8.9 %conditional.9 = (f32[32,768]{1,0:T(8,128)}, f32[32,768]{1,0:T(8,128)}, f32[32,768]{1,0:T(8,128)}, f32[256,768]{1,0:T(8,128)S(1)}, f32[256,768]{1,0:T(8,128)}, /*index=5*/f32[256,768]{1,0:T(8,128)}) conditional(s32[]{:T(128)} %convert_element_type.2, () %tuple.75, (f32[32,768]{1,0:T(8,128)S(1)}, f32[32,768]{1,0:T(8,128)S(1)}, ...), branch_computations={%region_2.0_spmd, %region_3.0_spmd} | conditional | flops 1724999936 | bytes 7471352 | solution.py:1009
  110.5 2.7 own_part.3
  115.4 4.3 %delta.1 = (f32[8,768]{1,0:T(8,128)}, f32[256,768]{1,0:T(8,128)}) custom-call(f32[32,768]{1,0:T(8,128)} %get-tuple-element.456.refs_0_, f32[32,768]{1,0:T(8,128)} %get-tuple-element.457.refs_1_, f32[32,768]{1,0:T(8,128)} %get-tuple-element.458.refs_2_, f32[256,768]{1,0:T(8,128)S(1)} %get-tuple-element.459.refs_3_, ...), custom_call_target="tpu_custom_call" | custom-call | flops 3220000000 | tf_op jit(solution)/shard_map/delta/pallas_call | solution.py:270
  119.8 22.6 %conditional.10 = (f32[256,768]{1,0:T(8,128)}, f32[256,768]{1,0:T(8,128)}, f32[256,768]{1,0:T(8,128)}, bf16[768,768]{1,0:T(8,128)(2,1)}, f32[1,768]{1,0:T(1,128)...) conditional(s32[]{:T(128)} %convert_element_type.2, () %tuple.79, ...), branch_computations={%region_4.0_spmd, %region_5.0_spmd} | conditional | flops 20584998912 | bytes 9450292 | solution.py:1009
  123.9 5.9 %cut.2 = (bf16[768,768]{1,0:T(8,128)(2,1)}, bf16[768,768]{1,0:T(8,128)(2,1)}, f32[8,128]{1,0:T(8,128)S(1)}) custom-call(f32[256,768]{1,0:T(8,128)} %get-tuple-element.221.refs_0_.refs_1_, s32[4]{0:T(128)S(1)} %pad_add_fusion.refs_1_, s32[2]{0:T(128)S(1)} %pad_add_fusion.1.refs_2_, bf16[2,768,3072]{2,1,0:T(8,128)(2,1)} %get-tuple-element.225.refs_3_, ...), custom_call_target="tpu_custom_call" | custom-call | flops 6784999936 | tf_op jit(solution)/shard_map/cond/branch_1_fun/cut/pallas_call | solution.py:270
  130.1 12.3 %layer_stream.1 = (f32[256,768]{1,0:T(8,128)S(1)}, f32[8,768]{1,0:T(8,128)}, f32[256,768]{1,0:T(8,128)S(1)}, f32[32,768]{1,0:T(8,128)S(1)}, f32[32,768]{1,0:T(8,128)S(1)}, /*index=5*/f32[32,768]{1,0:T(8,128)S(1)}) custom-call(f32[8,128]{1,0:T(8,128)S(1)} %get-tuple-element.230.refs_0_, f32[256,768]{1,0:T(8,128)} %get-tuple-element.221.refs_0_.refs_1_, ...), custom_call_target="tpu_custom_call" | custom-call | flops 13799999488 | tf_op jit(solution)/shard_map/cond/branch_1_fun/layer_stream/pallas_call | solution.py:270
  142.4 16.0 %conditional.11 = (f32[32,768]{1,0:T(8,128)}, f32[32,768]{1,0:T(8,128)}, f32[32,768]{1,0:T(8,128)}, f32[256,768]{1,0:T(8,128)}, f32[128,768]{1,0:T(8,128)}, /*index=5*/f32[128,768]{1,0:T(8,128)}) conditional(s32[]{:T(128)} %convert_element_type.2, () %tuple.81, (f32[32,768]{1,0:T(8,128)S(1)}, f32[32,768]{1,0:T(8,128)S(1)}, f32[32,768]{1,0:T(8,128)S(1)}, ...), branch_computations={%region_6.0_spmd, %region_7.0_spmd} | conditional | flops 1724999936 | bytes 5898488 | solution.py:1009
  149.3 2.5 own_part.4
  151.7 6.7 %collective-permute-done.7 = f32[32,768]{1,0:T(8,128)} collective-permute-done((f32[32,768]{1,0:T(8,128)S(1)}, f32[32,768]{1,0:T(8,128)}, u32[]{:S(2)}, u32[]{:S(2)}) %collective-permute-start.7) | collective-permute-done | bytes 98336 | tf_op jit(solution)/shard_map/cond/branch_1_fun/ppermute | solution.py:718
  158.5 39.4 %conditional.12 = (f32[4,192,768]{2,1,0:T(8,128)S(1)}, f32[4,96,768]{2,1,0:T(8,128)S(1)}, f32[4,96,768]{2,1,0:T(8,128)}, f32[4,96,768]{2,1,0:T(8,128)}, f32[4,96,768]{2,1,0:T(8,128)}, /*index=5*/f32[8,32,768]{2,1,0:T(8,128)}) conditional(s32[]{:T(128)} %convert_element_type.2, () %tuple.74, (s32[]{:T(128)}, s32[]{:T(128)}, f32[1024,768]{1,0:T(8,128)}, ...), branch_computations={%region_8.0_spmd, %region_9.0_spmd} | conditional | flops 27600588800 | bytes 48759232 | solution.py:1009
  159.1 13.0 %weight_grads.2 = (f32[4,192,768]{2,1,0:T(8,128)}, f32[4,192,768]{2,1,0:T(8,128)}, f32[8,128]{1,0:T(8,128)}) custom-call(s32[4]{0:T(128)} %pad_add_fusion.2.refs_0_, f32[1024,768]{1,0:T(8,128)} %get-tuple-element.254.refs_1_, f32[256,768]{1,0:T(8,128)} %get-tuple-element.255.refs_2_, f32[256,768]{1,0:T(8,128)} %get-tuple-element.256.refs_3_, ...), custom_call_target="tpu_custom_call" | custom-call | flops 13799999488 | tf_op jit(solution)/shard_map/cond/branch_1_fun/weight_grads/pallas_call | solution.py:270
  172.7 4.6 %all-to-all-start = ((f32[8,32,768]{2,1,0:T(8,128)}), f32[8,32,768]{2,1,0:T(8,128)}, u32[]{:S(2)}, u32[]{:S(2)}) async-start(f32[8,32,768]{2,1,0:T(8,128)} %get-tuple-element.280), calls=%async_computation | async-start | bytes 1572864 | tf_op jit(solution)/shard_map/cond/branch_1_fun/all_to_all | solution.py:1094
  179.0 12.2 %weight_grads.3 = (f32[4,96,768]{2,1,0:T(8,128)}, f32[4,96,768]{2,1,0:T(8,128)}, f32[4,96,768]{2,1,0:T(8,128)}, f32[4,96,768]{2,1,0:T(8,128)}, f32[8,128]{1,0:T(8,128)}) custom-call(f32[8,128]{1,0:T(8,128)} %get-tuple-element.265.refs_0_, s32[1]{0:T(128)} %constant.41.clone.refs_1_, f32[256,768]{1,0:T(8,128)} %get-tuple-element.266.refs_2_, ...), custom_call_target="tpu_custom_call" | custom-call | flops 13799999488 | tf_op jit(solution)/shard_map/cond/branch_1_fun/weight_grads/pallas_call | solution.py:270
  194.7 3.2 all-to-all-done
  199.3 29.8 %conditional.13 = (f32[2,96,768]{2,1,0:T(8,128)S(1)}, f32[2,96,768]{2,1,0:T(8,128)S(1)}, f32[2,96,768]{2,1,0:T(8,128)S(1)}, f32[2,96,768]{2,1,0:T(8,128)S(1)}, f...) conditional(s32[]{:T(128)} %convert_element_type.2, () %tuple.73, (f32[4,96,768]{2,1,0:T(8,128)S(1)}, ...), branch_computations={%region_10.0_spmd, %region_11.0_spmd} | conditional | flops 1035589824 | bytes 16515200 | solution.py:1009
  202.3 3.3 %leave.1 = (f32[8,768]{1,0:T(8,128)S(1)}, f32[8,32,768]{2,1,0:T(8,128)}) custom-call(f32[32,768]{1,0:T(8,128)} %get-tuple-element.285.refs_0_, f32[32,768]{1,0:T(8,128)} %get-tuple-element.286.refs_1_, f32[32,768]{1,0:T(8,128)} %get-tuple-element.287.refs_2_, s32[1]{0:T(128)} %get-tuple-element.288.refs_3_, f32[256,768]{1,0:T(8,128)} %get-tuple-element.289.refs_4_, ...), custom_call_target="tpu_custom_call" | custom-call | flops 1035000000 | tf_op jit(solution)/shard_map/cond/branch_1_fun/leave/pallas_call | solution.py:270
  205.7 20.6 %collective-permute-done.17 = f32[4,96,768]{2,1,0:T(8,128)S(1)} collective-permute-done((f32[4,96,768]{2,1,0:T(8,128)}, f32[4,96,768]{2,1,0:T(8,128)S(1)}, u32[]{:S(2)}, u32[]{:S(2)}) %collective-permute-start.17) | collective-permute-done | bytes 1179680 | tf_op jit(solution)/shard_map/cond/branch_1_fun/ppermute | solution.py:718
  229.1 15.5 %conditional.14 = (f32[192,768]{1,0:T(8,128)}, f32[192,768]{1,0:T(8,128)S(1)}, f32[40,768]{1,0:T(8,128)}, f32[2,128,768]{2,1,0:T(8,128)}) conditional(s32[]{:T(128)} %convert_element_type.2, () %tuple.72, (f32[2,96,768]{2,1,0:T(8,128)S(1)}, f32[2,96,768]{2,1,0:T(8,128)S(1)}, f32[2,96,768]{2,1,0:T(8,128)S(1)}, f32[2,96,768]{2,1,0:T(8,128)S(1)}, ...), branch_computations={%region_12.0_spmd, %region_13.0_spmd} | conditional | flops 2530620416 | bytes 11722904 | solution.py:1009
  231.3 2.3 collect.2
  234.2 8.2 %collective-permute-done.19 = f32[2,96,768]{2,1,0:T(8,128)S(1)} collective-permute-done((f32[2,96,768]{2,1,0:T(8,128)S(1)}, f32[2,96,768]{2,1,0:T(8,128)S(1)}, u32[]{:S(2)}, u32[]{:S(2)}) %collective-permute-start.19) | collective-permute-done | bytes 589856 | tf_op jit(solution)/shard_map/cond/branch_1_fun/ppermute | solution.py:718
  246.5 32.0 %conditional.15 = (f32[192,768]{1,0:T(8,128)}, f32[40,768]{1,0:T(8,128)S(1)}, f32[2,768,384]{2,1,0:T(8,128)}, f32[2,384,768]{2,1,0:T(8,128)}) conditional(s32[]{:T(128)} %convert_element_type.2, () %tuple.86, (f32[192,768]{1,0:T(8,128)}, f32[192,768]{1,0:T(8,128)S(1)}, f32[40,768]{1,0:T(8,128)}, f32[192,768]{1,0:T(8,128)}, s32[1]{0:T(128)}) %tuple.87), branch_computations={%region_15.0_spmd, %region_16.0_spmd} | conditional | flops 3795239680 | bytes 15655252 | solution.py:1009
  249.9 11.7 %collective-permute-done.27.refs_3_ = f32[192,768]{1,0:T(8,128)S(1)} collective-permute-done((f32[192,768]{1,0:T(8,128)}, f32[192,768]{1,0:T(8,128)S(1)}, u32[]{:S(2)}, u32[]{:S(2)}) %collective-permute-start.27) | collective-permute-done | bytes 589856 | tf_op jit(solution)/shard_map/cond/branch_1_fun/ppermute | solution.py:718
  264.6 3.0 collective-permute-done.23
  267.6 2.4 collective-permute-start.25
  270.0 3.7 %collective-permute-done.25 = f32[40,768]{1,0:T(8,128)S(1)} collective-permute-done((f32[40,768]{1,0:T(8,128)}, f32[40,768]{1,0:T(8,128)S(1)}, u32[]{:S(2)}, u32[]{:S(2)}) %collective-permute-start.25) | collective-permute-done | bytes 122912 | tf_op jit(solution)/shard_map/cond/branch_1_fun/ppermute | solution.py:718
  278.5 3.2 %collective-permute-start.43 = (f32[40,768]{1,0:T(8,128)S(1)}, f32[40,768]{1,0:T(8,128)S(1)}, u32[]{:S(2)}, u32[]{:S(2)}) collective-permute-start(f32[40,768]{1,0:T(8,128)S(1)} %get-tuple-element.509), channel_id=1, source_target_pairs={{0,4},{2,6},{4,0},{6,2},{1,5},{3,7},{5,1},{7,3},{8,12},{10,14},{12... | collective-permute-start | bytes 368648 | tf_op jit(solution)/shard_map/ppermute | solution.py:718
  283.4 4.9 %all-to-all-start.2 = ((f32[8,32,768]{2,1,0:T(8,128)}), f32[8,32,768]{2,1,0:T(8,128)S(1)}, u32[]{:S(2)}, u32[]{:S(2)}) async-start(f32[8,32,768]{2,1,0:T(8,128)} %hold.1), calls=%async_computation.3 | async-start | bytes 1572864 | tf_op jit(solution)/shard_map/all_to_all | solution.py:1156
  288.2 2.9 collective-permute-done.43
  291.9 5.6 %collective-permute-done.46.refs_3_ = f32[192,768]{1,0:T(8,128)S(1)} collective-permute-done((f32[192,768]{1,0:T(8,128)}, f32[192,768]{1,0:T(8,128)S(1)}, u32[]{:S(2)}, u32[]{:S(2)}) %collective-permute-start.46) | collective-permute-done | bytes 589856 | tf_op jit(solution)/shard_map/ppermute | solution.py:718
  300.0 2.9 finish.3
  302.9 6.8 %all-to-all-done.2.refs_0_ = f32[8,32,768]{2,1,0:T(8,128)S(1)} async-done(((f32[8,32,768]{2,1,0:T(8,128)}), f32[8,32,768]{2,1,0:T(8,128)S(1)}, u32[]{:S(2)}, u32[]{:S(2)}) %all-to-all-start.2) | async-done | bytes 786464 | tf_op jit(solution)/shard_map/all_to_all | solution.py:1156
  (197 shorter events, 74.2 us)
Async XLA Ops:
  7.2 151.3 %all-gather.2.cloned.1.call-start = ((), (), s32[]{:S(2)}) async-start(), calls=%async_computation.4 | async-start | bytes 3932160 | tf_op jit(solution)/shard_map/all_gather | solution.py:1050
  9.9 8.9 %collective-permute-start.29 = (f32[32,896]{1,0:T(8,128)S(1)}, f32[32,896]{1,0:T(8,128)S(1)}, u32[]{:S(2)}, u32[]{:S(2)}) collective-permute-start(f32[32,896]{1,0:T(8,128)S(1)} %get-tuple-element.418), channel_id=1, source_target_pairs={{0,1},{1,0},{2,3},{3,2},{4,5},{5,4},{6,7},{7,6},{8,9},{9,8},{10,11... | collective-permute-start | bytes 344072 | tf_op jit(solution)/shard_map/ppermute | solution.py:718
  12.9 9.7 %collective-permute-start.30 = (f32[32,896]{1,0:T(8,128)S(1)}, f32[32,896]{1,0:T(8,128)S(1)}, u32[]{:S(2)}, u32[]{:S(2)}) collective-permute-start(f32[32,896]{1,0:T(8,128)S(1)} %get-tuple-element.419), channel_id=1, source_target_pairs={{0,2},{1,3},{2,0},{3,1},{4,6},{5,7},{6,4},{7,5},{8,10},{9,11},{10,... | collective-permute-start | bytes 344072 | tf_op jit(solution)/shard_map/ppermute | solution.py:718
  14.5 8.2 %collective-permute-start.31 = (f32[32,896]{1,0:T(8,128)S(1)}, f32[32,896]{1,0:T(8,128)S(1)}, u32[]{:S(2)}, u32[]{:S(2)}) collective-permute-start(f32[32,896]{1,0:T(8,128)S(1)} %get-tuple-element.420), channel_id=1, source_target_pairs={{0,3},{1,2},{2,1},{3,0},{4,7},{5,6},{6,5},{7,4},{8,11},{9,10},{10,... | collective-permute-start | bytes 344072 | tf_op jit(solution)/shard_map/ppermute | solution.py:718
  14.5 16.1 %collective-permute-start.32 = (f32[32,896]{1,0:T(8,128)S(1)}, f32[32,896]{1,0:T(8,128)S(1)}, u32[]{:S(2)}, u32[]{:S(2)}) collective-permute-start(f32[32,896]{1,0:T(8,128)S(1)} %get-tuple-element.423), channel_id=1, source_target_pairs={{0,4},{1,5},{2,6},{3,7},{4,0},{5,1},{6,2},{7,3},{8,12},{9,13},{10,... | collective-permute-start | bytes 344072 | tf_op jit(solution)/shard_map/ppermute | solution.py:718
  17.5 17.2 %collective-permute-start.33 = (f32[32,896]{1,0:T(8,128)S(1)}, f32[32,896]{1,0:T(8,128)S(1)}, u32[]{:S(2)}, u32[]{:S(2)}) collective-permute-start(f32[32,896]{1,0:T(8,128)S(1)} %get-tuple-element.424), channel_id=1, source_target_pairs={{0,5},{1,4},{2,7},{3,6},{4,1},{5,0},{6,3},{7,2},{8,13},{9,12},{10,... | collective-permute-start | bytes 344072 | tf_op jit(solution)/shard_map/ppermute | solution.py:718
  18.9 15.8 %collective-permute-start.34 = (f32[32,896]{1,0:T(8,128)S(1)}, f32[32,896]{1,0:T(8,128)S(1)}, u32[]{:S(2)}, u32[]{:S(2)}) collective-permute-start(f32[32,896]{1,0:T(8,128)S(1)} %get-tuple-element.425), channel_id=1, source_target_pairs={{0,6},{1,7},{2,4},{3,5},{4,2},{5,3},{6,0},{7,1},{8,14},{9,15},{10,... | collective-permute-start | bytes 344072 | tf_op jit(solution)/shard_map/ppermute | solution.py:718
  22.5 12.2 %collective-permute-start.35 = (f32[32,896]{1,0:T(8,128)S(1)}, f32[32,896]{1,0:T(8,128)S(1)}, u32[]{:S(2)}, u32[]{:S(2)}) collective-permute-start(f32[32,896]{1,0:T(8,128)S(1)} %get-tuple-element.426), channel_id=1, source_target_pairs={{0,7},{1,6},{2,5},{3,4},{4,3},{5,2},{6,1},{7,0},{8,15},{9,14},{10,... | collective-permute-start | bytes 344072 | tf_op jit(solution)/shard_map/ppermute | solution.py:718
  39.4 8.6 %collective-permute-start.36 = (f32[32,768]{1,0:T(8,128)S(1)}, f32[32,768]{1,0:T(8,128)S(1)}, u32[]{:S(2)}, u32[]{:S(2)}) collective-permute-start(f32[32,768]{1,0:T(8,128)S(1)} %get-tuple-element.428.refs_0_), channel_id=1, source_target_pairs={{0,1},{1,0},{2,3},{3,2},{4,5},{5,4},{6,7},{7,6},{8,9},{9,8},{10,11... | collective-permute-start | bytes 294920 | tf_op jit(solution)/shard_map/ppermute | solution.py:718
  41.4 7.3 %collective-permute-start.37 = (f32[32,768]{1,0:T(8,128)S(1)}, f32[32,768]{1,0:T(8,128)S(1)}, u32[]{:S(2)}, u32[]{:S(2)}) collective-permute-start(f32[32,768]{1,0:T(8,128)S(1)} %get-tuple-element.429), channel_id=1, source_target_pairs={{0,2},{1,3},{2,0},{3,1},{4,6},{5,7},{6,4},{7,5},{8,10},{9,11},{10,... | collective-permute-start | bytes 294920 | tf_op jit(solution)/shard_map/ppermute | solution.py:718
  53.4 23.5 %all-to-all-start.1 = ((f32[8,32,768]{2,1,0:T(8,128)}), f32[8,32,768]{2,1,0:T(8,128)S(1)}, u32[]{:S(2)}, u32[]{:S(2)}) async-start(f32[8,32,768]{2,1,0:T(8,128)} %get-tuple-element.441), calls=%async_computation.1 | async-start | bytes 1572864 | tf_op jit(solution)/shard_map/all_to_all | solution.py:758
  58.4 188.1 %reduce-scatter.2.cloned.1.call-start = ((), (), s32[]{:S(2)}) async-start(), calls=%async_computation.5 | async-start | bytes 2949120 | tf_op jit(solution)/shard_map/reduce_scatter | solution.py:1003
  72.4 9.8 %collective-permute-start.39 = (f32[32,768]{1,0:T(8,128)S(1)}, f32[32,768]{1,0:T(8,128)S(1)}, u32[]{:S(2)}, u32[]{:S(2)}) collective-permute-start(f32[32,768]{1,0:T(8,128)S(1)} %get-tuple-element.438), channel_id=1, source_target_pairs={{0,1},{1,0},{2,3},{3,2},{4,5},{5,4},{6,7},{7,6},{8,9},{9,8},{10,11... | collective-permute-start | bytes 294920 | tf_op jit(solution)/shard_map/ppermute | solution.py:718
  74.4 7.8 %collective-permute-start.40 = (f32[32,768]{1,0:T(8,128)S(1)}, f32[32,768]{1,0:T(8,128)S(1)}, u32[]{:S(2)}, u32[]{:S(2)}) collective-permute-start(f32[32,768]{1,0:T(8,128)S(1)} %get-tuple-element.439), channel_id=1, source_target_pairs={{0,2},{1,3},{2,0},{3,1},{4,6},{5,7},{6,4},{7,5},{8,10},{9,11},{10,... | collective-permute-start | bytes 294920 | tf_op jit(solution)/shard_map/ppermute | solution.py:718
  75.9 6.3 %collective-permute-start.41 = (f32[32,768]{1,0:T(8,128)S(1)}, f32[32,768]{1,0:T(8,128)S(1)}, u32[]{:S(2)}, u32[]{:S(2)}) collective-permute-start(f32[32,768]{1,0:T(8,128)S(1)} %get-tuple-element.440), channel_id=1, source_target_pairs={{0,3},{1,2},{2,1},{3,0},{4,7},{5,6},{6,5},{7,4},{8,11},{9,10},{10,... | collective-permute-start | bytes 294920 | tf_op jit(solution)/shard_map/ppermute | solution.py:718
  86.5 20.0 %collective-permute-start = (f32[256,768]{1,0:T(8,128)S(1)}, f32[256,768]{1,0:T(8,128)}, u32[]{:S(2)}, u32[]{:S(2)}) collective-permute-start(f32[256,768]{1,0:T(8,128)S(1)} %get-tuple-element.188.refs_0_), channel_id=1, source_target_pairs={{0,8},{8,0},{1,9},{9,1},{2,10},{10,2},{3,11},{11,3},{4,12},{12,4},... | collective-permute-start | bytes 2359304 | tf_op jit(solution)/shard_map/cond/branch_1_fun/ppermute | solution.py:718
  86.5 20.1 %collective-permute-start.1 = (f32[256,768]{1,0:T(8,128)S(1)}, f32[256,768]{1,0:T(8,128)}, u32[]{:S(2)}, u32[]{:S(2)}) collective-permute-start(f32[256,768]{1,0:T(8,128)S(1)} %get-tuple-element.188.refs_0_), channel_id=1, source_target_pairs={{0,2},{2,0},{1,3},{3,1},{4,6},{6,4},{5,7},{7,5},{8,10},{10,8},{9,1... | collective-permute-start | bytes 2359304 | tf_op jit(solution)/shard_map/cond/branch_1_fun/ppermute | solution.py:718
  106.5 8.9 %collective-permute-start.5 = (f32[256,768]{1,0:T(8,128)}, f32[256,768]{1,0:T(8,128)}, u32[]{:S(2)}, u32[]{:S(2)}) collective-permute-start(f32[256,768]{1,0:T(8,128)} %get-tuple-element.218), channel_id=1, source_target_pairs={{0,8},{8,0},{1,9},{9,1},{2,10},{10,2},{3,11},{11,3},{4,12},{12,4},... | collective-permute-start | bytes 2359304 | tf_op jit(solution)/shard_map/cond/branch_1_fun/ppermute | solution.py:718
  106.8 8.6 %collective-permute-start.6 = (f32[256,768]{1,0:T(8,128)}, f32[256,768]{1,0:T(8,128)}, u32[]{:S(2)}, u32[]{:S(2)}) collective-permute-start(f32[256,768]{1,0:T(8,128)} %get-tuple-element.219), channel_id=1, source_target_pairs={{0,8},{8,0},{1,9},{9,1},{2,10},{10,2},{3,11},{11,3},{4,12},{12,4},... | collective-permute-start | bytes 2359304 | tf_op jit(solution)/shard_map/cond/branch_1_fun/ppermute | solution.py:718
  107.0 6.2 %collective-permute-start.2 = (f32[32,768]{1,0:T(8,128)S(1)}, f32[32,768]{1,0:T(8,128)}, u32[]{:S(2)}, u32[]{:S(2)}) collective-permute-start(f32[32,768]{1,0:T(8,128)S(1)} %get-tuple-element.210), channel_id=1, source_target_pairs={{0,1},{1,0},{2,3},{3,2},{4,5},{5,4},{6,7},{7,6},{8,9},{9,8},{10,11... | collective-permute-start | bytes 294920 | tf_op jit(solution)/shard_map/cond/branch_1_fun/ppermute | solution.py:718
  109.5 5.9 %collective-permute-start.4 = (f32[32,768]{1,0:T(8,128)S(1)}, f32[32,768]{1,0:T(8,128)}, u32[]{:S(2)}, u32[]{:S(2)}) collective-permute-start(f32[32,768]{1,0:T(8,128)S(1)} %get-tuple-element.212), channel_id=1, source_target_pairs={{0,3},{1,2},{2,1},{3,0},{4,7},{5,6},{6,5},{7,4},{8,11},{9,10},{10,... | collective-permute-start | bytes 294920 | tf_op jit(solution)/shard_map/cond/branch_1_fun/ppermute | solution.py:718
  119.8 22.6 %collective-permute-start.13 = (f32[256,768]{1,0:T(8,128)}, f32[256,768]{1,0:T(8,128)}, u32[]{:S(2)}, u32[]{:S(2)}) collective-permute-start(f32[256,768]{1,0:T(8,128)} %get-tuple-element.221.refs_0_.refs_1_), channel_id=1, source_target_pairs={{0,1},{1,0},{2,3},{3,2},{4,5},{5,4},{6,7},{7,6},{8,9},{9,8},{10,11... | collective-permute-start | bytes 2359304 | tf_op jit(solution)/shard_map/cond/branch_1_fun/ppermute | solution.py:718
  121.3 21.0 %collective-permute-start.14 = (f32[256,768]{1,0:T(8,128)}, f32[256,768]{1,0:T(8,128)}, u32[]{:S(2)}, u32[]{:S(2)}) collective-permute-start(f32[256,768]{1,0:T(8,128)} %get-tuple-element.221.refs_0_.refs_1_), channel_id=1, source_target_pairs={{0,16},{16,0},{1,17},{17,1},{2,18},{18,2},{3,19},{19,3},{4,20},{20... | collective-permute-start | bytes 2359304 | tf_op jit(solution)/shard_map/cond/branch_1_fun/ppermute | solution.py:718
  122.8 19.6 %collective-permute-start.12 = (f32[256,768]{1,0:T(8,128)}, f32[256,768]{1,0:T(8,128)}, u32[]{:S(2)}, u32[]{:S(2)}) collective-permute-start(f32[256,768]{1,0:T(8,128)} %get-tuple-element.220), channel_id=1, source_target_pairs={{0,2},{2,0},{1,3},{3,1},{4,6},{6,4},{5,7},{7,5},{8,10},{10,8},{9,1... | collective-permute-start | bytes 2359304 | tf_op jit(solution)/shard_map/cond/branch_1_fun/ppermute | solution.py:718
  143.4 15.0 %collective-permute-start.10 = (f32[128,768]{1,0:T(8,128)S(1)}, f32[128,768]{1,0:T(8,128)}, u32[]{:S(2)}, u32[]{:S(2)}) collective-permute-start(f32[128,768]{1,0:T(8,128)S(1)} %slice.80), channel_id=1, source_target_pairs={{0,16},{16,0},{1,17},{17,1},{2,18},{18,2},{3,19},{19,3},{4,20},{20... | collective-permute-start | bytes 1179656 | tf_op jit(solution)/shard_map/cond/branch_1_fun/ppermute | solution.py:718
  145.0 13.4 %collective-permute-start.11 = (f32[128,768]{1,0:T(8,128)S(1)}, f32[128,768]{1,0:T(8,128)}, u32[]{:S(2)}, u32[]{:S(2)}) collective-permute-start(f32[128,768]{1,0:T(8,128)S(1)} %slice.81), channel_id=1, source_target_pairs={{0,1},{1,0},{2,3},{3,2},{4,5},{5,4},{6,7},{7,6},{8,9},{9,8},{10,11... | collective-permute-start | bytes 1179656 | tf_op jit(solution)/shard_map/cond/branch_1_fun/ppermute | solution.py:718
  145.8 12.6 %collective-permute-start.7 = (f32[32,768]{1,0:T(8,128)S(1)}, f32[32,768]{1,0:T(8,128)}, u32[]{:S(2)}, u32[]{:S(2)}) collective-permute-start(f32[32,768]{1,0:T(8,128)S(1)} %get-tuple-element.242), channel_id=1, source_target_pairs={{0,1},{1,0},{2,3},{3,2},{4,5},{5,4},{6,7},{7,6},{8,9},{9,8},{10,11... | collective-permute-start | bytes 294920 | tf_op jit(solution)/shard_map/cond/branch_1_fun/ppermute | solution.py:718
  147.1 11.3 %collective-permute-start.8 = (f32[32,768]{1,0:T(8,128)S(1)}, f32[32,768]{1,0:T(8,128)}, u32[]{:S(2)}, u32[]{:S(2)}) collective-permute-start(f32[32,768]{1,0:T(8,128)S(1)} %get-tuple-element.243), channel_id=1, source_target_pairs={{0,2},{1,3},{2,0},{3,1},{4,6},{5,7},{6,4},{7,5},{8,10},{9,11},{10,... | collective-permute-start | bytes 294920 | tf_op jit(solution)/shard_map/cond/branch_1_fun/ppermute | solution.py:718
  148.2 10.2 %collective-permute-start.9 = (f32[32,768]{1,0:T(8,128)S(1)}, f32[32,768]{1,0:T(8,128)}, u32[]{:S(2)}, u32[]{:S(2)}) collective-permute-start(f32[32,768]{1,0:T(8,128)S(1)} %get-tuple-element.244), channel_id=1, source_target_pairs={{0,3},{1,2},{2,1},{3,0},{4,7},{5,6},{6,5},{7,4},{8,11},{9,10},{10,... | collective-permute-start | bytes 294920 | tf_op jit(solution)/shard_map/cond/branch_1_fun/ppermute | solution.py:718
  172.1 19.1 %collective-permute-start.15 = (f32[4,192,768]{2,1,0:T(8,128)}, f32[4,192,768]{2,1,0:T(8,128)S(1)}, u32[]{:S(2)}, u32[]{:S(2)}) collective-permute-start(f32[4,192,768]{2,1,0:T(8,128)} %get-tuple-element.264), channel_id=1, source_target_pairs={{0,8},{8,0},{1,9},{9,1},{2,10},{10,2},{3,11},{11,3},{4,12},{12,4},... | collective-permute-start | bytes 7077896 | tf_op jit(solution)/shard_map/cond/branch_1_fun/ppermute | solution.py:718
  172.7 25.1 %all-to-all-start = ((f32[8,32,768]{2,1,0:T(8,128)}), f32[8,32,768]{2,1,0:T(8,128)}, u32[]{:S(2)}, u32[]{:S(2)}) async-start(f32[8,32,768]{2,1,0:T(8,128)} %get-tuple-element.280), calls=%async_computation | async-start | bytes 1572864 | tf_op jit(solution)/shard_map/cond/branch_1_fun/all_to_all | solution.py:1094
  199.3 26.9 %collective-permute-start.17 = (f32[4,96,768]{2,1,0:T(8,128)}, f32[4,96,768]{2,1,0:T(8,128)S(1)}, u32[]{:S(2)}, u32[]{:S(2)}) collective-permute-start(f32[4,96,768]{2,1,0:T(8,128)} %get-tuple-element.282), channel_id=1, source_target_pairs={{0,1},{1,0},{2,3},{3,2},{4,5},{5,4},{6,7},{7,6},{8,9},{9,8},{10,11... | collective-permute-start | bytes 3538952 | tf_op jit(solution)/shard_map/cond/branch_1_fun/ppermute | solution.py:718
  200.8 26.9 %collective-permute-start.18 = (f32[4,96,768]{2,1,0:T(8,128)}, f32[4,96,768]{2,1,0:T(8,128)S(1)}, u32[]{:S(2)}, u32[]{:S(2)}) collective-permute-start(f32[4,96,768]{2,1,0:T(8,128)} %get-tuple-element.284), channel_id=1, source_target_pairs={{0,16},{16,0},{1,17},{17,1},{2,18},{18,2},{3,19},{19,3},{4,20},{20... | collective-permute-start | bytes 3538952 | tf_op jit(solution)/shard_map/cond/branch_1_fun/ppermute | solution.py:718
  229.2 13.3 %collective-permute-start.19 = (f32[2,96,768]{2,1,0:T(8,128)S(1)}, f32[2,96,768]{2,1,0:T(8,128)S(1)}, u32[]{:S(2)}, u32[]{:S(2)}) collective-permute-start(f32[2,96,768]{2,1,0:T(8,128)S(1)} %get-tuple-element.296), channel_id=1, source_target_pairs={{0,16},{16,0},{1,17},{17,1},{2,18},{18,2},{3,19},{19,3},{4,20},{20... | collective-permute-start | bytes 1769480 | tf_op jit(solution)/shard_map/cond/branch_1_fun/ppermute | solution.py:718
  230.8 12.9 %collective-permute-start.20 = (f32[2,96,768]{2,1,0:T(8,128)S(1)}, f32[2,96,768]{2,1,0:T(8,128)S(1)}, u32[]{:S(2)}, u32[]{:S(2)}) collective-permute-start(f32[2,96,768]{2,1,0:T(8,128)S(1)} %get-tuple-element.298), channel_id=1, source_target_pairs={{0,1},{1,0},{2,3},{3,2},{4,5},{5,4},{6,7},{7,6},{8,9},{9,8},{10,11... | collective-permute-start | bytes 1769480 | tf_op jit(solution)/shard_map/cond/branch_1_fun/ppermute | solution.py:718
  246.5 15.1 %collective-permute-start.27 = (f32[192,768]{1,0:T(8,128)}, f32[192,768]{1,0:T(8,128)S(1)}, u32[]{:S(2)}, u32[]{:S(2)}) collective-permute-start(f32[192,768]{1,0:T(8,128)} %get-tuple-element.310.refs_1_), channel_id=1, source_target_pairs={{0,16},{16,0},{1,17},{17,1},{2,18},{18,2},{3,19},{19,3},{4,20},{20... | collective-permute-start | bytes 1769480 | tf_op jit(solution)/shard_map/cond/branch_1_fun/ppermute | solution.py:718
  248.0 27.7 %collective-permute-start.22 = (f32[192,768]{1,0:T(8,128)}, f32[192,768]{1,0:T(8,128)S(1)}, u32[]{:S(2)}, u32[]{:S(2)}) collective-permute-start(f32[192,768]{1,0:T(8,128)} %get-tuple-element.307), channel_id=1, source_target_pairs={{0,4},{4,0},{1,5},{5,1},{2,6},{6,2},{3,7},{7,3},{8,12},{12,8},{9,1... | collective-permute-start | bytes 1769480 | tf_op jit(solution)/shard_map/cond/branch_1_fun/ppermute | solution.py:718
  249.9 26.7 %collective-permute-start.26 = (f32[192,768]{1,0:T(8,128)}, f32[192,768]{1,0:T(8,128)S(1)}, u32[]{:S(2)}, u32[]{:S(2)}) collective-permute-start(f32[192,768]{1,0:T(8,128)} %get-tuple-element.310.refs_1_), channel_id=1, source_target_pairs={{0,8},{8,0},{1,9},{9,1},{2,10},{10,2},{3,11},{11,3},{4,12},{12,4},... | collective-permute-start | bytes 1769480 | tf_op jit(solution)/shard_map/cond/branch_1_fun/ppermute | solution.py:718
  261.6 15.0 %collective-permute-start.28 = (f32[192,768]{1,0:T(8,128)S(1)}, f32[192,768]{1,0:T(8,128)S(1)}, u32[]{:S(2)}, u32[]{:S(2)}) collective-permute-start(f32[192,768]{1,0:T(8,128)S(1)} %collective-permute-done.27.refs_3_), channel_id=1, source_target_pairs={{0,8},{8,0},{1,9},{9,1},{2,10},{10,2},{3,11},{11,3},{4,12},{12,4},... | collective-permute-start | bytes 1769480 | tf_op jit(solution)/shard_map/cond/branch_1_fun/ppermute | solution.py:718
  261.6 5.9 %collective-permute-start.23 = (f32[40,768]{1,0:T(8,128)}, f32[40,768]{1,0:T(8,128)S(1)}, u32[]{:S(2)}, u32[]{:S(2)}) collective-permute-start(f32[40,768]{1,0:T(8,128)} %get-tuple-element.308), channel_id=1, source_target_pairs={{0,1},{1,0},{16,17},{17,16},{2,3},{3,2},{18,19},{19,18},{4,5},{5,4... | collective-permute-start | bytes 368648 | tf_op jit(solution)/shard_map/cond/branch_1_fun/ppermute | solution.py:718
  263.1 6.9 %collective-permute-start.24 = (f32[40,768]{1,0:T(8,128)}, f32[40,768]{1,0:T(8,128)S(1)}, u32[]{:S(2)}, u32[]{:S(2)}) collective-permute-start(f32[40,768]{1,0:T(8,128)} %get-tuple-element.308), channel_id=1, source_target_pairs={{0,16},{1,17},{16,0},{17,1},{2,18},{3,19},{18,2},{19,3},{4,20},{5,... | collective-permute-start | bytes 368648 | tf_op jit(solution)/shard_map/cond/branch_1_fun/ppermute | solution.py:718
  267.6 6.1 %collective-permute-start.25 = (f32[40,768]{1,0:T(8,128)}, f32[40,768]{1,0:T(8,128)S(1)}, u32[]{:S(2)}, u32[]{:S(2)}) collective-permute-start(f32[40,768]{1,0:T(8,128)} %get-tuple-element.308), channel_id=1, source_target_pairs={{0,17},{1,16},{16,1},{17,0},{2,19},{3,18},{18,3},{19,2},{4,21},{5,... | collective-permute-start | bytes 368648 | tf_op jit(solution)/shard_map/cond/branch_1_fun/ppermute | solution.py:718
  278.5 9.8 %collective-permute-start.42 = (f32[40,768]{1,0:T(8,128)S(1)}, f32[40,768]{1,0:T(8,128)S(1)}, u32[]{:S(2)}, u32[]{:S(2)}) collective-permute-start(f32[40,768]{1,0:T(8,128)S(1)} %get-tuple-element.509), channel_id=1, source_target_pairs={{0,2},{2,0},{4,6},{6,4},{1,3},{3,1},{5,7},{7,5},{8,10},{10,8},{12,... | collective-permute-start | bytes 368648 | tf_op jit(solution)/shard_map/ppermute | solution.py:718
  278.5 12.7 %collective-permute-start.43 = (f32[40,768]{1,0:T(8,128)S(1)}, f32[40,768]{1,0:T(8,128)S(1)}, u32[]{:S(2)}, u32[]{:S(2)}) collective-permute-start(f32[40,768]{1,0:T(8,128)S(1)} %get-tuple-element.509), channel_id=1, source_target_pairs={{0,4},{2,6},{4,0},{6,2},{1,5},{3,7},{5,1},{7,3},{8,12},{10,14},{12... | collective-permute-start | bytes 368648 | tf_op jit(solution)/shard_map/ppermute | solution.py:718
  281.7 9.5 %collective-permute-start.44 = (f32[40,768]{1,0:T(8,128)S(1)}, f32[40,768]{1,0:T(8,128)S(1)}, u32[]{:S(2)}, u32[]{:S(2)}) collective-permute-start(f32[40,768]{1,0:T(8,128)S(1)} %get-tuple-element.509), channel_id=1, source_target_pairs={{0,6},{2,4},{4,2},{6,0},{1,7},{3,5},{5,3},{7,1},{8,14},{10,12},{12... | collective-permute-start | bytes 368648 | tf_op jit(solution)/shard_map/ppermute | solution.py:718
  282.9 14.6 %collective-permute-start.46 = (f32[192,768]{1,0:T(8,128)}, f32[192,768]{1,0:T(8,128)S(1)}, u32[]{:S(2)}, u32[]{:S(2)}) collective-permute-start(f32[192,768]{1,0:T(8,128)} %get-tuple-element.506.refs_0_.refs_1_), channel_id=1, source_target_pairs={{0,16},{16,0},{1,17},{17,1},{2,18},{18,2},{3,19},{19,3},{4,20},{20... | collective-permute-start | bytes 1769480 | tf_op jit(solution)/shard_map/ppermute | solution.py:718
  283.4 16.6 %collective-permute-start.45 = (f32[192,768]{1,0:T(8,128)}, f32[192,768]{1,0:T(8,128)S(1)}, u32[]{:S(2)}, u32[]{:S(2)}) collective-permute-start(f32[192,768]{1,0:T(8,128)} %get-tuple-element.506.refs_0_.refs_1_), channel_id=1, source_target_pairs={{0,8},{8,0},{1,9},{9,1},{2,10},{10,2},{3,11},{11,3},{4,12},{12,4},... | collective-permute-start | bytes 1769480 | tf_op jit(solution)/shard_map/ppermute | solution.py:718
  283.4 26.3 %all-to-all-start.2 = ((f32[8,32,768]{2,1,0:T(8,128)}), f32[8,32,768]{2,1,0:T(8,128)S(1)}, u32[]{:S(2)}, u32[]{:S(2)}) async-start(f32[8,32,768]{2,1,0:T(8,128)} %hold.1), calls=%async_computation.3 | async-start | bytes 1572864 | tf_op jit(solution)/shard_map/all_to_all | solution.py:1156
  (39 other events, 449.2 us)
Sparse Core Ops, SparseCore 0:
  53.5 51.9 all-gather.1
  199.4 47.0 reduce-scatter.1
